TPU v7x, 256 devices: a whole 4x4x8 slice. The times are simulated.
256 devices in a mesh: ctx: 32 (over x_lo, z, core), head: 8 (over x_hi, y).
Axes of the slice: x: 4 (x_hi: 2, x_lo: 2; x = x_hi * 2 + x_lo), y: 4, z: 8, core: 2. Of those that a mesh axis runs over, the one named last changes fastest.
Arguments:
- tokens: bfloat16 [4096, 5120], P('ctx', 'head'), may hold values from -6 to 6
- kv_values: bfloat16 [2560, 576], P('head'), may hold values from -0.125 to 0.125
- kv_pattern: int32 [1280, 576], P('head'), may hold values from 0 to 5
- kv_down: bfloat16 [5120, 16], P('head'), may hold values from -0.078125 to 0.078125
- kv_up: bfloat16 [16, 576], replicated, may hold values from -1.5 to 1.5
- kv_gain: float32 [512], replicated, may hold values from 0.5 to 1.5
- queries: bfloat16 [4096, 64, 192], P('ctx', 'head'), may hold values from -110 to 110
- absorb_k: bfloat16 [64, 128, 512], P('head'), may hold values from -0.5 to 0.5
- absorb_v: bfloat16 [64, 512, 128], P('head'), may hold values from -0.25 to 0.25
- o_values: bfloat16 [4096, 2560], P('head'), may hold values from -0.09375 to 0.09375
- o_pattern: int32 [2048, 2560], P('head'), may hold values from 0 to 5
- o_down: bfloat16 [8192, 16], P('head'), may hold values from -0.0625 to 0.0625
- o_up: bfloat16 [16, 2560], replicated, may hold values from -1.5 to 1.5
Outputs:
- mixed: float32 [4096, 2560], P('ctx', 'head')
All inputs are finite; a program needn't handle non-finite values.
Results may differ from a plain program's by a relative error of at most 0.01265.
The roundings to bfloat16 on the way count: a program that leaves them out, or rounds other values in their place, can miss the bound.
Values may be sent and summed in bfloat16 or wider, within the bound.
No kernel may reach another device: no remote copies, remote signals or barrier semaphores. Data moves between devices by JAX's collectives and lax.ppermute only.
A program may use at most 128 MiB of HBM per device.

v0:
```python
import math

import jax
import jax.numpy as jnp
from jax import lax
from jax.sharding import PartitionSpec as P


def densify(values, pattern):
    groups = pattern.shape[0]
    columns = values.shape[1]
    pairs = values.reshape(groups, 2, columns)
    upper = (pattern >= 3).astype(jnp.int32)
    topmost = (pattern >= 5).astype(jnp.int32)
    first = upper + topmost
    second = pattern + 1 - 2 * upper - topmost
    slots = jnp.arange(4, dtype=jnp.int32)[None, :, None]
    nothing = jnp.zeros((), values.dtype)
    dense = jnp.where(slots == first[:, None, :], pairs[:, 0:1, :], nothing) + jnp.where(
        slots == second[:, None, :], pairs[:, 1:2, :], nothing
    )
    return dense.reshape(groups * 4, columns)


def rotate(vector, positions):
    half_width = vector.shape[-1] // 2
    freqs = 10000.0 ** (-jnp.arange(half_width, dtype=jnp.float32) / half_width)
    angles = positions.astype(jnp.float32)[..., None] * freqs
    lower = vector[..., :half_width]
    higher = vector[..., half_width:]
    return jnp.concatenate(
        [
            lower * jnp.cos(angles) - higher * jnp.sin(angles),
            higher * jnp.cos(angles) + lower * jnp.sin(angles),
        ],
        axis=-1,
    )


def finish_cache(raw, positions, gain, width):
    latent = raw[:, :width]
    meansq = jnp.mean(latent * latent, axis=-1, keepdims=True)
    normed = latent * lax.rsqrt(meansq + 1e-06) * gain
    return jnp.concatenate([normed, rotate(raw[:, width:], positions)], axis=1).astype(jnp.bfloat16)


def local(
    tokens,
    kv_values,
    kv_pattern,
    kv_down,
    kv_up,
    kv_gain,
    queries,
    absorb_k,
    absorb_v,
    o_values,
    o_pattern,
    o_down,
    o_up,
):
    tok_rows = tokens.shape[0]
    half_rows = tok_rows // 2
    lat_width = kv_gain.shape[0]
    nope_width = absorb_k.shape[1]
    ctx_index = lax.axis_index("ctx")
    first_row = ctx_index * tok_rows
    row_positions = first_row + jnp.arange(tok_rows, dtype=jnp.int32)
    kv_dense = densify(kv_values, kv_pattern)
    lowrank = jnp.dot(tokens, kv_down, preferred_element_type=jnp.float32)
    partial_raw = jnp.dot(tokens, kv_dense, preferred_element_type=jnp.float32) + jnp.dot(
        lowrank, kv_up.astype(jnp.float32), precision=lax.Precision.HIGHEST
    )
    latent_query = jnp.einsum(
        "thn,hnl->thl", queries[:, :, :nope_width], absorb_k, preferred_element_type=jnp.float32
    ).astype(jnp.bfloat16)
    rope_query = rotate(
        queries[:, :, nope_width:].astype(jnp.float32), row_positions[:, None]
    ).astype(jnp.bfloat16)
    full_query = jnp.concatenate([latent_query, rope_query], axis=2)
    score_scale = 1.0 / math.sqrt(queries.shape[2])
    head_rows = queries.shape[1]
    group_queries = (full_query[:half_rows], full_query[half_rows:])
    group_positions = (row_positions[:half_rows], row_positions[half_rows:])

    def update_group(state, query_rows, query_positions, piece):
        running_max, running_total, running_sum = state
        key_positions = jnp.arange(piece.shape[0], dtype=jnp.int32)
        scores = (
            jnp.einsum("rhc,nc->rhn", query_rows, piece, preferred_element_type=jnp.float32)
            * score_scale
        )
        visible = key_positions[None, None, :] <= query_positions[:, None, None]
        scores = jnp.where(visible, scores, -jnp.inf)
        new_max = jnp.max(scores, axis=-1)
        safe_max = jnp.where(new_max == -jnp.inf, 0.0, new_max)
        factor = jnp.exp(running_max - safe_max)
        weights = jnp.exp(scores - safe_max[..., None])
        new_total = running_total * factor + jnp.sum(weights, axis=-1)
        new_sum = running_sum * factor[..., None] + jnp.einsum(
            "rhn,nl->rhl",
            weights.astype(jnp.bfloat16),
            piece[:, :lat_width],
            preferred_element_type=jnp.float32,
        )
        return (new_max, new_total, new_sum)

    def empty_state():
        return (
            jnp.full((half_rows, head_rows), -jnp.inf, jnp.float32),
            jnp.zeros((half_rows, head_rows), jnp.float32),
            jnp.zeros((half_rows, head_rows, lat_width), jnp.float32),
        )

    initial = (empty_state(), empty_state())
    whole = lax.psum(partial_raw, "head")
    cache = finish_cache(whole, row_positions, kv_gain, lat_width)
    piece = lax.all_gather(cache, "ctx", axis=0, tiled=True)
    start = jnp.int32(0)
    updated = []
    for which in range(2):
        query_rows = group_queries[which]
        query_positions = group_positions[which]
        needed = start <= jnp.max(query_positions)
        updated.append(
            lax.cond(
                needed,
                lambda state: update_group(state, query_rows, query_positions, piece),
                lambda state: state,
                initial[which],
            )
        )
    folded = (updated[0], updated[1])
    attended_groups = [(state[2] / state[1][..., None]).astype(jnp.bfloat16) for state in folded]
    attended = jnp.concatenate(attended_groups, axis=0)
    head_out = jnp.einsum(
        "thl,hlv->thv", attended, absorb_v, preferred_element_type=jnp.float32
    ).astype(jnp.bfloat16)
    flat = head_out.reshape(tok_rows, head_rows * absorb_v.shape[2])
    o_dense = densify(o_values, o_pattern)
    adapter = jnp.dot(flat, o_down, preferred_element_type=jnp.float32)
    terms = jnp.dot(flat, o_dense, preferred_element_type=jnp.float32) + jnp.dot(
        adapter, o_up.astype(jnp.float32), precision=lax.Precision.HIGHEST
    )
    return lax.psum_scatter(terms, "head", scatter_dimension=1, tiled=True)


def solution(mesh):
    in_specs = (
        P("ctx", "head"),
        P("head", None),
        P("head", None),
        P("head", None),
        P(),
        P(),
        P("ctx", "head", None),
        P("head", None, None),
        P("head", None, None),
        P("head", None),
        P("head", None),
        P("head", None),
        P(),
    )
    out_specs = P("ctx", "head")
    return jax.shard_map(local, mesh=mesh, in_specs=in_specs, out_specs=out_specs, check_vma=False)
```

profile of v0, /device:TPU:2, one launch (start us, length us, event | category | flops | bytes accessed | tf_op | source)
XLA Modules:
  0.0 343.7 jit_solution(4992695835391838667)
XLA Ops:
  6.5 1.3 reshape.240
  7.8 0.6 fusion.51
  8.4 0.7 copy_bitcast_fusion.2
  9.1 0.2 broadcast_in_dim.99
  9.4 0.4 broadcast_in_dim.100
  9.8 0.9 convert_subtract_fusion.1
  10.7 1.5 eq.105
  12.2 1.8 eq.106
  14.0 2.1 broadcast_in_dim.103
  16.1 2.3 broadcast_in_dim.104
  18.4 2.4 eq.108
  20.8 2.8 eq.109
  23.6 0.6 eq.102
  24.3 1.0 eq.103
  25.3 1.0 fusion.52
  26.3 0.4 fusion.53
  26.7 3.1 fusion.38
  29.8 0.0 all-gather.2.cloned.1.call-start
  29.9 92.0 %all-reduce.2.cloned.1.call-done = f32[128,576]{0,1:T(8,128)} async-done(((f32[128,576]{0,1:T(8,128)}), f32[128,576]{0,1:T(8,128)}) %all-reduce.2.cloned.1.call-update) | async-done | bytes 294928 | tf_op jit(solution)/shard_map/psum | solution.py:116
  122.0 1.0 multiply_reduce_fusion
  123.0 0.9 subtract_convert_fusion.1
  123.9 1.1 multiply_convert_fusion
  125.0 0.7 pad_maximum_fusion.1
  125.7 0.2 reduce-scatter.2.cloned.1.call-start
  125.9 0.7 slice_reduce_fusion.1
  127.8 6.5 %reshape.242 = bf16[256,2,2560]{2,1,0:T(2,128)(2,1)} reshape(bf16[512,2560]{1,0:T(8,128)(2,1)} %param.26) | data formatting | bytes 5242880 | tf_op jit(solution)/shard_map/reshape | solution.py:12
  134.3 6.7 %fusion.50 = (bf16[256,1,2560]{2,1,0:T(2,128)(2,1)S(1)}, bf16[256,1,2560]{2,1,0:T(2,128)(2,1)S(1)}) fusion(bf16[256,2,2560]{2,1,0:T(2,128)(2,1)} %reshape.242), kind=kLoop, calls=%fused_computation.93 | loop fusion | bytes 5242880 | tf_op jit(solution)/shard_map/slice | solution.py:19
  141.0 0.5 copy_bitcast_fusion
  141.5 1.2 copy-done.4
  142.7 0.8 convert_add_fusion
  143.5 11.7 %fusion.36 = bf16[256,4,2560]{2,1,0:T(4,128)(2,1)} fusion(s32[256,2560]{1,0:T(8,128)S(1)} %get-tuple-element.66, s32[256,2560]{1,0:T(8,128)S(1)} %get-tuple-element.65, bf16[256,2560]{1,0:T(8,128)(2,1)S(1)} %get-tuple-element.81, bf16[256,2560]{1,0:T(8,128)(2,1)S(1)} %get-tuple-element.82), kind=kLoop, calls=%fused_computation.44 | loop fusion | flops 20971520 | bytes 13107200 | tf_op jit(solution)/shard_map/add | solution.py:19
  155.1 9.2 %add.104 = bf16[1024,2560]{1,0:T(8,128)(2,1)} reshape(bf16[256,4,2560]{2,1,0:T(4,128)(2,1)} %fusion.36) | data formatting | bytes 10485760 | tf_op jit(solution)/shard_map/add | solution.py:19
  164.4 0.5 fusion.37
  164.9 0.1 pad_maximum_fusion
  165.0 33.0 %all-gather.2.cloned.1.call-done = bf16[4096,576]{0,1:T(8,128)(2,1)} async-done(((bf16[128,576]{0,1:T(8,128)(2,1)}), bf16[4096,576]{0,1:T(8,128)(2,1)}) %all-gather.2.cloned.1.call-update) | async-done | bytes 4718608 | tf_op jit(solution)/shard_map/all_gather | solution.py:118
  198.0 25.8 %conditional.3 = (f32[64,8]{1,0:T(8,128)}, f32[64,8,512]{2,0,1:T(8,128)S(1)}) conditional(s32[]{:T(128)} %convert_element_type.71, () %tuple.23, (s32[64]{0:T(128)S(1)}, bf16[128,8,576]{0,2,1:T(8,128)(2,1)S(1)}, bf16[4096,576]{0,1:T(8,128)(2,1)}) %tuple.24), branch_computations={%region_8.9_spmd, %region_9.12_spmd} | conditional | flops 4586998272 | bytes 84826416 | solution.py:126
  198.0 0.2 iota_compare_fusion.1
  198.2 1.4 copy.48
  199.6 5.9 %fusion.17 = (f32[64,8]{1,0:T(8,128)S(1)}, f32[64,8,4096]{2,1,0:T(8,128)S(1)}) fusion(pred[64,4096]{1,0:T(8,128)(4,1)S(1)} %iota_compare_fusion.1, bf16[128,8,576]{2,1,0:T(8,128)(2,1)S(1)} %copy.48, bf16[4096,576]{0,1:T(8,128)(2,1)} %get-tuple-element.50), kind=kOutput, calls=%fused_computation.22 | convolution fusion | flops 2422210048 | bytes 14551040 | tf_op jit(solution)/shard_map/cond/branch_1_fun/rhc,nc->rhn/dot_general | solution.py:90
  205.6 2.6 fusion.19
  208.2 0.6 copy-done.2
  208.8 0.6 exponential_multiply_fusion.1
  209.4 7.6 %copy.49 = bf16[4096,576]{1,0:T(8,128)(2,1)} copy(bf16[4096,576]{0,1:T(8,128)(2,1)} %get-tuple-element.50) | data formatting | bytes 9437184 | tf_op jit(solution)/shard_map
  217.0 6.1 %fusion.28 = f32[64,8,512]{2,1,0:T(8,128)S(1)} fusion(bf16[4096,576]{1,0:T(8,128)(2,1)} %copy.49, f32[64,8,4096]{2,1,0:T(8,128)} %copy-done.2, f32[64,8]{1,0:T(8,128)S(1)} %compare_select_fusion.1, pred[64,4096]{1,0:T(8,128)(4,1)S(1)} %iota_compare_fusion.1, f32[64,8]{1,0:T(8,128)S(1)} %get-tuple-element.59), kind=kOutput, calls=%fused_computation.33 | convolution fusion | flops 2156134400 | bytes 13897728 | tf_op jit(solution)/shard_map/cond/branch_1_fun/rhn,nl->rhl/dot_general | solution.py:100
  223.2 0.6 copy.58
  223.8 0.8 copy.50
  224.6 26.5 %conditional.2 = (f32[64,8]{1,0:T(8,128)}, f32[64,8,512]{2,0,1:T(8,128)S(1)}) conditional(s32[]{:T(128)} %convert_element_type.63, () %tuple.21, (s32[64]{0:T(128)S(1)}, bf16[128,8,576]{0,2,1:T(8,128)(2,1)S(1)}, bf16[4096,576]{0,1:T(8,128)(2,1)}) %tuple.22), branch_computations={%region_3.4_spmd, %region_4.7_spmd} | conditional | flops 4586998272 | bytes 85875016 | solution.py:126
  224.6 0.9 iota_compare_fusion
  225.5 1.3 copy.44
  226.9 6.0 %fusion = (f32[64,8]{1,0:T(8,128)S(1)}, f32[64,8,4096]{2,1,0:T(8,128)S(1)}) fusion(pred[64,4096]{1,0:T(8,128)(4,1)} %iota_compare_fusion, bf16[128,8,576]{2,1,0:T(8,128)(2,1)S(1)} %copy.44, bf16[4096,576]{0,1:T(8,128)(2,1)} %get-tuple-element.47), kind=kOutput, calls=%fused_computation.2 | convolution fusion | flops 2422210048 | bytes 14551040 | tf_op jit(solution)/shard_map/cond/branch_1_fun/rhc,nc->rhn/dot_general | solution.py:90
  232.9 2.6 fusion.2
  235.5 0.6 copy-done.3
  236.1 0.6 exponential_multiply_fusion
  236.7 7.6 %copy.45 = bf16[4096,576]{1,0:T(8,128)(2,1)} copy(bf16[4096,576]{0,1:T(8,128)(2,1)} %get-tuple-element.47) | data formatting | bytes 9437184 | tf_op jit(solution)/shard_map
  244.4 6.1 %fusion.11 = f32[64,8,512]{2,1,0:T(8,128)S(1)} fusion(bf16[4096,576]{1,0:T(8,128)(2,1)} %copy.45, f32[64,8,4096]{2,1,0:T(8,128)} %copy-done.3, f32[64,8]{1,0:T(8,128)S(1)} %compare_select_fusion, pred[64,4096]{1,0:T(8,128)(4,1)S(1)} %copy-done.5, f32[64,8]{1,0:T(8,128)S(1)} %get-tuple-element.55), kind=kOutput, calls=%fused_computation.13 | convolution fusion | flops 2156134400 | bytes 13897728 | tf_op jit(solution)/shard_map/cond/branch_1_fun/rhn,nl->rhl/dot_general | solution.py:100
  250.5 0.6 copy.56
  251.2 0.9 copy.46
  252.0 0.1 divide_convert_fusion
  252.2 0.1 divide_convert_fusion.1
  252.3 1.7 convolution_convert_fusion.1
  254.1 0.2 fusion.55
  254.2 0.8 fusion.54
  255.0 5.6 %convolution_add_fusion = f32[128,2560]{0,1:T(8,128)} fusion(f32[128,2560]{0,1:T(8,128)S(1)} %fusion.54, bf16[128,1024]{0,1:T(8,128)(2,1)S(1)} %bitcast.53, bf16[1024,2560]{1,0:T(8,128)(2,1)} %add.104), kind=kOutput, calls=%fused_computation.45 | convolution fusion | flops 671416320 | bytes 8126464 | tf_op jit(solution)/shard_map/dot_general | solution.py:142
  260.7 76.5 %reduce-scatter.2.cloned.1.call-done = f32[128,320]{0,1:T(8,128)} async-done(((f32[128,2560]{0,1:T(8,128)}), f32[128,320]{0,1:T(8,128)}) %reduce-scatter.2.cloned.1.call-update) | async-done | bytes 163856 | tf_op jit(solution)/shard_map/reduce_scatter | solution.py:145
  (35 shorter events, 0.2 us)
Async XLA Ops:
  6.5 157.8 %copy-start = (bf16[8,128,512]{2,1,0:T(8,128)(2,1)S(1)}, bf16[8,128,512]{2,1,0:T(8,128)(2,1)}, u32[]{:S(2)}) copy-start(bf16[8,128,512]{2,1,0:T(8,128)(2,1)} %param.24) | copy-start | bytes 3145732
  6.5 3.2 copy-start.6
  6.5 115.4 %all-reduce.2.cloned.1.call-start = ((), (), s32[]{:S(2)}) async-start(), calls=%async_computation.1 | async-start | bytes 589824 | tf_op jit(solution)/shard_map/psum | solution.py:116
  14.0 11.3 %copy-start.11 = (bf16[640,16]{0,1:T(8,128)(2,1)S(1)}, bf16[640,16]{0,1:T(8,128)(2,1)}, u32[]{:S(2)}) copy-start(bf16[640,16]{0,1:T(8,128)(2,1)} %param.20) | copy-start | bytes 61444
  14.0 12.3 %copy-start.10 = (bf16[16,576]{1,0:T(8,128)(2,1)S(1)}, bf16[16,576]{1,0:T(8,128)(2,1)}, u32[]{:S(2)}) copy-start(bf16[16,576]{1,0:T(8,128)(2,1)} %param.21) | copy-start | bytes 55300
  23.6 100.2 %copy-start.12 = (f32[512]{0:T(512)S(1)}, f32[512]{0:T(512)}, u32[]{:S(2)}) copy-start(f32[512]{0:T(512)} %param.22) | copy-start | bytes 6148
  29.8 168.2 %all-gather.2.cloned.1.call-start = ((), (), s32[]{:S(2)}) async-start(), calls=%async_computation.2 | async-start | bytes 4866048 | tf_op jit(solution)/shard_map/all_gather | solution.py:118
  125.7 211.5 %reduce-scatter.2.cloned.1.call-start = ((), (), s32[]{:S(2)}) async-start(), calls=%async_computation.3 | async-start | bytes 1474560 | tf_op jit(solution)/shard_map/reduce_scatter | solution.py:145
  141.0 1.7 copy-start.4
  155.1 9.2 %copy-start.7 = (bf16[128,8,192]{0,2,1:T(8,128)(2,1)S(1)}, bf16[128,8,192]{0,2,1:T(8,128)(2,1)}, u32[]{:S(2)}) copy-start(bf16[128,8,192]{0,2,1:T(8,128)(2,1)} %param.23) | copy-start | bytes 1179652
  205.5 3.2 copy-start.2
  226.9 6.1 %copy-start.5 = (pred[64,4096]{1,0:T(8,128)(4,1)S(1)}, pred[64,4096]{1,0:T(8,128)(4,1)}, u32[]{:S(2)}) copy-start(pred[64,4096]{1,0:T(8,128)(4,1)} %iota_compare_fusion) | copy-start | bytes 786436 | tf_op jit(solution)/shard_map/cond
  232.9 3.2 copy-start.3
  251.1 2.9 copy-start.9
  251.2 3.1 copy-start.8
  254.2 83.0 %copy-start.1 = (bf16[8,128,512]{2,1,0:T(8,128)(2,1)S(1)}, bf16[8,128,512]{2,1,0:T(8,128)(2,1)}, u32[]{:S(2)}) copy-start(bf16[8,128,512]{2,1,0:T(8,128)(2,1)} %param.24) | copy-start | bytes 3145732
Sparse Core Ops, SparseCore 0:
  30.0 91.9 all-reduce.1
  125.8 72.1 all-gather.1
  260.8 76.3 reduce-scatter.1
where the time goes:
time: 346 us; the launch traced here: 344 us
  waiting for transfers between devices  202 us (58%)
  local copies, waits for them, and re-layouts  63.9 us (18%)
  matrix products  37.6 us (11%)
  other arithmetic  25.7 us (7%)
  between operations  14.6 us (4%)
    psum x1, waiting for transfers between devices, local(): whole = lax.psum(partial_raw, 'head')  92 us
    reduce_scatter x1, waiting for transfers between devices, local(): return lax.psum_scatter(terms, 'head', scatter_dimension=1, tiled=True)  76.5 us
    all_gather x1, waiting for transfers between devices, local(): piece = lax.all_gather(cache, 'ctx', axis=0, tiled=True)  33 us
    another operation x4, local copies, waits for them, and re-layouts  18 us
    dot_general x2, matrix products, update_group(): jnp.einsum('rhn,nl->rhl', weights.astype(jnp.bfloat16), piece[:, :lat_wid...  12.3 us
    dot_general x2, matrix products, update_group(): jnp.einsum('rhc,nc->rhn', query_rows, piece, preferred_element_type=jnp.f...  12 us
    add x1, other arithmetic, densify(): jnp.where(slots == first[:, None, :], pairs[:, 0:1, :], nothing)  11.7 us
    add x1, local copies, waits for them, and re-layouts, densify(): jnp.where(slots == first[:, None, :], pairs[:, 0:1, :], nothing)  9.2 us
  transfers between devices with their start and end apart: 3, of which 3 were waited for; matrix products, arithmetic and copies ran while one was open for 11% of the time, Pallas kernels for 0%

commit v1 on v0

v1 whole, which is shorter than its diff:
```python
import functools
import math

import jax
import jax.numpy as jnp
from jax import lax
from jax.experimental import pallas as pl
from jax.experimental.pallas import tpu as pltpu
from jax.sharding import PartitionSpec as P

BF16 = jnp.bfloat16
F32 = jnp.float32
MIB = 1024 * 1024
HEADS = 8
ROWS = 128
PIECE = ROWS // HEADS
LAT = 512
ROPE = 64
WIDTH = LAT + ROPE
NOPE = 128
VDIM = 128
CHIPS = 16
GROUP = 4
KEYS = GROUP * ROWS
BLOCK = 256
COLS = 640
LOG2E = 1.4426950408889634


def dot(a, b):
    return jnp.dot(a, b, preferred_element_type=F32)


def one_hot(shape, column_of_row):
    rows = lax.broadcasted_iota(jnp.int32, shape, 0)
    columns = lax.broadcasted_iota(jnp.int32, shape, 1)
    return jnp.where(columns == column_of_row(rows), 1.0, 0.0).astype(BF16)


def unpair(count):
    half = count // 2
    return one_hot((count, count), lambda r: jnp.where(r < half, 2 * r, 2 * (r - half) + 1))


def by_slot():
    rows = lax.broadcasted_iota(jnp.int32, (128, 128), 0)
    columns = lax.broadcasted_iota(jnp.int32, (128, 128), 1)
    return jnp.where(rows == 4 * (columns % 32) + columns // 32, 1.0, 0.0).astype(BF16)


def densify(values_ref, pattern_ref, dense_ref):
    total = values_ref.shape[0]
    begin = 0
    while begin < total:
        count = min(256, total - begin)
        half = count // 2
        pair = dot(unpair(count), values_ref[begin : begin + count, :])
        v0, v1 = pair[:half], pair[half:]
        p = pattern_ref[begin // 2 : begin // 2 + half, :]
        slots = (
            jnp.where(p < 3, v0, 0.0),
            jnp.where(p == 0, v1, jnp.where((p == 3) | (p == 4), v0, 0.0)),
            jnp.where((p == 1) | (p == 3), v1, jnp.where(p == 5, v0, 0.0)),
            jnp.where((p == 2) | (p >= 4), v1, 0.0),
        )
        for k, slot in enumerate(slots):
            slot = slot.astype(BF16)
            for b in range(half // 32):
                row = 2 * begin + 128 * b + 32 * k
                dense_ref[row : row + 32, :] = slot[32 * b : 32 * b + 32]
        begin += count


def thirds(x):
    high = x.astype(BF16)
    rest = x - high.astype(F32)
    middle = rest.astype(BF16)
    low = (rest - middle.astype(F32)).astype(BF16)
    return high, middle, low


def turn(x, table):
    half = ROPE // 2
    swapped = jnp.concatenate([x[:, half:], x[:, :half]], axis=1)
    return x * table[:, :ROPE] + swapped * table[:, ROPE:]


def project_kernel(tokens_ref, values_ref, pattern_ref, down_ref, up_ref, raw_ref, dense_ref):
    densify(values_ref, pattern_ref, dense_ref)
    order = by_slot()
    tokens = tokens_ref[...]
    parts = [dot(tokens[:, b : b + 128], order).astype(BF16) for b in range(0, tokens.shape[1], 128)]
    raw = dot(jnp.concatenate(parts, axis=1), dense_ref[...])
    up = up_ref[...]
    for term in thirds(dot(tokens, down_ref[...])):
        raw += dot(term, up)
    raw_ref[...] = raw.reshape(raw_ref.shape)


def query_kernel(queries_ref, absorb_ref, table_ref, out_ref):
    table = table_ref[...]
    for h in range(HEADS):
        rows = slice(h * ROWS, (h + 1) * ROWS)
        out_ref[rows, :LAT] = dot(queries_ref[h, :, :NOPE], absorb_ref[h]).astype(BF16)
        out_ref[rows, LAT:] = turn(queries_ref[h, :, NOPE:].astype(F32), table).astype(BF16)


def finish_kernel(where_ref, parts_ref, gain_ref, table_ref, out_ref):
    raw = parts_ref[0]
    for h in range(1, HEADS):
        raw += parts_ref[h]
    latent = raw[:, :LAT]
    meansq = jnp.mean(latent * latent, axis=-1, keepdims=True)
    normed = (latent * lax.rsqrt(meansq + 1e-06) * gain_ref[...]).astype(BF16)
    table = table_ref[pl.ds(pl.multiple_of(where_ref[2] * PIECE, PIECE), PIECE), :]
    turned = turn(raw[:, LAT:], table).astype(BF16)
    for c in range(CHIPS):
        out_ref[c, :, :LAT] = normed
        out_ref[c, :, LAT:] = turned


def attend(where_ref, q_ref, keys_ref, m_ref, l_ref, acc_ref, key_core, scale):
    chip, core = where_ref[0], where_ref[1]

    def chunk(j, masked):
        keys = jnp.concatenate(
            [keys_ref[:, GROUP * j + b].reshape(ROWS, WIDTH) for b in range(GROUP)], axis=0
        )
        if masked:
            row = lax.broadcasted_iota(jnp.int32, (BLOCK, KEYS), 0) % ROWS
            column = lax.broadcasted_iota(jnp.int32, (BLOCK, KEYS), 1)
            ahead = (2 * chip + core) * ROWS + row
            place = (2 * (GROUP * j + column // ROWS) + key_core) * ROWS + column % ROWS
            visible = place <= ahead
        for b in range(HEADS * ROWS // BLOCK):
            rows = slice(b * BLOCK, (b + 1) * BLOCK)
            scores = lax.dot_general(
                q_ref[rows, :], keys, (((1,), (1,)), ((), ())), preferred_element_type=F32
            ) * scale
            if masked:
                scores = jnp.where(visible, scores, -jnp.inf)
            old = m_ref[rows, :]
            new = jnp.maximum(old, jnp.max(scores, axis=1, keepdims=True))
            factor = jnp.exp2(old - new)
            weights = jnp.exp2(scores - jnp.concatenate([new] * (KEYS // 128), axis=1))
            part = weights[:, :128]
            for c in range(128, KEYS, 128):
                part += weights[:, c : c + 128]
            m_ref[rows, :] = new
            l_ref[rows, :] = l_ref[rows, :] * factor + part
            acc_ref[rows, :] = acc_ref[rows, :] * jnp.concatenate(
                [factor] * (LAT // 128), axis=1
            ) + dot(weights.astype(BF16), keys[:, :LAT])

    last = chip // GROUP

    @pl.loop(0, last)
    def _(j):
        chunk(j, False)

    chunk(last, True)


def first_kernel(scale, where_ref, q_ref, keys_ref, m_ref, l_ref, acc_ref):
    m_ref[...] = jnp.full(m_ref.shape, -jnp.inf, F32)
    l_ref[...] = jnp.zeros(l_ref.shape, F32)
    acc_ref[...] = jnp.zeros(acc_ref.shape, F32)
    attend(where_ref, q_ref, keys_ref, m_ref, l_ref, acc_ref, where_ref[1], scale)


def second_kernel(
    scale, where_ref, q_ref, keys_ref, m_in, l_in, acc_in, absorb_ref, down_ref,
    flat_ref, low_ref, m_ref, l_ref, acc_ref,
):
    m_ref[...] = m_in[...]
    l_ref[...] = l_in[...]
    acc_ref[...] = acc_in[...]
    attend(where_ref, q_ref, keys_ref, m_ref, l_ref, acc_ref, 1 - where_ref[1], scale)
    order = by_slot()
    lowrank = jnp.zeros((ROWS, down_ref.shape[1]), F32)
    for h in range(HEADS):
        rows = slice(h * ROWS, (h + 1) * ROWS)
        total = jnp.sum(l_ref[rows, :], axis=1, keepdims=True)
        attended = (acc_ref[rows, :] / total).astype(BF16)
        out = dot(attended, absorb_ref[h]).astype(BF16)
        lowrank += dot(out, down_ref[h * VDIM : (h + 1) * VDIM, :])
        flat_ref[:, h * VDIM : (h + 1) * VDIM] = dot(out, order).astype(BF16)
    for n, term in enumerate(thirds(lowrank)):
        low_ref[n] = term


def output_kernel(flat_ref, low_ref, values_ref, pattern_ref, up_ref, out_ref, dense_ref):
    densify(values_ref, pattern_ref, dense_ref)
    terms = dot(flat_ref[...], dense_ref[...])
    up = up_ref[...]
    for n in range(3):
        terms += dot(low_ref[n], up)
    out_ref[...] = terms.T.astype(BF16)


def sum_kernel(parts_ref, out_ref):
    total = parts_ref[0].astype(F32)
    for h in range(1, HEADS):
        total += parts_ref[h].astype(F32)
    out_ref[...] = total.T


def shape(*dims, dtype=F32):
    return jax.ShapeDtypeStruct(dims, dtype)


def params(mib):
    return pltpu.CompilerParams(vmem_limit_bytes=mib * MIB)


VMEM = pl.BlockSpec(memory_space=pltpu.VMEM)
SMEM = pl.BlockSpec(memory_space=pltpu.SMEM)


def local(
    tokens, kv_values, kv_pattern, kv_down, kv_up, kv_gain, queries, absorb_k, absorb_v,
    o_values, o_pattern, o_down, o_up,
):
    ctx = lax.axis_index("ctx")
    head = lax.axis_index("head")
    where = jnp.stack([ctx // 2, ctx % 2, head]).astype(jnp.int32)
    scale = LOG2E / math.sqrt(queries.shape[2])
    out_cols = o_values.shape[1]

    raw = pl.pallas_call(
        project_kernel,
        out_shape=shape(HEADS, PIECE, WIDTH),
        in_specs=[VMEM] * 5,
        out_specs=VMEM,
        scratch_shapes=[pltpu.VMEM((tokens.shape[1], WIDTH), BF16)],
        compiler_params=params(24),
        name="project",
    )(tokens, kv_values, kv_pattern, kv_down, kv_up)
    parts = lax.all_to_all(raw, "head", 0, 0, tiled=True)

    half = ROPE // 2
    freqs = 10000.0 ** (-jnp.arange(half, dtype=F32) / half)
    positions = ctx * ROWS + jnp.arange(ROWS, dtype=jnp.int32)
    angles = positions.astype(F32)[:, None] * freqs
    cos, sin = jnp.cos(angles), jnp.sin(angles)
    table = jnp.concatenate([cos, cos, -sin, sin], axis=1)

    piece = pl.pallas_call(
        finish_kernel,
        out_shape=shape(CHIPS, PIECE, WIDTH, dtype=BF16),
        in_specs=[SMEM, VMEM, VMEM, VMEM],
        out_specs=VMEM,
        compiler_params=params(24),
        name="finish",
    )(where, parts, kv_gain.reshape(1, LAT), table)

    chips = [[2 * chip + core for chip in range(CHIPS)] for core in range(2)]
    column = lax.all_to_all(piece, "ctx", 0, 0, tiled=True, axis_index_groups=chips)
    keys = lax.all_to_all(
        jnp.broadcast_to(column[None], (HEADS,) + column.shape), "head", 0, 0, tiled=True
    )
    others = lax.ppermute(keys, "ctx", [(i, i ^ 1) for i in range(2 * CHIPS)])

    query = pl.pallas_call(
        query_kernel,
        out_shape=shape(HEADS * ROWS, WIDTH, dtype=BF16),
        in_specs=[VMEM] * 3,
        out_specs=VMEM,
        compiler_params=params(24),
        name="query",
    )(jnp.transpose(queries, (1, 0, 2)), absorb_k, table)

    state = (
        shape(HEADS * ROWS, 128),
        shape(HEADS * ROWS, 128),
        shape(HEADS * ROWS, LAT),
    )
    work = pl.CostEstimate(
        flops=2 * HEADS * ROWS * CHIPS * ROWS * (WIDTH + LAT),
        bytes_accessed=8 * MIB,
        transcendentals=HEADS * ROWS * CHIPS * ROWS,
    )
    state = pl.pallas_call(
        functools.partial(first_kernel, scale),
        out_shape=state,
        in_specs=[SMEM, VMEM, VMEM],
        out_specs=(VMEM,) * 3,
        compiler_params=params(32),
        cost_estimate=work,
        name="first",
    )(where, query, keys)
    flat, low = pl.pallas_call(
        functools.partial(second_kernel, scale),
        out_shape=(
            shape(ROWS, HEADS * VDIM, dtype=BF16),
            shape(3, ROWS, o_down.shape[1], dtype=BF16),
        ),
        in_specs=[SMEM] + [VMEM] * 7,
        out_specs=(VMEM,) * 2,
        scratch_shapes=[
            pltpu.VMEM((HEADS * ROWS, 128), F32),
            pltpu.VMEM((HEADS * ROWS, 128), F32),
            pltpu.VMEM((HEADS * ROWS, LAT), F32),
        ],
        compiler_params=params(32),
        cost_estimate=work,
        name="second",
    )(where, query, others, *state, absorb_v, o_down)

    terms = pl.pallas_call(
        output_kernel,
        grid=(out_cols // COLS,),
        out_shape=shape(out_cols, ROWS, dtype=BF16),
        in_specs=[
            pl.BlockSpec((ROWS, HEADS * VDIM), lambda i: (0, 0)),
            pl.BlockSpec((3, ROWS, o_up.shape[0]), lambda i: (0, 0, 0)),
            pl.BlockSpec((o_values.shape[0], COLS), lambda i: (0, i)),
            pl.BlockSpec((o_pattern.shape[0], COLS), lambda i: (0, i)),
            pl.BlockSpec((o_up.shape[0], COLS), lambda i: (0, i)),
        ],
        out_specs=pl.BlockSpec((COLS, ROWS), lambda i: (i, 0)),
        scratch_shapes=[pltpu.VMEM((2 * o_values.shape[0], COLS), BF16)],
        compiler_params=params(32),
        name="output",
    )(flat, low, o_values, o_pattern, o_up)
    shares = lax.all_to_all(
        terms.reshape(HEADS, out_cols // HEADS, ROWS), "head", 0, 0, tiled=True
    )
    return pl.pallas_call(
        sum_kernel,
        out_shape=shape(ROWS, out_cols // HEADS),
        in_specs=[VMEM],
        out_specs=VMEM,
        compiler_params=params(24),
        name="total",
    )(shares)


def solution(mesh):
    in_specs = (
        P("ctx", "head"),
        P("head", None),
        P("head", None),
        P("head", None),
        P(),
        P(),
        P("ctx", "head", None),
        P("head", None, None),
        P("head", None, None),
        P("head", None),
        P("head", None),
        P("head", None),
        P(),
    )
    out_specs = P("ctx", "head")
    return jax.shard_map(local, mesh=mesh, in_specs=in_specs, out_specs=out_specs, check_vma=False)
```

time: 346 us -> 123 us (0.36)
  the two profiles are of different devices: /device:TPU:2 before, /device:TPU:130 now
where the time goes in v1:
time: 123 us; the launch traced here: 122 us
  blocking collectives  68 us (55%)
  Pallas kernels  30.7 us (25%)
  waiting for transfers between devices  8.78 us (7%)
  local copies, waits for them, and re-layouts  8.16 us (7%)
  starting transfers between devices  6.03 us (5%)
    all_to_all x1, blocking collectives, local(): lax.all_to_all(jnp.broadcast_to(column[None], (HEADS,) + column.shape), '...  37.5 us
    all_to_all x1, blocking collectives, local(): lax.all_to_all(terms.reshape(HEADS, out_cols // HEADS, ROWS), 'head', 0,...  16.4 us
    all_to_all x1, blocking collectives, local(): lax.all_to_all(piece, 'ctx', 0, 0, tiled=True, axis_index_groups=chips)  14.1 us
    pallas_call x1, Pallas kernels, local(): pl.pallas_call(functools.partial(second_kernel, scale), out_shape=(shape(...  12.7 us
    pallas_call x1, Pallas kernels, local(): pl.pallas_call(functools.partial(first_kernel, scale), out_shape=state, i...  10.1 us
    all_to_all x1, waiting for transfers between devices, local(): parts = lax.all_to_all(raw, 'head', 0, 0, tiled=True)  8.78 us
    unnamed x25, local copies, waits for them, and re-layouts  7.17 us
    all_to_all x1, starting transfers between devices, local(): parts = lax.all_to_all(raw, 'head', 0, 0, tiled=True)  6.03 us
  transfers between devices with their start and end apart: 2, of which 1 were waited for; matrix products, arithmetic and copies ran while one was open for 2% of the time, Pallas kernels for 9%

profile of v1, /device:TPU:130, one launch (start us, length us, event | category | flops | bytes accessed | tf_op | source)
XLA Modules:
  0.0 122.4 jit_solution(9573114616277237737)
XLA Ops:
  0.0 0.0 copy-start.8
  0.0 0.9 copy.20.down_ref
  0.9 0.0 copy-start.3
  0.9 1.0 copy-done.3
  1.9 0.0 copy-start.4
  1.9 1.0 copy-done.4
  2.9 0.0 copy-start.5
  2.9 0.9 copy-done.5
  3.8 0.0 copy-start.7
  3.8 0.7 copy-done.7
  4.6 1.7 %project.1 = f32[8,16,576]{2,1,0:T(8,128)} custom-call(bf16[128,640]{1,0:T(8,128)(2,1)S(1)} %copy-done.5, bf16[320,576]{1,0:T(8,128)(2,1)S(1)} %copy-done.3, s32[160,576]{1,0:T(8,128)S(1)} %copy-done.4, bf16[640,16]{1,0:T(8,128)(2,1)S(1)} %copy.20.down_ref, bf16[16,576]{1,0:T(8,128)(2,1)S(1)} %copy-done.7), custom_call_target="tpu_custom_call" | custom-call | tf_op jit(solution)/shard_map/project/pallas_call | solution.py:230
  6.3 6.0 %all-to-all-start = ((f32[8,16,576]{2,1,0:T(8,128)}), f32[8,16,576]{2,1,0:T(8,128)S(1)}, u32[]{:S(2)}, u32[]{:S(2)}) async-start(f32[8,16,576]{2,1,0:T(8,128)} %project.1), calls=%async_computation | async-start | bytes 655360 | tf_op jit(solution)/shard_map/all_to_all | solution.py:239
  12.3 0.3 multiply_cosine_fusion
  12.6 0.1 pad_add_fusion.where_ref
  12.7 0.1 pad_maximum_fusion.table_ref
  12.8 8.8 %all-to-all-done.parts_ref = f32[8,16,576]{2,1,0:T(8,128)S(1)} async-done(((f32[8,16,576]{2,1,0:T(8,128)}), f32[8,16,576]{2,1,0:T(8,128)S(1)}, u32[]{:S(2)}, u32[]{:S(2)}) %all-to-all-start) | async-done | bytes 294944 | tf_op jit(solution)/shard_map/all_to_all | solution.py:239
  21.6 0.0 copy-done.8
  21.6 0.7 finish.1
  22.3 14.1 %all_to_all.20 = bf16[16,16,576]{2,1,0:T(8,128)(2,1)S(1)} all-to-all(bf16[16,16,576]{2,1,0:T(8,128)(2,1)S(1)} %finish.1), channel_id=1, replica_groups={{0,16,32,48,64,80,96,112,128,144,160,176,192,208,224,240},{8,24,40,56,7..., dimensions={0} | all-to-all | bytes 589824 | tf_op jit(solution)/shard_map/all_to_all | solution.py:258
  36.4 0.2 broadcast_in_dim.2
  36.6 0.0 copy-start.10
  36.6 37.5 %all_to_all.21.keys_ref = bf16[8,16,16,576]{3,2,1,0:T(8,128)(2,1)S(1)} all-to-all(bf16[8,16,16,576]{3,2,1,0:T(8,128)(2,1)S(1)} %broadcast_in_dim.2), channel_id=1, replica_groups=mesh['ctx'=32,'head'=8] {'head'}, dimensions={0} | all-to-all | bytes 4718592 | tf_op jit(solution)/shard_map/all_to_all | solution.py:259
  74.1 0.0 collective-permute-start
  74.1 1.2 copy.18
  75.3 0.0 copy-done.10
  75.3 0.2 copy.21.down_ref
  75.5 0.0 copy-start.2
  75.5 1.2 copy-done.2
  76.7 0.5 query.1.q_ref
  77.2 0.0 copy-start.9
  77.2 10.1 %first.1 = (f32[1024,128]{1,0:T(8,128)S(1)}, f32[1024,128]{1,0:T(8,128)S(1)}, f32[1024,512]{1,0:T(8,128)S(1)}) custom-call(s32[3]{0:T(128)S(1)} %pad_add_fusion.where_ref, bf16[1024,576]{1,0:T(8,128)(2,1)S(1)} %query.1.q_ref, bf16[8,16,16,576]{3,2,1,0:T(8,128)(2,1)S(1)} %all_to_all.21.keys_ref), custom_call_target="tpu_custom_call" | custom-call | flops 4563402752 | bytes 8388608 | tf_op jit(solution)/shard_map/first/pallas_call | solution.py:283
  87.3 0.0 collective-permute-done.keys_ref
  87.3 0.0 copy-done.9
  87.4 0.0 copy-start
  87.4 0.0 copy-start.1
  87.4 0.0 copy-start.6
  87.4 12.7 %second.1 = (bf16[128,1024]{1,0:T(8,128)(2,1)S(1)}, bf16[3,128,16]{2,1,0:T(8,128)(2,1)S(1)}) custom-call(s32[3]{0:T(128)S(1)} %pad_add_fusion.where_ref, bf16[1024,576]{1,0:T(8,128)(2,1)S(1)} %query.1.q_ref, bf16[8,16,16,576]{3,2,1,0:T(8,128)(2,1)} %collective-permute-done.keys_ref, f32[1024,128]{1,0:T(8,128)S(1)} %get-tuple-element.10.m_in, ...), custom_call_target="tpu_custom_call" | custom-call | flops 4563402752 | bytes 8388608 | tf_op jit(solution)/shard_map/second/pallas_call | solution.py:292
  100.1 0.0 copy-done
  100.1 0.0 copy-done.1
  100.1 0.0 copy-done.6
  100.1 5.0 %output.1 = bf16[2560,128]{1,0:T(8,128)(2,1)S(1)} custom-call(bf16[128,1024]{1,0:T(8,128)(2,1)S(1)} %get-tuple-element.13.flat_ref, bf16[3,128,16]{2,1,0:T(8,128)(2,1)S(1)} %get-tuple-element.14.low_ref, bf16[512,2560]{1,0:T(8,128)(2,1)S(1)} %copy-done, s32[256,2560]{1,0:T(8,128)S(1)} %copy-done.1, bf16[16,2560]{1,0:T(8,128)(2,1)S(1)} %copy-done.6), custom_call_target="tpu_custom_call" | custom-call | tf_op jit(solution)/shard_map/output/pallas_call | solution.py:310
  105.1 16.4 %all_to_all.22.parts_ref = bf16[8,320,128]{2,1,0:T(8,128)(2,1)S(1)} all-to-all(bf16[8,320,128]{2,1,0:T(8,128)(2,1)S(1)} %bitcast.6), channel_id=1, replica_groups=mesh['ctx'=32,'head'=8] {'head'}, dimensions={0} | all-to-all | bytes 1310720 | tf_op jit(solution)/shard_map/all_to_all | solution.py:326
  121.5 0.2 total.1
  121.6 0.8 copy.22
  (2 shorter events, 0.0 us)
Async XLA Ops:
  0.0 21.6 %copy-start.8 = (f32[512]{0:T(512)S(1)}, f32[512]{0:T(512)}, u32[]{:S(2)}) copy-start(f32[512]{0:T(512)} %param.18) | copy-start | bytes 6148
  0.9 1.0 copy-start.3
  1.9 1.0 copy-start.4
  2.9 0.9 copy-start.5
  3.8 0.7 copy-start.7
  6.3 15.4 %all-to-all-start = ((f32[8,16,576]{2,1,0:T(8,128)}), f32[8,16,576]{2,1,0:T(8,128)S(1)}, u32[]{:S(2)}, u32[]{:S(2)}) async-start(f32[8,16,576]{2,1,0:T(8,128)} %project.1), calls=%async_computation | async-start | bytes 655360 | tf_op jit(solution)/shard_map/all_to_all | solution.py:239
  36.6 38.8 %copy-start.10 = (bf16[1024,16]{0,1:T(8,128)(2,1)S(1)}, bf16[1024,16]{0,1:T(8,128)(2,1)}, u32[]{:S(2)}) copy-start(bf16[1024,16]{0,1:T(8,128)(2,1)} %param.24) | copy-start | bytes 98308
  74.1 13.2 %collective-permute-start = (bf16[8,16,16,576]{3,2,1,0:T(8,128)(2,1)S(1)}, bf16[8,16,16,576]{3,2,1,0:T(8,128)(2,1)}, u32[]{:S(2)}, u32[]{:S(2)}) collective-permute-start(bf16[8,16,16,576]{3,2,1,0:T(8,128)(2,1)S(1)} %all_to_all.21.keys_ref), channel_id=1, source_target_pairs={{0,8},{8,0},{16,24},{24,16},{32,40},{40,32},{48,56},{56,48},{64,72... | collective-permute-start | bytes 7077896 | tf_op jit(solution)/shard_map/ppermute | solution.py:262
  75.5 1.2 %copy-start.2 = (bf16[8,128,512]{2,1,0:T(8,128)(2,1)S(1)}, bf16[8,128,512]{2,1,0:T(8,128)(2,1)}, u32[]{:S(2)}) copy-start(bf16[8,128,512]{2,1,0:T(8,128)(2,1)} %absorb_ref.2) | copy-start | bytes 3145732
  77.2 10.1 %copy-start.9 = (bf16[8,512,128]{2,1,0:T(8,128)(2,1)S(1)}, bf16[8,512,128]{2,1,0:T(8,128)(2,1)}, u32[]{:S(2)}) copy-start(bf16[8,512,128]{2,1,0:T(8,128)(2,1)} %absorb_ref.3) | copy-start | bytes 3145732
  87.4 12.7 %copy-start = (bf16[512,2560]{1,0:T(8,128)(2,1)S(1)}, bf16[512,2560]{1,0:T(8,128)(2,1)}, u32[]{:S(2)}) copy-start(bf16[512,2560]{1,0:T(8,128)(2,1)} %values_ref.3) | copy-start | bytes 7864324
  87.4 12.7 %copy-start.1 = (s32[256,2560]{1,0:T(8,128)S(1)}, s32[256,2560]{1,0:T(8,128)}, u32[]{:S(2)}) copy-start(s32[256,2560]{1,0:T(8,128)} %pattern_ref.3) | copy-start | bytes 7864324
  87.4 12.7 %copy-start.6 = (bf16[16,2560]{1,0:T(8,128)(2,1)S(1)}, bf16[16,2560]{1,0:T(8,128)(2,1)}, u32[]{:S(2)}) copy-start(bf16[16,2560]{1,0:T(8,128)(2,1)} %up_ref.3) | copy-start | bytes 245764

commit v2 on v1

v2 whole, which is shorter than its diff:
```python
import functools
import math

import jax
import jax.numpy as jnp
from jax import lax
from jax.experimental import pallas as pl
from jax.experimental.pallas import tpu as pltpu
from jax.sharding import PartitionSpec as P

BF16 = jnp.bfloat16
F32 = jnp.float32
MIB = 1024 * 1024
HEADS = 8
ROWS = 128
ALL = HEADS * ROWS
PIECE = ROWS // HEADS
LAT = 512
ROPE = 64
WIDTH = LAT + ROPE
NOPE = 128
VDIM = 128
CTX = 32
CHIPS = 8
GROUP = 4
KEYS = GROUP * ROWS
COLS = 640
LOG2E = 1.4426950408889634


def dot(a, b):
    return jnp.dot(a, b, preferred_element_type=F32)


def dot_first(a, b):
    return lax.dot_general(a, b, (((0,), (0,)), ((), ())), preferred_element_type=F32)


def dot_last(a, b):
    return lax.dot_general(a, b, (((1,), (1,)), ((), ())), preferred_element_type=F32)


def unpair(count):
    half = count // 2
    rows = lax.broadcasted_iota(jnp.int32, (count, count), 0)
    columns = lax.broadcasted_iota(jnp.int32, (count, count), 1)
    wanted = jnp.where(rows < half, 2 * rows, 2 * (rows - half) + 1)
    return jnp.where(columns == wanted, 1.0, 0.0).astype(BF16)


def by_slot():
    rows = lax.broadcasted_iota(jnp.int32, (128, 128), 0)
    columns = lax.broadcasted_iota(jnp.int32, (128, 128), 1)
    return jnp.where(rows == 4 * (columns % 32) + columns // 32, 1.0, 0.0).astype(BF16)


def densify(values_ref, pattern_ref, dense_ref):
    total = values_ref.shape[0]
    begin = 0
    while begin < total:
        count = min(256, total - begin)
        half = count // 2
        pair = dot(unpair(count), values_ref[begin : begin + count, :])
        v0, v1 = pair[:half], pair[half:]
        p = pattern_ref[begin // 2 : begin // 2 + half, :]
        slots = (
            jnp.where(p < 3, v0, 0.0),
            jnp.where(p == 0, v1, jnp.where((p == 3) | (p == 4), v0, 0.0)),
            jnp.where((p == 1) | (p == 3), v1, jnp.where(p == 5, v0, 0.0)),
            jnp.where((p == 2) | (p >= 4), v1, 0.0),
        )
        for k, slot in enumerate(slots):
            slot = slot.astype(BF16)
            for b in range(half // 32):
                row = 2 * begin + 128 * b + 32 * k
                dense_ref[row : row + 32, :] = slot[32 * b : 32 * b + 32]
        begin += count


def thirds(x):
    high = x.astype(BF16)
    rest = x - high.astype(F32)
    middle = rest.astype(BF16)
    low = (rest - middle.astype(F32)).astype(BF16)
    return high, middle, low


def project_kernel(
    tokens_hbm, values_hbm, pattern_hbm, down_hbm, up_hbm,
    raw_ref, tokens_ref, values_ref, pattern_ref, down_ref, up_ref, dense_ref, sems,
):
    copies = [
        pltpu.make_async_copy(source, target, sems.at[n])
        for n, (source, target) in enumerate(
            (
                (values_hbm, values_ref),
                (pattern_hbm, pattern_ref),
                (tokens_hbm, tokens_ref),
                (down_hbm, down_ref),
                (up_hbm, up_ref),
            )
        )
    ]
    for copy in copies:
        copy.start()
    for copy in copies:
        copy.wait()
    densify(values_ref, pattern_ref, dense_ref)
    order = by_slot()
    tokens = tokens_ref[...]
    parts = [dot(tokens[:, b : b + 128], order).astype(BF16) for b in range(0, tokens.shape[1], 128)]
    raw = dot(jnp.concatenate(parts, axis=1), dense_ref[...])
    up = up_ref[...]
    for term in thirds(dot_last(tokens, down_ref[...])):
        raw += dot(term, up)
    raw_ref[...] = raw.reshape(raw_ref.shape)


def query_kernel(queries_ref, absorb_ref, table_ref, out_ref):
    half = ROPE // 2
    cos, sin = table_ref[:ROPE, :], table_ref[ROPE:, :]
    for h in range(HEADS):
        columns = slice(h * ROWS, (h + 1) * ROWS)
        out_ref[:LAT, columns] = dot_first(absorb_ref[h], queries_ref[h, :NOPE, :]).astype(BF16)
        x = queries_ref[h, NOPE:, :].astype(F32)
        swapped = jnp.concatenate([x[half:], x[:half]], axis=0)
        out_ref[LAT:, columns] = (x * cos + swapped * sin).astype(BF16)


def finish_kernel(where_ref, parts_ref, gain_ref, table_ref, out_ref):
    raw = parts_ref[0]
    for h in range(1, HEADS):
        raw += parts_ref[h]
    latent = raw[:, :LAT]
    meansq = jnp.mean(latent * latent, axis=-1, keepdims=True)
    normed = (latent * lax.rsqrt(meansq + 1e-06) * gain_ref[...]).astype(BF16)
    table = table_ref[pl.ds(pl.multiple_of(where_ref[3] * PIECE, PIECE), PIECE), :]
    x = raw[:, LAT:]
    half = ROPE // 2
    swapped = jnp.concatenate([x[:, half:], x[:, :half]], axis=1)
    turned = (x * table[:, :ROPE] + swapped * table[:, ROPE:]).astype(BF16)
    for c in range(CHIPS):
        out_ref[c, :, :LAT] = normed
        out_ref[c, :, LAT:] = turned


class Rows:
    def __init__(self, where_ref, q_ref, m_ref, l_ref, acc_ref, scale):
        self.chip, self.core = where_ref[1], where_ref[2]
        self.q_ref, self.m_ref, self.l_ref, self.acc_ref = q_ref, m_ref, l_ref, acc_ref
        self.scale = scale

    def clear(self):
        self.m_ref[...] = jnp.full(self.m_ref.shape, -jnp.inf, F32)
        self.l_ref[...] = jnp.zeros(self.l_ref.shape, F32)
        self.acc_ref[...] = jnp.zeros(self.acc_ref.shape, F32)

    def chunk(self, keys_ref, j, key_core=None):
        keys = jnp.concatenate(
            [keys_ref[:, GROUP * j + b].reshape(ROWS, WIDTH) for b in range(GROUP)], axis=0
        )
        scores = dot(keys, self.q_ref[...]) * self.scale
        if key_core is not None:
            query = lax.broadcasted_iota(jnp.int32, (1, ALL), 1) % ROWS
            key = lax.broadcasted_iota(jnp.int32, (KEYS, 1), 0)
            ahead = (2 * self.chip + self.core) * ROWS + query
            place = (2 * (GROUP * j + key // ROWS) + key_core) * ROWS + key % ROWS
            scores = jnp.where(place <= ahead, scores, -jnp.inf)
        old = self.m_ref[...]
        new = jnp.maximum(old, jnp.max(scores, axis=0, keepdims=True))
        factor = jnp.exp2(old - new)
        weights = jnp.exp2(scores - new[:1])
        self.m_ref[...] = new
        self.l_ref[...] = self.l_ref[...] * factor + jnp.sum(
            weights.reshape(KEYS // 8, 8, ALL), axis=0
        )
        self.acc_ref[...] = self.acc_ref[...] * factor[:1] + dot(
            keys[:, :LAT].T, weights.astype(BF16)
        )

    def whole(self, keys_ref, count):
        @pl.loop(0, count)
        def _(j):
            self.chunk(keys_ref, j)

    def causal(self, keys_ref, key_core):
        self.whole(keys_ref, self.chip // GROUP)
        self.chunk(keys_ref, self.chip // GROUP, key_core)

    def head_out(self, h, absorb_ref):
        columns = slice(h * ROWS, (h + 1) * ROWS)
        total = jnp.sum(self.l_ref[:, columns], axis=0, keepdims=True)
        attended = (self.acc_ref[:, columns] / total).astype(BF16)
        return dot_first(absorb_ref[h], attended), self.m_ref[:1, columns] + jnp.log2(total)


def first_kernel(scale, where_ref, own_ref, partner_ref, keys_ref, m_ref, l_ref, acc_ref):
    upper = where_ref[0]
    for q_ref, mine in ((own_ref, upper == 1), (partner_ref, upper == 0)):
        rows = Rows(where_ref, q_ref, m_ref, l_ref, acc_ref, scale)

        @pl.when(mine)
        def _():
            rows.clear()
            if q_ref is own_ref:
                rows.causal(keys_ref, where_ref[2])
            else:
                rows.whole(keys_ref, CHIPS // GROUP)


def second_kernel(
    scale, where_ref, own_ref, partner_ref, keys_ref, absorb_ref, m_in, l_in, acc_in,
    part_ref, m_ref, l_ref, acc_ref,
):
    del m_in, l_in, acc_in
    upper = where_ref[0]

    @pl.when(upper == 1)
    def _():
        rows = Rows(where_ref, own_ref, m_ref, l_ref, acc_ref, scale)
        rows.causal(keys_ref, 1 - where_ref[2])

    @pl.when(upper == 0)
    def _():
        rows = Rows(where_ref, partner_ref, m_ref, l_ref, acc_ref, scale)
        rows.whole(keys_ref, CHIPS // GROUP)
        logs = []
        for h in range(HEADS):
            out, log = rows.head_out(h, absorb_ref)
            part_ref[h * VDIM : (h + 1) * VDIM, :] = out.astype(BF16)
            logs.append(log)
        logs = jnp.concatenate(logs, axis=0)
        terms = [t.astype(F32) for t in thirds(logs)] + [jnp.zeros_like(logs)]
        part_ref[HEADS * VDIM :, :] = jnp.concatenate(terms, axis=0).astype(BF16)


def third_kernel(
    scale, where_ref, own_ref, keys_ref, others_ref, m_in, l_in, acc_in, m_ref, l_ref, acc_ref
):
    del m_in, l_in, acc_in

    @pl.when(where_ref[0] == 0)
    def _():
        rows = Rows(where_ref, own_ref, m_ref, l_ref, acc_ref, scale)
        rows.clear()
        rows.causal(keys_ref, where_ref[2])
        rows.causal(others_ref, 1 - where_ref[2])


def output_kernel(
    where_ref, m_ref, l_ref, acc_ref, part_ref, absorb_ref, down_ref, up_ref, dense_ref,
    out_ref, flat_ref,
):
    upper = where_ref[0]
    rows = Rows(where_ref, None, m_ref, l_ref, acc_ref, None)
    logs = part_ref[HEADS * VDIM :, :].astype(F32)
    logs = logs[:HEADS] + logs[HEADS : 2 * HEADS] + logs[2 * HEADS : 3 * HEADS]
    order = by_slot()
    lowrank = jnp.zeros((down_ref.shape[0], ROWS), F32)
    for h in range(HEADS):
        span = slice(h * VDIM, (h + 1) * VDIM)
        mine, log = rows.head_out(h, absorb_ref)
        other_log = jnp.where(upper == 1, logs[h : h + 1], -jnp.inf)
        top = jnp.maximum(log, other_log)
        weight, other_weight = jnp.exp2(log - top), jnp.exp2(other_log - top)
        other = part_ref[span, :].astype(F32)
        out = (mine * weight + other * other_weight) / (weight + other_weight)
        out = out.astype(BF16)
        lowrank += dot(down_ref[:, span], out)
        flat_ref[span, :] = dot_first(order, out).astype(BF16)
    low = thirds(lowrank)
    for c in range(0, out_ref.shape[0], COLS):
        terms = dot_first(flat_ref[...], dense_ref[:, c : c + COLS])
        for term in low:
            terms += dot_first(term, up_ref[:, c : c + COLS])
        out_ref[c : c + COLS, :] = terms.T.astype(BF16)


def sum_kernel(parts_ref, out_ref):
    total = parts_ref[0].astype(F32)
    for h in range(1, HEADS):
        total += parts_ref[h].astype(F32)
    out_ref[...] = total


def shape(*dims, dtype=F32):
    return jax.ShapeDtypeStruct(dims, dtype)


def params(mib):
    return pltpu.CompilerParams(vmem_limit_bytes=mib * MIB)


def cost(flops, nbytes, exps=0):
    return pl.CostEstimate(flops=flops, bytes_accessed=nbytes, transcendentals=exps)


VMEM = pl.BlockSpec(memory_space=pltpu.VMEM)
SMEM = pl.BlockSpec(memory_space=pltpu.SMEM)
ANY = pl.BlockSpec(memory_space=pl.ANY)


def tables(positions):
    half = ROPE // 2
    freqs = 10000.0 ** (-jnp.arange(half, dtype=F32) / half)
    angles = positions.astype(F32)[:, None] * freqs
    cos, sin = jnp.cos(angles), jnp.sin(angles)
    return jnp.concatenate([cos, cos, -sin, sin], axis=1)


def local(
    tokens, kv_values, kv_pattern, kv_down, kv_up, kv_gain, queries, absorb_k, absorb_v,
    o_values, o_pattern, o_down, o_up,
):
    ctx = lax.axis_index("ctx")
    head = lax.axis_index("head")
    upper = ctx // (2 * CHIPS)
    where = jnp.stack([upper, (ctx // 2) % CHIPS, ctx % 2, head]).astype(jnp.int32)
    scale = LOG2E / math.sqrt(queries.shape[2])
    out_cols = o_values.shape[1]
    rank = o_down.shape[1]

    columns = jnp.transpose(queries, (1, 2, 0))
    partner = lax.ppermute(columns, "ctx", [(i + 2 * CHIPS, i) for i in range(2 * CHIPS)])

    raw = pl.pallas_call(
        project_kernel,
        out_shape=shape(HEADS, PIECE, WIDTH),
        in_specs=[ANY] * 5,
        out_specs=VMEM,
        scratch_shapes=[
            pltpu.VMEM(tokens.shape, BF16),
            pltpu.VMEM(kv_values.shape, BF16),
            pltpu.VMEM(kv_pattern.shape, jnp.int32),
            pltpu.VMEM(kv_down.shape[::-1], BF16),
            pltpu.VMEM(kv_up.shape, BF16),
            pltpu.VMEM((tokens.shape[1], WIDTH), BF16),
            pltpu.SemaphoreType.DMA((5,)),
        ],
        compiler_params=params(24),
        name="project",
    )(tokens, kv_values, kv_pattern, kv_down.T, kv_up)
    parts = lax.all_to_all(raw, "head", 0, 0, tiled=True)

    positions = ctx * ROWS + jnp.arange(ROWS, dtype=jnp.int32)
    table = tables(positions)
    partner_table = tables(positions + 2 * CHIPS * ROWS)

    piece = pl.pallas_call(
        finish_kernel,
        out_shape=shape(CHIPS, PIECE, WIDTH, dtype=BF16),
        in_specs=[SMEM, VMEM, VMEM, VMEM],
        out_specs=VMEM,
        compiler_params=params(16),
        name="finish",
    )(where, parts, kv_gain.reshape(1, LAT), table)

    along_z = [
        [(u * CHIPS + chip) * 2 + core for chip in range(CHIPS)]
        for u in range(2)
        for core in range(2)
    ]
    column = lax.all_to_all(piece, "ctx", 0, 0, tiled=True, axis_index_groups=along_z)
    keys = lax.all_to_all(
        jnp.broadcast_to(column[None], (HEADS,) + column.shape), "head", 0, 0, tiled=True
    )
    others = lax.ppermute(keys, "ctx", [(i, i ^ 1) for i in range(CTX)])

    def query(x, t):
        return pl.pallas_call(
            query_kernel,
            out_shape=shape(WIDTH, ALL, dtype=BF16),
            in_specs=[VMEM] * 3,
            out_specs=VMEM,
            compiler_params=params(16),
            cost_estimate=cost(2 * ALL * NOPE * LAT, 4 * MIB),
            name="query",
        )(x, absorb_k, t.T)

    own_query = query(columns, table)
    partner_query = query(partner, partner_table)

    dense = pl.pallas_call(
        densify,
        grid=(out_cols // COLS,),
        out_shape=shape(2 * o_values.shape[0], out_cols, dtype=BF16),
        in_specs=[
            pl.BlockSpec((o_values.shape[0], COLS), lambda i: (0, i)),
            pl.BlockSpec((o_pattern.shape[0], COLS), lambda i: (0, i)),
        ],
        out_specs=pl.BlockSpec((2 * o_values.shape[0], COLS), lambda i: (0, i)),
        compiler_params=params(24),
        cost_estimate=cost(2 * 256 * o_values.size, 12 * MIB),
        name="densify",
    )(o_values, o_pattern)

    state = (shape(8, ALL), shape(8, ALL), shape(LAT, ALL))
    scores = ALL * CHIPS * ROWS
    work = cost(2 * scores * (WIDTH + LAT), 8 * MIB, scores)
    first = pl.pallas_call(
        functools.partial(first_kernel, scale),
        out_shape=state,
        in_specs=[SMEM, VMEM, VMEM, VMEM],
        out_specs=(VMEM,) * 3,
        compiler_params=params(32),
        cost_estimate=work,
        name="first",
    )(where, own_query, partner_query, keys)
    part, *second = pl.pallas_call(
        functools.partial(second_kernel, scale),
        out_shape=(shape(HEADS * VDIM + 4 * HEADS, ROWS, dtype=BF16),) + state,
        in_specs=[SMEM] + [VMEM] * 7,
        out_specs=(VMEM,) * 4,
        input_output_aliases={5: 1, 6: 2, 7: 3},
        compiler_params=params(32),
        cost_estimate=work,
        name="second",
    )(where, own_query, partner_query, others, absorb_v, *first)
    received = lax.ppermute(part, "ctx", [(i, i + 2 * CHIPS) for i in range(2 * CHIPS)])
    third = pl.pallas_call(
        functools.partial(third_kernel, scale),
        out_shape=state,
        in_specs=[SMEM] + [VMEM] * 6,
        out_specs=(VMEM,) * 3,
        input_output_aliases={4: 0, 5: 1, 6: 2},
        compiler_params=params(32),
        cost_estimate=work,
        name="third",
    )(where, own_query, keys, others, *second)

    terms = pl.pallas_call(
        output_kernel,
        out_shape=shape(out_cols, ROWS, dtype=BF16),
        in_specs=[SMEM] + [VMEM] * 8,
        out_specs=VMEM,
        scratch_shapes=[pltpu.VMEM((HEADS * VDIM, ROWS), BF16)],
        compiler_params=params(32),
        cost_estimate=cost(2 * ROWS * HEADS * VDIM * out_cols, 8 * MIB),
        name="output",
    )(where, *third, received, absorb_v, o_down.T, o_up, dense)
    shares = lax.all_to_all(
        terms.reshape(HEADS, out_cols // HEADS, ROWS), "head", 0, 0, tiled=True
    )
    return pl.pallas_call(
        sum_kernel,
        out_shape=shape(out_cols // HEADS, ROWS),
        in_specs=[VMEM],
        out_specs=VMEM,
        compiler_params=params(16),
        name="total",
    )(shares).T


def solution(mesh):
    in_specs = (
        P("ctx", "head"),
        P("head", None),
        P("head", None),
        P("head", None),
        P(),
        P(),
        P("ctx", "head", None),
        P("head", None, None),
        P("head", None, None),
        P("head", None),
        P("head", None),
        P("head", None),
        P(),
    )
    out_specs = P("ctx", "head")
    return jax.shard_map(local, mesh=mesh, in_specs=in_specs, out_specs=out_specs, check_vma=False)
```

time: 123 us -> 115 us (0.935)
  the two profiles are of different devices: /device:TPU:130 before, /device:TPU:2 now
where the time goes in v2:
time: 115 us; the launch traced here: 114 us
  blocking collectives  53.5 us (47%)
  waiting for transfers between devices  25.9 us (23%)
  Pallas kernels  18.5 us (16%)
  starting transfers between devices  10.7 us (9%)
  local copies, waits for them, and re-layouts  4.61 us (4%)
    all_to_all x1, blocking collectives, local(): lax.all_to_all(jnp.broadcast_to(column[None], (HEADS,) + column.shape), '...  20.8 us
    all_to_all x1, blocking collectives, local(): lax.all_to_all(piece, 'ctx', 0, 0, tiled=True, axis_index_groups=along_z)  17.7 us
    all_to_all x1, blocking collectives, local(): lax.all_to_all(terms.reshape(HEADS, out_cols // HEADS, ROWS), 'head', 0,...  15 us
    all_to_all x1, waiting for transfers between devices, local(): parts = lax.all_to_all(raw, 'head', 0, 0, tiled=True)  8.86 us
    ppermute x1, waiting for transfers between devices, local(): lax.ppermute(part, 'ctx', [(i, i + 2 * CHIPS) for i in range(2 * CHIPS)])  8.57 us
    ppermute x1, waiting for transfers between devices, local(): lax.ppermute(columns, 'ctx', [(i + 2 * CHIPS, i) for i in range(2 * CHIPS)])  8.51 us
    all_to_all x1, starting transfers between devices, local(): parts = lax.all_to_all(raw, 'head', 0, 0, tiled=True)  6.03 us
    unnamed x26, local copies, waits for them, and re-layouts  4.41 us
  transfers between devices with their start and end apart: 4, of which 3 were waited for; matrix products, arithmetic and copies ran while one was open for 0% of the time, Pallas kernels for 7%

profile of v2, /device:TPU:2, one launch (start us, length us, event | category | flops | bytes accessed | tf_op | source)
XLA Modules:
  0.0 113.8 jit_solution(14769284832323344718)
XLA Ops:
  0.0 0.0 copy-start.4
  0.0 1.0 copy-done.4
  1.0 0.0 copy-start.5
  1.0 1.0 copy-done.5
  2.0 0.0 copy-start.7
  2.0 0.9 copy-done.7
  2.9 0.0 copy-start.10
  2.9 0.7 copy-done.10
  3.6 0.0 copy-start.11
  3.7 0.7 copy-done.11
  4.4 0.0 copy-start.12
  4.4 2.7 %project.1 = f32[8,16,576]{2,1,0:T(8,128)} custom-call(bf16[128,640]{1,0:T(8,128)(2,1)S(1)} %copy-done.7, bf16[320,576]{1,0:T(8,128)(2,1)S(1)} %copy-done.4, s32[160,576]{1,0:T(8,128)S(1)} %copy-done.5, bf16[16,640]{1,0:T(8,128)(2,1)S(1)} %bitcast.18, bf16[16,576]{1,0:T(8,128)(2,1)S(1)} %copy-done.11), custom_call_target="tpu_custom_call" | custom-call | tf_op jit(solution)/shard_map/project/pallas_call | solution.py:326
  7.1 6.0 %all-to-all-start = ((f32[8,16,576]{2,1,0:T(8,128)}), f32[8,16,576]{2,1,0:T(8,128)S(1)}, u32[]{:S(2)}, u32[]{:S(2)}) async-start(f32[8,16,576]{2,1,0:T(8,128)} %project.1), calls=%async_computation | async-start | bytes 655360 | tf_op jit(solution)/shard_map/all_to_all | solution.py:343
  13.2 0.2 multiply_cosine_fusion
  13.4 0.1 copy.20.table_ref
  13.6 0.1 pad_add_fusion.where_ref
  13.6 8.9 %all-to-all-done.parts_ref = f32[8,16,576]{2,1,0:T(8,128)S(1)} async-done(((f32[8,16,576]{2,1,0:T(8,128)}), f32[8,16,576]{2,1,0:T(8,128)S(1)}, u32[]{:S(2)}, u32[]{:S(2)}) %all-to-all-start) | async-done | bytes 294944 | tf_op jit(solution)/shard_map/all_to_all | solution.py:343
  22.5 0.0 copy-done.12
  22.5 0.6 finish.1
  23.2 17.7 %all_to_all.20 = bf16[8,16,576]{2,1,0:T(8,128)(2,1)S(1)} all-to-all(bf16[8,16,576]{2,1,0:T(8,128)(2,1)S(1)} %finish.1), channel_id=1, replica_groups={{0,16,32,48,64,80,96,112},{8,24,40,56,72,88,104,120},{128,144,160,176,1..., dimensions={0} | all-to-all | bytes 294912 | tf_op jit(solution)/shard_map/all_to_all | solution.py:363
  40.8 0.0 copy-start.6
  40.8 0.0 copy-start
  40.8 0.1 broadcast_in_dim.2
  41.0 20.8 %all_to_all.21.keys_ref = bf16[8,8,16,576]{3,2,1,0:T(8,128)(2,1)S(1)} all-to-all(bf16[8,8,16,576]{3,2,1,0:T(8,128)(2,1)S(1)} %broadcast_in_dim.2), channel_id=1, replica_groups=mesh['ctx'=32,'head'=8] {'head'}, dimensions={0} | all-to-all | bytes 2359296 | tf_op jit(solution)/shard_map/all_to_all | solution.py:364
  61.8 0.0 collective-permute-start
  61.8 0.0 copy-done.6
  61.8 3.4 %collective-permute-start.1 = (bf16[8,192,128]{2,1,0:T(8,128)(2,1)S(1)}, bf16[8,192,128]{2,1,0:T(8,128)(2,1)S(1)}, u32[]{:S(2)}, u32[]{:S(2)}) collective-permute-start(bf16[8,192,128]{2,1,0:T(8,128)(2,1)S(1)} %bitcast.15), channel_id=1, source_target_pairs={{128,0},{136,8},{144,16},{152,24},{160,32},{168,40},{176,48},{184,... | collective-permute-start | bytes 1179656 | tf_op jit(solution)/shard_map/ppermute | solution.py:324
  65.2 0.0 copy-done
  65.2 0.5 query.2.own_ref
  65.7 8.5 %collective-permute-done.1.queries_ref = bf16[8,192,128]{2,1,0:T(8,128)(2,1)S(1)} collective-permute-done((bf16[8,192,128]{2,1,0:T(8,128)(2,1)S(1)}, bf16[8,192,128]{2,1,0:T(8,128)(2,1)S(1)}, u32[]{:S(2)}, u32[]{:S(2)}) %collective-permute-start.1) | collective-permute-done | bytes 393248 | tf_op jit(solution)/shard_map/ppermute | solution.py:324
  74.2 0.5 query.3.partner_ref
  74.6 0.0 copy-start.3
  74.7 2.5 %first.1 = (f32[8,1024]{1,0:T(8,128)S(1)}, f32[8,1024]{1,0:T(8,128)S(1)}, f32[512,1024]{1,0:T(8,128)S(1)}) custom-call(s32[4]{0:T(128)S(1)} %pad_add_fusion.where_ref, bf16[576,1024]{1,0:T(8,128)(2,1)S(1)} %query.2.own_ref, bf16[576,1024]{1,0:T(8,128)(2,1)S(1)} %query.3.partner_ref, bf16[8,8,16,576]{3,2,1,0:T(8,128)(2,1)S(1)} %all_to_all.21.keys_ref), custom_call_target="tpu_custom_call" | custom-call | flops 2281701376 | bytes 8388608 | tf_op jit(solution)/shard_map/first/pallas_call | solution.py:400
  77.2 0.0 collective-permute-done.keys_ref.others_ref
  77.2 0.0 copy-done.3
  77.2 0.0 copy-start.1
  77.2 0.0 copy-start.2
  77.2 2.6 %second.1 = (bf16[1056,128]{1,0:T(8,128)(2,1)S(1)}, f32[8,1024]{1,0:T(8,128)S(1)}, f32[8,1024]{1,0:T(8,128)S(1)}, f32[512,1024]{1,0:T(8,128)S(1)}) custom-call(s32[4]{0:T(128)S(1)} %pad_add_fusion.where_ref, bf16[576,1024]{1,0:T(8,128)(2,1)S(1)} %query.2.own_ref, ...), custom_call_target="tpu_custom_call", output_to_operand_aliasing={{1}: (5, {}), {2}: (6, {}), {3}: (7, {})} | custom-call | flops 2281701376 | bytes 8388608 | tf_op jit(solution)/shard_map/second/pallas_call | solution.py:409
  79.8 1.3 %collective-permute-start.2 = (bf16[1056,128]{1,0:T(8,128)(2,1)S(1)}, bf16[1056,128]{1,0:T(8,128)(2,1)S(1)}, u32[]{:S(2)}, u32[]{:S(2)}) collective-permute-start(bf16[1056,128]{1,0:T(8,128)(2,1)S(1)} %get-tuple-element.24), channel_id=1, source_target_pairs={{0,128},{8,136},{16,144},{24,152},{32,160},{40,168},{48,176},{56,1... | collective-permute-start | bytes 811016 | tf_op jit(solution)/shard_map/ppermute | solution.py:419
  81.1 0.0 copy-done.1
  81.1 0.0 copy-done.2
  81.2 3.6 %densify.1.dense_ref = bf16[1024,2560]{1,0:T(8,128)(2,1)S(1)} custom-call(bf16[512,2560]{1,0:T(8,128)(2,1)S(1)} %copy-done.1, s32[256,2560]{1,0:T(8,128)S(1)} %copy-done.2), custom_call_target="tpu_custom_call" | custom-call | flops 671088640 | bytes 12582912 | tf_op jit(solution)/shard_map/densify/pallas_call | solution.py:383
  84.8 0.0 copy-start.8
  84.8 0.0 copy-start.9
  84.8 0.6 third.1
  85.4 8.6 %collective-permute-done.2.part_ref = bf16[1056,128]{1,0:T(8,128)(2,1)S(1)} collective-permute-done((bf16[1056,128]{1,0:T(8,128)(2,1)S(1)}, bf16[1056,128]{1,0:T(8,128)(2,1)S(1)}, u32[]{:S(2)}, u32[]{:S(2)}) %collective-permute-start.2) | collective-permute-done | bytes 270368 | tf_op jit(solution)/shard_map/ppermute | solution.py:419
  94.0 0.0 copy-done.8
  94.0 0.0 copy-done.9
  94.0 4.1 %output.1 = bf16[2560,128]{1,0:T(8,128)(2,1)S(1)} custom-call(s32[4]{0:T(128)S(1)} %pad_add_fusion.where_ref, f32[8,1024]{1,0:T(8,128)S(1)} %get-tuple-element.21.m_ref, f32[8,1024]{1,0:T(8,128)S(1)} %get-tuple-element.22.l_ref, f32[512,1024]{1,0:T(8,128)S(1)} %get-tuple-element.23.acc_ref, bf16[1056,128]{1,0:T(8,128)(2,1)S(1)} %collective-permute-done.2.part_ref, ...), custom_call_target="tpu_custom_call" | custom-call | flops 671088640 | bytes 8388608 | tf_op jit(solution)/shard_map/output/pallas_call | solution.py:431
  98.1 15.0 %all_to_all.22.parts_ref = bf16[8,320,128]{2,1,0:T(8,128)(2,1)S(1)} all-to-all(bf16[8,320,128]{2,1,0:T(8,128)(2,1)S(1)} %bitcast.14), channel_id=1, replica_groups=mesh['ctx'=32,'head'=8] {'head'}, dimensions={0} | all-to-all | bytes 1310720 | tf_op jit(solution)/shard_map/all_to_all | solution.py:441
  113.1 0.8 total.1
  (4 shorter events, 0.0 us)
Async XLA Ops:
  0.0 1.0 copy-start.4
  1.0 1.0 copy-start.5
  2.0 0.9 copy-start.7
  2.9 0.7 copy-start.10
  3.6 0.7 copy-start.11
  4.4 18.1 %copy-start.12 = (f32[512]{0:T(512)S(1)}, f32[512]{0:T(512)}, u32[]{:S(2)}) copy-start(f32[512]{0:T(512)} %param.18) | copy-start | bytes 6148
  7.1 15.4 %all-to-all-start = ((f32[8,16,576]{2,1,0:T(8,128)}), f32[8,16,576]{2,1,0:T(8,128)S(1)}, u32[]{:S(2)}, u32[]{:S(2)}) async-start(f32[8,16,576]{2,1,0:T(8,128)} %project.1), calls=%async_computation | async-start | bytes 655360 | tf_op jit(solution)/shard_map/all_to_all | solution.py:343
  40.8 21.0 %copy-start.6 = (bf16[128,8,192]{0,2,1:T(8,128)(2,1)S(1)}, bf16[128,8,192]{0,2,1:T(8,128)(2,1)}, u32[]{:S(2)}) copy-start(bf16[128,8,192]{0,2,1:T(8,128)(2,1)} %param.19) | copy-start | bytes 1179652
  40.8 24.3 %copy-start = (bf16[8,128,512]{2,1,0:T(8,128)(2,1)S(1)}, bf16[8,128,512]{2,1,0:T(8,128)(2,1)}, u32[]{:S(2)}) copy-start(bf16[8,128,512]{2,1,0:T(8,128)(2,1)} %absorb_ref.5) | copy-start | bytes 3145732
  61.8 15.4 %collective-permute-start = (bf16[8,8,16,576]{3,2,1,0:T(8,128)(2,1)S(1)}, bf16[8,8,16,576]{3,2,1,0:T(8,128)(2,1)S(1)}, u32[]{:S(2)}, u32[]{:S(2)}) collective-permute-start(bf16[8,8,16,576]{3,2,1,0:T(8,128)(2,1)S(1)} %all_to_all.21.keys_ref), channel_id=1, source_target_pairs={{0,8},{8,0},{16,24},{24,16},{32,40},{40,32},{48,56},{56,48},{64,72... | collective-permute-start | bytes 3538952 | tf_op jit(solution)/shard_map/ppermute | solution.py:367
  61.8 12.4 %collective-permute-start.1 = (bf16[8,192,128]{2,1,0:T(8,128)(2,1)S(1)}, bf16[8,192,128]{2,1,0:T(8,128)(2,1)S(1)}, u32[]{:S(2)}, u32[]{:S(2)}) collective-permute-start(bf16[8,192,128]{2,1,0:T(8,128)(2,1)S(1)} %bitcast.15), channel_id=1, source_target_pairs={{128,0},{136,8},{144,16},{152,24},{160,32},{168,40},{176,48},{184,... | collective-permute-start | bytes 1179656 | tf_op jit(solution)/shard_map/ppermute | solution.py:324
  74.6 2.6 %copy-start.3 = (bf16[8,512,128]{2,1,0:T(8,128)(2,1)S(1)}, bf16[8,512,128]{2,1,0:T(8,128)(2,1)}, u32[]{:S(2)}) copy-start(bf16[8,512,128]{2,1,0:T(8,128)(2,1)} %absorb_ref.7) | copy-start | bytes 3145732
  77.2 3.9 %copy-start.1 = (bf16[512,2560]{1,0:T(8,128)(2,1)S(1)}, bf16[512,2560]{1,0:T(8,128)(2,1)}, u32[]{:S(2)}) copy-start(bf16[512,2560]{1,0:T(8,128)(2,1)} %values_ref.1) | copy-start | bytes 7864324
  77.2 3.9 %copy-start.2 = (s32[256,2560]{1,0:T(8,128)S(1)}, s32[256,2560]{1,0:T(8,128)}, u32[]{:S(2)}) copy-start(s32[256,2560]{1,0:T(8,128)} %pattern_ref.1) | copy-start | bytes 7864324
  79.8 14.1 %collective-permute-start.2 = (bf16[1056,128]{1,0:T(8,128)(2,1)S(1)}, bf16[1056,128]{1,0:T(8,128)(2,1)S(1)}, u32[]{:S(2)}, u32[]{:S(2)}) collective-permute-start(bf16[1056,128]{1,0:T(8,128)(2,1)S(1)} %get-tuple-element.24), channel_id=1, source_target_pairs={{0,128},{8,136},{16,144},{24,152},{32,160},{40,168},{48,176},{56,1... | collective-permute-start | bytes 811016 | tf_op jit(solution)/shard_map/ppermute | solution.py:419
  84.8 9.2 %copy-start.8 = (bf16[16,2560]{1,0:T(8,128)(2,1)S(1)}, bf16[16,2560]{1,0:T(8,128)(2,1)}, u32[]{:S(2)}) copy-start(bf16[16,2560]{1,0:T(8,128)(2,1)} %up_ref.1) | copy-start | bytes 245764
  84.8 9.1 %copy-start.9 = (bf16[1024,16]{0,1:T(8,128)(2,1)S(1)}, bf16[1024,16]{0,1:T(8,128)(2,1)}, u32[]{:S(2)}) copy-start(bf16[1024,16]{0,1:T(8,128)(2,1)} %param.24) | copy-start | bytes 98308

commit v3 on v2

--- a/solution.py
+++ b/solution.py
@@ -22,8 +22,11 @@
 VDIM = 128
 CTX = 32
 CHIPS = 8
-GROUP = 4
-KEYS = GROUP * ROWS
+SLICES = 4
+PACKED = ROWS * WIDTH // 128
+KEYS = SLICES * ROWS
+WIDE = 640
+UNSEEN = -1e30
 COLS = 640
 LOG2E = 1.4426950408889634
 
@@ -56,21 +59,22 @@
 
 def densify(values_ref, pattern_ref, dense_ref):
     total = values_ref.shape[0]
+    zero = jnp.zeros((), BF16)
     begin = 0
     while begin < total:
         count = min(256, total - begin)
         half = count // 2
-        pair = dot(unpair(count), values_ref[begin : begin + count, :])
+        pair = dot(unpair(count), values_ref[begin : begin + count, :]).astype(BF16)
         v0, v1 = pair[:half], pair[half:]
-        p = pattern_ref[begin // 2 : begin // 2 + half, :]
+        p = pattern_ref[begin // 2 : begin // 2 + half, :].astype(F32).astype(BF16)
+        is_0, is_1, is_2, is_3, is_4, is_5 = (p == jnp.asarray(k, BF16) for k in range(6))
         slots = (
-            jnp.where(p < 3, v0, 0.0),
-            jnp.where(p == 0, v1, jnp.where((p == 3) | (p == 4), v0, 0.0)),
-            jnp.where((p == 1) | (p == 3), v1, jnp.where(p == 5, v0, 0.0)),
-            jnp.where((p == 2) | (p >= 4), v1, 0.0),
+            jnp.where(p < jnp.asarray(3, BF16), v0, zero),
+            jnp.where(is_0, v1, jnp.where(is_3 | is_4, v0, zero)),
+            jnp.where(is_1 | is_3, v1, jnp.where(is_5, v0, zero)),
+            jnp.where(is_2 | is_4 | is_5, v1, zero),
         )
         for k, slot in enumerate(slots):
-            slot = slot.astype(BF16)
             for b in range(half // 32):
                 row = 2 * begin + 128 * b + 32 * k
                 dense_ref[row : row + 32, :] = slot[32 * b : 32 * b + 32]
@@ -113,10 +117,12 @@
     up = up_ref[...]
     for term in thirds(dot_last(tokens, down_ref[...])):
         raw += dot(term, up)
-    raw_ref[...] = raw.reshape(raw_ref.shape)
-
-
-def query_kernel(queries_ref, absorb_ref, table_ref, out_ref):
+    raw_ref[:, :, :WIDTH] = raw.reshape(HEADS, PIECE, WIDTH)
+    raw_ref[:, :, WIDTH:] = jnp.zeros((HEADS, PIECE, WIDE - WIDTH), F32)
+
+
+def query_kernel(queries_ref, absorb_ref, table_ref, out_ref, token_ref):
+    token_ref[...] = jnp.zeros(token_ref.shape, F32)
     half = ROPE // 2
     cos, sin = table_ref[:ROPE, :], table_ref[ROPE:, :]
     for h in range(HEADS):
@@ -127,7 +133,8 @@
         out_ref[LAT:, columns] = (x * cos + swapped * sin).astype(BF16)
 
 
-def finish_kernel(where_ref, parts_ref, gain_ref, table_ref, out_ref):
+def finish_kernel(where_ref, parts_ref, gain_ref, table_ref, *refs):
+    out_ref = refs[-1]
     raw = parts_ref[0]
     for h in range(1, HEADS):
         raw += parts_ref[h]
@@ -135,13 +142,38 @@
     meansq = jnp.mean(latent * latent, axis=-1, keepdims=True)
     normed = (latent * lax.rsqrt(meansq + 1e-06) * gain_ref[...]).astype(BF16)
     table = table_ref[pl.ds(pl.multiple_of(where_ref[3] * PIECE, PIECE), PIECE), :]
-    x = raw[:, LAT:]
+    x = raw[:, LAT:WIDTH]
     half = ROPE // 2
     swapped = jnp.concatenate([x[:, half:], x[:, :half]], axis=1)
     turned = (x * table[:, :ROPE] + swapped * table[:, ROPE:]).astype(BF16)
     for c in range(CHIPS):
         out_ref[c, :, :LAT] = normed
-        out_ref[c, :, LAT:] = turned
+        out_ref[c, :, LAT:WIDTH] = turned
+        out_ref[c, :, WIDTH:] = jnp.zeros((PIECE, WIDE - WIDTH), BF16)
+
+
+def pack_kernel(column_ref, *refs):
+    out_ref = refs[-1]
+    keys = column_ref[...].reshape(ROWS, WIDE)
+    rope = keys[:, LAT:WIDTH]
+    rope = jnp.concatenate([rope[: ROWS // 2], rope[ROWS // 2 :]], axis=1)
+    for k in range(HEADS):
+        for c in range(LAT // 128):
+            out_ref[k, c * ROWS : (c + 1) * ROWS, :] = keys[:, c * 128 : (c + 1) * 128]
+        out_ref[k, LAT // 128 * ROWS :, :] = rope
+
+
+def unpack(keys_ref, part):
+    latents, ropes = [], []
+    for k in range(part * SLICES, (part + 1) * SLICES):
+        latents.append(
+            jnp.concatenate(
+                [keys_ref[k, c * ROWS : (c + 1) * ROWS, :] for c in range(LAT // 128)], axis=1
+            )
+        )
+        rope = keys_ref[k, LAT // 128 * ROWS :, :]
+        ropes += [rope[:, :ROPE], rope[:, ROPE:]]
+    return jnp.concatenate(latents, axis=0), jnp.concatenate(ropes, axis=0)
 
 
 class Rows:
@@ -151,21 +183,20 @@
         self.scale = scale
 
     def clear(self):
-        self.m_ref[...] = jnp.full(self.m_ref.shape, -jnp.inf, F32)
+        self.m_ref[...] = jnp.full(self.m_ref.shape, UNSEEN, F32)
         self.l_ref[...] = jnp.zeros(self.l_ref.shape, F32)
         self.acc_ref[...] = jnp.zeros(self.acc_ref.shape, F32)
 
-    def chunk(self, keys_ref, j, key_core=None):
-        keys = jnp.concatenate(
-            [keys_ref[:, GROUP * j + b].reshape(ROWS, WIDTH) for b in range(GROUP)], axis=0
-        )
-        scores = dot(keys, self.q_ref[...]) * self.scale
+    def chunk(self, keys_ref, part, key_core=None):
+        latent, rope = unpack(keys_ref, part)
+        scores = dot(jnp.concatenate([latent, rope], axis=1), self.q_ref[...]) * self.scale
         if key_core is not None:
             query = lax.broadcasted_iota(jnp.int32, (1, ALL), 1) % ROWS
             key = lax.broadcasted_iota(jnp.int32, (KEYS, 1), 0)
             ahead = (2 * self.chip + self.core) * ROWS + query
-            place = (2 * (GROUP * j + key // ROWS) + key_core) * ROWS + key % ROWS
-            scores = jnp.where(place <= ahead, scores, -jnp.inf)
+            place = (2 * (key % ROWS // PIECE) + key_core) * ROWS
+            place += (part * SLICES + key // ROWS) * PIECE + key % PIECE
+            scores = jnp.where(place <= ahead, scores, UNSEEN)
         old = self.m_ref[...]
         new = jnp.maximum(old, jnp.max(scores, axis=0, keepdims=True))
         factor = jnp.exp2(old - new)
@@ -174,105 +205,86 @@
         self.l_ref[...] = self.l_ref[...] * factor + jnp.sum(
             weights.reshape(KEYS // 8, 8, ALL), axis=0
         )
-        self.acc_ref[...] = self.acc_ref[...] * factor[:1] + dot(
-            keys[:, :LAT].T, weights.astype(BF16)
-        )
-
-    def whole(self, keys_ref, count):
-        @pl.loop(0, count)
-        def _(j):
-            self.chunk(keys_ref, j)
-
-    def causal(self, keys_ref, key_core):
-        self.whole(keys_ref, self.chip // GROUP)
-        self.chunk(keys_ref, self.chip // GROUP, key_core)
+        self.acc_ref[...] = self.acc_ref[...] * factor[:1] + dot(latent.T, weights.astype(BF16))
+
+    def run(self, keys_ref, key_core=None):
+        for part in range(HEADS // SLICES):
+            self.chunk(keys_ref, part, key_core)
 
     def head_out(self, h, absorb_ref):
         columns = slice(h * ROWS, (h + 1) * ROWS)
         total = jnp.sum(self.l_ref[:, columns], axis=0, keepdims=True)
-        attended = (self.acc_ref[:, columns] / total).astype(BF16)
+        attended = (self.acc_ref[:, columns] * (1.0 / total)).astype(BF16)
         return dot_first(absorb_ref[h], attended), self.m_ref[:1, columns] + jnp.log2(total)
 
 
-def first_kernel(scale, where_ref, own_ref, partner_ref, keys_ref, m_ref, l_ref, acc_ref):
-    upper = where_ref[0]
-    for q_ref, mine in ((own_ref, upper == 1), (partner_ref, upper == 0)):
-        rows = Rows(where_ref, q_ref, m_ref, l_ref, acc_ref, scale)
-
-        @pl.when(mine)
-        def _():
-            rows.clear()
-            if q_ref is own_ref:
-                rows.causal(keys_ref, where_ref[2])
-            else:
-                rows.whole(keys_ref, CHIPS // GROUP)
-
-
-def second_kernel(
-    scale, where_ref, own_ref, partner_ref, keys_ref, absorb_ref, m_in, l_in, acc_in,
-    part_ref, m_ref, l_ref, acc_ref,
-):
-    del m_in, l_in, acc_in
-    upper = where_ref[0]
-
-    @pl.when(upper == 1)
+def first_kernel(scale, where_ref, own_ref, partner_ref, keys_ref, *state):
+    @pl.when(where_ref[0] == 0)
     def _():
-        rows = Rows(where_ref, own_ref, m_ref, l_ref, acc_ref, scale)
-        rows.causal(keys_ref, 1 - where_ref[2])
-
-    @pl.when(upper == 0)
+        rows = Rows(where_ref, partner_ref, *state, scale)
+        rows.clear()
+        rows.run(keys_ref)
+
+    @pl.when(where_ref[0] == 1)
     def _():
-        rows = Rows(where_ref, partner_ref, m_ref, l_ref, acc_ref, scale)
-        rows.whole(keys_ref, CHIPS // GROUP)
-        logs = []
-        for h in range(HEADS):
-            out, log = rows.head_out(h, absorb_ref)
+        rows = Rows(where_ref, own_ref, *state, scale)
+        rows.clear()
+        rows.run(keys_ref, where_ref[2])
+
+
+def second_kernel(scale, where_ref, own_ref, partner_ref, keys_ref, absorb_ref, *refs):
+    part_ref, *state = refs[3:]
+
+    @pl.when(where_ref[0] == 0)
+    def _():
+        rows = Rows(where_ref, partner_ref, *state, scale)
+        rows.run(keys_ref)
+        outs = [rows.head_out(h, absorb_ref) for h in range(HEADS)]
+        for h, (out, _) in enumerate(outs):
             part_ref[h * VDIM : (h + 1) * VDIM, :] = out.astype(BF16)
-            logs.append(log)
-        logs = jnp.concatenate(logs, axis=0)
+        logs = jnp.concatenate([log for _, log in outs], axis=0)
         terms = [t.astype(F32) for t in thirds(logs)] + [jnp.zeros_like(logs)]
         part_ref[HEADS * VDIM :, :] = jnp.concatenate(terms, axis=0).astype(BF16)
 
-
-def third_kernel(
-    scale, where_ref, own_ref, keys_ref, others_ref, m_in, l_in, acc_in, m_ref, l_ref, acc_ref
-):
-    del m_in, l_in, acc_in
-
+    @pl.when(where_ref[0] == 1)
+    def _():
+        Rows(where_ref, own_ref, *state, scale).run(keys_ref, 1 - where_ref[2])
+
+
+def third_kernel(scale, where_ref, own_ref, keys_ref, others_ref, *refs):
     @pl.when(where_ref[0] == 0)
     def _():
-        rows = Rows(where_ref, own_ref, m_ref, l_ref, acc_ref, scale)
+        rows = Rows(where_ref, own_ref, *refs[3:], scale)
         rows.clear()
-        rows.causal(keys_ref, where_ref[2])
-        rows.causal(others_ref, 1 - where_ref[2])
+        rows.run(keys_ref, where_ref[2])
+        rows.run(others_ref, 1 - where_ref[2])
 
 
 def output_kernel(
     where_ref, m_ref, l_ref, acc_ref, part_ref, absorb_ref, down_ref, up_ref, dense_ref,
-    out_ref, flat_ref,
+    out_ref,
 ):
     upper = where_ref[0]
     rows = Rows(where_ref, None, m_ref, l_ref, acc_ref, None)
     logs = part_ref[HEADS * VDIM :, :].astype(F32)
     logs = logs[:HEADS] + logs[HEADS : 2 * HEADS] + logs[2 * HEADS : 3 * HEADS]
-    order = by_slot()
-    lowrank = jnp.zeros((down_ref.shape[0], ROWS), F32)
-    for h in range(HEADS):
-        span = slice(h * VDIM, (h + 1) * VDIM)
-        mine, log = rows.head_out(h, absorb_ref)
+    mine = [rows.head_out(h, absorb_ref) for h in range(HEADS)]
+    outs = []
+    for h, (own, log) in enumerate(mine):
         other_log = jnp.where(upper == 1, logs[h : h + 1], -jnp.inf)
         top = jnp.maximum(log, other_log)
         weight, other_weight = jnp.exp2(log - top), jnp.exp2(other_log - top)
-        other = part_ref[span, :].astype(F32)
-        out = (mine * weight + other * other_weight) / (weight + other_weight)
-        out = out.astype(BF16)
-        lowrank += dot(down_ref[:, span], out)
-        flat_ref[span, :] = dot_first(order, out).astype(BF16)
-    low = thirds(lowrank)
+        share = 1.0 / (weight + other_weight)
+        other = part_ref[h * VDIM : (h + 1) * VDIM, :].astype(F32)
+        outs.append((own * (weight * share) + other * (other_weight * share)).astype(BF16))
+    order = by_slot()
+    flat = jnp.concatenate([dot_first(out, order).astype(BF16) for out in outs], axis=1)
+    lowrank = dot(down_ref[...], jnp.concatenate(outs, axis=0))
+    low = jnp.concatenate(thirds(lowrank.T), axis=1)
     for c in range(0, out_ref.shape[0], COLS):
-        terms = dot_first(flat_ref[...], dense_ref[:, c : c + COLS])
-        for term in low:
-            terms += dot_first(term, up_ref[:, c : c + COLS])
+        up = up_ref[:, c : c + COLS]
+        terms = dot(flat, dense_ref[:, c : c + COLS])
+        terms += dot(low, jnp.concatenate([up] * 3, axis=0))
         out_ref[c : c + COLS, :] = terms.T.astype(BF16)
 
 
@@ -325,7 +337,7 @@
 
     raw = pl.pallas_call(
         project_kernel,
-        out_shape=shape(HEADS, PIECE, WIDTH),
+        out_shape=shape(HEADS, PIECE, WIDE),
         in_specs=[ANY] * 5,
         out_specs=VMEM,
         scratch_shapes=[
@@ -337,7 +349,7 @@
             pltpu.VMEM((tokens.shape[1], WIDTH), BF16),
             pltpu.SemaphoreType.DMA((5,)),
         ],
-        compiler_params=params(24),
+        compiler_params=params(56),
         name="project",
     )(tokens, kv_values, kv_pattern, kv_down.T, kv_up)
     parts = lax.all_to_all(raw, "head", 0, 0, tiled=True)
@@ -346,14 +358,43 @@
     table = tables(positions)
     partner_table = tables(positions + 2 * CHIPS * ROWS)
 
+    def query(x, t):
+        return pl.pallas_call(
+            query_kernel,
+            out_shape=(shape(WIDTH, ALL, dtype=BF16), shape(8, 128)),
+            in_specs=[VMEM] * 3,
+            out_specs=(VMEM, VMEM),
+            compiler_params=params(16),
+            cost_estimate=cost(2 * ALL * NOPE * LAT, 4 * MIB),
+            name="query",
+        )(x, absorb_k, t.T)
+
+    own_query, own_token = query(columns, table)
+    partner_query, partner_token = query(partner, partner_table)
+
+    step = out_cols // 2
+    dense = pl.pallas_call(
+        densify,
+        grid=(out_cols // step,),
+        out_shape=shape(2 * o_values.shape[0], out_cols, dtype=BF16),
+        in_specs=[
+            pl.BlockSpec((o_values.shape[0], step), lambda i: (0, i)),
+            pl.BlockSpec((o_pattern.shape[0], step), lambda i: (0, i)),
+        ],
+        out_specs=pl.BlockSpec((2 * o_values.shape[0], step), lambda i: (0, i)),
+        compiler_params=params(24),
+        cost_estimate=cost(2 * 256 * o_values.size, 12 * MIB),
+        name="densify",
+    )(o_values, o_pattern)
+
     piece = pl.pallas_call(
         finish_kernel,
-        out_shape=shape(CHIPS, PIECE, WIDTH, dtype=BF16),
-        in_specs=[SMEM, VMEM, VMEM, VMEM],
+        out_shape=shape(CHIPS, PIECE, WIDE, dtype=BF16),
+        in_specs=[SMEM] + [VMEM] * 4,
         out_specs=VMEM,
         compiler_params=params(16),
         name="finish",
-    )(where, parts, kv_gain.reshape(1, LAT), table)
+    )(where, parts, kv_gain.reshape(1, LAT), table, own_token)
 
     along_z = [
         [(u * CHIPS + chip) * 2 + core for chip in range(CHIPS)]
@@ -361,38 +402,16 @@
         for core in range(2)
     ]
     column = lax.all_to_all(piece, "ctx", 0, 0, tiled=True, axis_index_groups=along_z)
-    keys = lax.all_to_all(
-        jnp.broadcast_to(column[None], (HEADS,) + column.shape), "head", 0, 0, tiled=True
-    )
+    packed = pl.pallas_call(
+        pack_kernel,
+        out_shape=shape(HEADS, PACKED, 128, dtype=BF16),
+        in_specs=[VMEM] * 2,
+        out_specs=VMEM,
+        compiler_params=params(16),
+        name="pack",
+    )(column, partner_token)
+    keys = lax.all_to_all(packed, "head", 0, 0, tiled=True)
     others = lax.ppermute(keys, "ctx", [(i, i ^ 1) for i in range(CTX)])
-
-    def query(x, t):
-        return pl.pallas_call(
-            query_kernel,
-            out_shape=shape(WIDTH, ALL, dtype=BF16),
-            in_specs=[VMEM] * 3,
-            out_specs=VMEM,
-            compiler_params=params(16),
-            cost_estimate=cost(2 * ALL * NOPE * LAT, 4 * MIB),
-            name="query",
-        )(x, absorb_k, t.T)
-
-    own_query = query(columns, table)
-    partner_query = query(partner, partner_table)
-
-    dense = pl.pallas_call(
-        densify,
-        grid=(out_cols // COLS,),
-        out_shape=shape(2 * o_values.shape[0], out_cols, dtype=BF16),
-        in_specs=[
-            pl.BlockSpec((o_values.shape[0], COLS), lambda i: (0, i)),
-            pl.BlockSpec((o_pattern.shape[0], COLS), lambda i: (0, i)),
-        ],
-        out_specs=pl.BlockSpec((2 * o_values.shape[0], COLS), lambda i: (0, i)),
-        compiler_params=params(24),
-        cost_estimate=cost(2 * 256 * o_values.size, 12 * MIB),
-        name="densify",
-    )(o_values, o_pattern)
 
     state = (shape(8, ALL), shape(8, ALL), shape(LAT, ALL))
     scores = ALL * CHIPS * ROWS
@@ -417,7 +436,7 @@
         name="second",
     )(where, own_query, partner_query, others, absorb_v, *first)
     received = lax.ppermute(part, "ctx", [(i, i + 2 * CHIPS) for i in range(2 * CHIPS)])
-    third = pl.pallas_call(
+    own = pl.pallas_call(
         functools.partial(third_kernel, scale),
         out_shape=state,
         in_specs=[SMEM] + [VMEM] * 6,
@@ -433,11 +452,10 @@
         out_shape=shape(out_cols, ROWS, dtype=BF16),
         in_specs=[SMEM] + [VMEM] * 8,
         out_specs=VMEM,
-        scratch_shapes=[pltpu.VMEM((HEADS * VDIM, ROWS), BF16)],
         compiler_params=params(32),
         cost_estimate=cost(2 * ROWS * HEADS * VDIM * out_cols, 8 * MIB),
         name="output",
-    )(where, *third, received, absorb_v, o_down.T, o_up, dense)
+    )(where, *own, received, absorb_v, o_down.T, o_up, dense)
     shares = lax.all_to_all(
         terms.reshape(HEADS, out_cols // HEADS, ROWS), "head", 0, 0, tiled=True
     )

time: 115 us -> 99.5 us (0.87)
  the two profiles are of different devices: /device:TPU:2 before, /device:TPU:1 now
where the time goes in v3:
time: 99.5 us; the launch traced here: 99.1 us
  blocking collectives  33.8 us (34%)
  Pallas kernels  27.5 us (28%)
  starting transfers between devices  23.6 us (24%)
  waiting for transfers between devices  12.4 us (12%)
  local copies, waits for them, and re-layouts  1.15 us (1%)
    all_to_all x1, blocking collectives, local(): keys = lax.all_to_all(packed, 'head', 0, 0, tiled=True)  18.8 us
    all_to_all x1, blocking collectives, local(): lax.all_to_all(terms.reshape(HEADS, out_cols // HEADS, ROWS), 'head', 0,...  15 us
    all_to_all x1, starting transfers between devices, local(): lax.all_to_all(piece, 'ctx', 0, 0, tiled=True, axis_index_groups=along_z)  8.18 us
    pallas_call x1, Pallas kernels, local(): pl.pallas_call(functools.partial(third_kernel, scale), out_shape=state, i...  7.7 us
    all_to_all x1, starting transfers between devices, local(): parts = lax.all_to_all(raw, 'head', 0, 0, tiled=True)  7.5 us
    all_to_all x1, waiting for transfers between devices, local(): lax.all_to_all(piece, 'ctx', 0, 0, tiled=True, axis_index_groups=along_z)  6.84 us
    all_to_all x1, waiting for transfers between devices, local(): parts = lax.all_to_all(raw, 'head', 0, 0, tiled=True)  5.55 us
    pallas_call x1, Pallas kernels, local(): pl.pallas_call(functools.partial(second_kernel, scale), out_shape=(shape(...  4.55 us
  transfers between devices with their start and end apart: 5, of which 2 were waited for; matrix products, arithmetic and copies ran while one was open for 0% of the time, Pallas kernels for 16%

profile of v3, /device:TPU:1, one launch (start us, length us, event | category | flops | bytes accessed | tf_op | source)
XLA Modules:
  0.0 99.1 jit_solution(10589141863923365570)
XLA Ops:
  0.0 0.0 copy-start.4
  0.0 0.0 copy-start
  0.0 0.0 copy-start.7
  0.0 3.0 %project.1 = f32[8,16,640]{2,1,0:T(8,128)} custom-call(bf16[128,640]{1,0:T(8,128)(2,1)} %tokens_hbm.1, bf16[320,576]{1,0:T(8,128)(2,1)} %values_hbm.1, s32[160,576]{1,0:T(8,128)} %pattern_hbm.1, bf16[16,640]{1,0:T(8,128)(2,1)} %bitcast.19, bf16[16,576]{1,0:T(8,128)(2,1)} %up_hbm.1), custom_call_target="tpu_custom_call" | custom-call | tf_op jit(solution)/shard_map/project/pallas_call | solution.py:338
  3.0 7.5 %all-to-all-start = ((f32[8,16,640]{2,1,0:T(8,128)}), f32[8,16,640]{2,1,0:T(8,128)S(1)}, u32[]{:S(2)}, u32[]{:S(2)}) async-start(f32[8,16,640]{2,1,0:T(8,128)} %project.1), calls=%async_computation | async-start | bytes 655360 | tf_op jit(solution)/shard_map/all_to_all | solution.py:355
  10.5 1.3 %collective-permute-start = (bf16[8,192,128]{2,1,0:T(8,128)(2,1)}, bf16[8,192,128]{2,1,0:T(8,128)(2,1)S(1)}, u32[]{:S(2)}, u32[]{:S(2)}) collective-permute-start(bf16[8,192,128]{2,1,0:T(8,128)(2,1)} %bitcast.15), channel_id=1, source_target_pairs={{128,0},{136,8},{144,16},{152,24},{160,32},{168,40},{176,48},{184,... | collective-permute-start | bytes 1179656 | tf_op jit(solution)/shard_map/ppermute | solution.py:336
  11.9 0.2 multiply_cosine_fusion
  12.1 0.1 copy.20.table_ref
  12.2 0.0 copy-done.4
  12.3 0.0 copy-done
  12.3 0.5 query.2
  12.8 0.1 pad_add_fusion.where_ref
  12.8 5.6 %all-to-all-done.parts_ref = f32[8,16,640]{2,1,0:T(8,128)S(1)} async-done(((f32[8,16,640]{2,1,0:T(8,128)}), f32[8,16,640]{2,1,0:T(8,128)S(1)}, u32[]{:S(2)}, u32[]{:S(2)}) %all-to-all-start) | async-done | bytes 327712 | tf_op jit(solution)/shard_map/all_to_all | solution.py:355
  18.4 0.0 copy-done.7
  18.4 1.3 %finish.1 = bf16[8,16,640]{2,1,0:T(8,128)(2,1)} custom-call(s32[4]{0:T(128)S(1)} %pad_add_fusion.where_ref, f32[8,16,640]{2,1,0:T(8,128)S(1)} %all-to-all-done.parts_ref, f32[1,512]{1,0:T(1,128)S(1)} %bitcast.18, f32[128,128]{1,0:T(8,128)S(1)} %copy.20.table_ref, f32[8,128]{1,0:T(8,128)S(1)} %get-tuple-element.20.refs_0_), custom_call_target="tpu_custom_call" | custom-call | tf_op jit(solution)/shard_map/finish/pallas_call | solution.py:390
  19.7 8.2 %all-to-all-start.1 = ((bf16[8,16,640]{2,1,0:T(8,128)(2,1)}), bf16[8,16,640]{2,1,0:T(8,128)(2,1)S(1)}, u32[]{:S(2)}, u32[]{:S(2)}) async-start(bf16[8,16,640]{2,1,0:T(8,128)(2,1)} %finish.1), calls=%async_computation.1 | async-start | bytes 327680 | tf_op jit(solution)/shard_map/all_to_all | solution.py:404
  27.9 0.0 collective-permute-done.queries_ref
  27.9 0.5 query.3
  28.4 0.0 copy-start.8
  28.4 1.0 %copy-done.8 = bf16[576,1024]{1,0:T(8,128)(2,1)} copy-done((bf16[576,1024]{1,0:T(8,128)(2,1)}, bf16[576,1024]{1,0:T(8,128)(2,1)S(1)}, u32[]{:S(2)}) %copy-start.8) | copy-done | bytes 1179672
  29.4 6.8 %all-to-all-done.1.column_ref = bf16[8,16,640]{2,1,0:T(8,128)(2,1)S(1)} async-done(((bf16[8,16,640]{2,1,0:T(8,128)(2,1)}), bf16[8,16,640]{2,1,0:T(8,128)(2,1)S(1)}, u32[]{:S(2)}, u32[]{:S(2)}) %all-to-all-start.1) | async-done | bytes 163872 | tf_op jit(solution)/shard_map/all_to_all | solution.py:404
  36.3 0.0 copy-start.9
  36.3 0.2 pack.1
  36.4 18.8 %all_to_all.20.keys_ref = bf16[8,576,128]{2,1,0:T(8,128)(2,1)S(1)} all-to-all(bf16[8,576,128]{2,1,0:T(8,128)(2,1)S(1)} %pack.1), channel_id=1, replica_groups=mesh['ctx'=32,'head'=8] {'head'}, dimensions={0} | all-to-all | bytes 2359296 | tf_op jit(solution)/shard_map/all_to_all | solution.py:413
  55.3 4.5 %collective-permute-start.1 = (bf16[8,576,128]{2,1,0:T(8,128)(2,1)S(1)}, bf16[8,576,128]{2,1,0:T(8,128)(2,1)S(1)}, u32[]{:S(2)}, u32[]{:S(2)}) collective-permute-start(bf16[8,576,128]{2,1,0:T(8,128)(2,1)S(1)} %all_to_all.20.keys_ref), channel_id=1, source_target_pairs={{0,8},{8,0},{16,24},{24,16},{32,40},{40,32},{48,56},{56,48},{64,72... | collective-permute-start | bytes 3538952 | tf_op jit(solution)/shard_map/ppermute | solution.py:414
  59.7 0.0 copy-done.9
  59.7 0.0 copy-start.3
  59.7 3.9 %first.1 = (f32[8,1024]{1,0:T(8,128)S(1)}, f32[8,1024]{1,0:T(8,128)S(1)}, f32[512,1024]{1,0:T(8,128)S(1)}) custom-call(s32[4]{0:T(128)S(1)} %pad_add_fusion.where_ref, bf16[576,1024]{1,0:T(8,128)(2,1)S(1)} %get-tuple-element.19.own_ref, bf16[576,1024]{1,0:T(8,128)(2,1)S(1)} %copy-done.9, bf16[8,576,128]{2,1,0:T(8,128)(2,1)S(1)} %all_to_all.20.keys_ref), custom_call_target="tpu_custom_call" | custom-call | flops 2281701376 | bytes 8388608 | tf_op jit(solution)/shard_map/first/pallas_call | solution.py:419
  63.7 0.0 collective-permute-done.1.keys_ref.others_ref
  63.7 0.0 copy-done.3
  63.7 0.0 copy-start.1
  63.7 0.0 copy-start.2
  63.7 4.5 %second.1 = (bf16[1056,128]{1,0:T(8,128)(2,1)S(1)}, f32[8,1024]{1,0:T(8,128)S(1)}, f32[8,1024]{1,0:T(8,128)S(1)}, f32[512,1024]{1,0:T(8,128)S(1)}) custom-call(s32[4]{0:T(128)S(1)} %pad_add_fusion.where_ref, bf16[576,1024]{1,0:T(8,128)(2,1)S(1)} %get-tuple-element.19.own_ref, ...), custom_call_target="tpu_custom_call", output_to_operand_aliasing={{1}: (5, {}), {2}: (6, {}), {3}: (7, {})} | custom-call | flops 2281701376 | bytes 8388608 | tf_op jit(solution)/shard_map/second/pallas_call | solution.py:428
  68.3 2.2 %collective-permute-start.2 = (bf16[1056,128]{1,0:T(8,128)(2,1)S(1)}, bf16[1056,128]{1,0:T(8,128)(2,1)S(1)}, u32[]{:S(2)}, u32[]{:S(2)}) collective-permute-start(bf16[1056,128]{1,0:T(8,128)(2,1)S(1)} %get-tuple-element.32), channel_id=1, source_target_pairs={{0,128},{8,136},{16,144},{24,152},{32,160},{40,168},{48,176},{56,1... | collective-permute-start | bytes 811016 | tf_op jit(solution)/shard_map/ppermute | solution.py:438
  70.4 0.0 copy-done.1
  70.5 0.0 copy-done.2
  70.5 2.4 %densify.1.dense_ref = bf16[1024,2560]{1,0:T(8,128)(2,1)S(1)} custom-call(bf16[512,2560]{1,0:T(8,128)(2,1)S(1)} %copy-done.1, s32[256,2560]{1,0:T(8,128)S(1)} %copy-done.2), custom_call_target="tpu_custom_call" | custom-call | flops 671088640 | bytes 12582912 | tf_op jit(solution)/shard_map/densify/pallas_call | solution.py:376
  72.9 0.0 copy-start.5
  72.9 0.0 copy-start.6
  72.9 7.7 %third.1 = (f32[8,1024]{1,0:T(8,128)S(1)}, f32[8,1024]{1,0:T(8,128)S(1)}, f32[512,1024]{1,0:T(8,128)S(1)}) custom-call(s32[4]{0:T(128)S(1)} %pad_add_fusion.where_ref, bf16[576,1024]{1,0:T(8,128)(2,1)S(1)} %get-tuple-element.19.own_ref, bf16[8,576,128]{2,1,0:T(8,128)(2,1)S(1)} %all_to_all.20.keys_ref, ...), custom_call_target="tpu_custom_call", output_to_operand_aliasing={{0}: (4, {}), {1}: (5, {}), {2}: (6, {})} | custom-call | flops 2281701376 | bytes 8388608 | tf_op jit(solution)/shard_map/third/pallas_call | solution.py:439
  80.6 0.0 collective-permute-done.2.part_ref
  80.6 0.0 copy-done.5
  80.6 0.0 copy-done.6
  80.6 2.7 %output.1 = bf16[2560,128]{1,0:T(8,128)(2,1)S(1)} custom-call(s32[4]{0:T(128)S(1)} %pad_add_fusion.where_ref, f32[8,1024]{1,0:T(8,128)S(1)} %get-tuple-element.29.m_ref, f32[8,1024]{1,0:T(8,128)S(1)} %get-tuple-element.30.l_ref, f32[512,1024]{1,0:T(8,128)S(1)} %get-tuple-element.31.acc_ref, bf16[1056,128]{1,0:T(8,128)(2,1)S(1)} %collective-permute-done.2.part_ref, ...), custom_call_target="tpu_custom_call" | custom-call | flops 671088640 | bytes 8388608 | tf_op jit(solution)/shard_map/output/pallas_call | solution.py:450
  83.4 15.0 %all_to_all.21.parts_ref = bf16[8,320,128]{2,1,0:T(8,128)(2,1)S(1)} all-to-all(bf16[8,320,128]{2,1,0:T(8,128)(2,1)S(1)} %bitcast.14), channel_id=1, replica_groups=mesh['ctx'=32,'head'=8] {'head'}, dimensions={0} | all-to-all | bytes 1310720 | tf_op jit(solution)/shard_map/all_to_all | solution.py:459
  98.4 0.8 total.1
  (4 shorter events, 0.0 us)
Async XLA Ops:
  0.0 12.2 %copy-start.4 = (bf16[128,8,192]{0,2,1:T(8,128)(2,1)S(1)}, bf16[128,8,192]{0,2,1:T(8,128)(2,1)}, u32[]{:S(2)}) copy-start(bf16[128,8,192]{0,2,1:T(8,128)(2,1)} %param.19) | copy-start | bytes 1179652
  0.0 12.3 %copy-start = (bf16[8,128,512]{2,1,0:T(8,128)(2,1)S(1)}, bf16[8,128,512]{2,1,0:T(8,128)(2,1)}, u32[]{:S(2)}) copy-start(bf16[8,128,512]{2,1,0:T(8,128)(2,1)} %absorb_ref.5) | copy-start | bytes 3145732
  0.0 18.4 %copy-start.7 = (f32[512]{0:T(512)S(1)}, f32[512]{0:T(512)}, u32[]{:S(2)}) copy-start(f32[512]{0:T(512)} %param.18) | copy-start | bytes 6148
  3.0 15.3 %all-to-all-start = ((f32[8,16,640]{2,1,0:T(8,128)}), f32[8,16,640]{2,1,0:T(8,128)S(1)}, u32[]{:S(2)}, u32[]{:S(2)}) async-start(f32[8,16,640]{2,1,0:T(8,128)} %project.1), calls=%async_computation | async-start | bytes 655360 | tf_op jit(solution)/shard_map/all_to_all | solution.py:355
  10.5 17.4 %collective-permute-start = (bf16[8,192,128]{2,1,0:T(8,128)(2,1)}, bf16[8,192,128]{2,1,0:T(8,128)(2,1)S(1)}, u32[]{:S(2)}, u32[]{:S(2)}) collective-permute-start(bf16[8,192,128]{2,1,0:T(8,128)(2,1)} %bitcast.15), channel_id=1, source_target_pairs={{128,0},{136,8},{144,16},{152,24},{160,32},{168,40},{176,48},{184,... | collective-permute-start | bytes 1179656 | tf_op jit(solution)/shard_map/ppermute | solution.py:336
  19.7 16.6 %all-to-all-start.1 = ((bf16[8,16,640]{2,1,0:T(8,128)(2,1)}), bf16[8,16,640]{2,1,0:T(8,128)(2,1)S(1)}, u32[]{:S(2)}, u32[]{:S(2)}) async-start(bf16[8,16,640]{2,1,0:T(8,128)(2,1)} %finish.1), calls=%async_computation.1 | async-start | bytes 327680 | tf_op jit(solution)/shard_map/all_to_all | solution.py:404
  28.4 1.0 %copy-start.8 = (bf16[576,1024]{1,0:T(8,128)(2,1)}, bf16[576,1024]{1,0:T(8,128)(2,1)S(1)}, u32[]{:S(2)}) copy-start(bf16[576,1024]{1,0:T(8,128)(2,1)S(1)} %get-tuple-element.22.partner_ref) | copy-start | bytes 3538948
  36.3 23.4 %copy-start.9 = (bf16[576,1024]{1,0:T(8,128)(2,1)S(1)}, bf16[576,1024]{1,0:T(8,128)(2,1)}, u32[]{:S(2)}) copy-start(bf16[576,1024]{1,0:T(8,128)(2,1)} %copy-done.8) | copy-start | bytes 3538948
  55.3 8.4 %collective-permute-start.1 = (bf16[8,576,128]{2,1,0:T(8,128)(2,1)S(1)}, bf16[8,576,128]{2,1,0:T(8,128)(2,1)S(1)}, u32[]{:S(2)}, u32[]{:S(2)}) collective-permute-start(bf16[8,576,128]{2,1,0:T(8,128)(2,1)S(1)} %all_to_all.20.keys_ref), channel_id=1, source_target_pairs={{0,8},{8,0},{16,24},{24,16},{32,40},{40,32},{48,56},{56,48},{64,72... | collective-permute-start | bytes 3538952 | tf_op jit(solution)/shard_map/ppermute | solution.py:414
  59.7 4.0 %copy-start.3 = (bf16[8,512,128]{2,1,0:T(8,128)(2,1)S(1)}, bf16[8,512,128]{2,1,0:T(8,128)(2,1)}, u32[]{:S(2)}) copy-start(bf16[8,512,128]{2,1,0:T(8,128)(2,1)} %absorb_ref.7) | copy-start | bytes 3145732
  63.7 6.8 %copy-start.1 = (bf16[512,2560]{1,0:T(8,128)(2,1)S(1)}, bf16[512,2560]{1,0:T(8,128)(2,1)}, u32[]{:S(2)}) copy-start(bf16[512,2560]{1,0:T(8,128)(2,1)} %values_ref.1) | copy-start | bytes 7864324
  63.7 6.8 %copy-start.2 = (s32[256,2560]{1,0:T(8,128)S(1)}, s32[256,2560]{1,0:T(8,128)}, u32[]{:S(2)}) copy-start(s32[256,2560]{1,0:T(8,128)} %pattern_ref.1) | copy-start | bytes 7864324
  68.3 12.3 %collective-permute-start.2 = (bf16[1056,128]{1,0:T(8,128)(2,1)S(1)}, bf16[1056,128]{1,0:T(8,128)(2,1)S(1)}, u32[]{:S(2)}, u32[]{:S(2)}) collective-permute-start(bf16[1056,128]{1,0:T(8,128)(2,1)S(1)} %get-tuple-element.32), channel_id=1, source_target_pairs={{0,128},{8,136},{16,144},{24,152},{32,160},{40,168},{48,176},{56,1... | collective-permute-start | bytes 811016 | tf_op jit(solution)/shard_map/ppermute | solution.py:438
  72.9 7.7 %copy-start.5 = (bf16[16,2560]{1,0:T(8,128)(2,1)S(1)}, bf16[16,2560]{1,0:T(8,128)(2,1)}, u32[]{:S(2)}) copy-start(bf16[16,2560]{1,0:T(8,128)(2,1)} %up_ref.1) | copy-start | bytes 245764
  72.9 7.7 %copy-start.6 = (bf16[1024,16]{0,1:T(8,128)(2,1)S(1)}, bf16[1024,16]{0,1:T(8,128)(2,1)}, u32[]{:S(2)}) copy-start(bf16[1024,16]{0,1:T(8,128)(2,1)} %param.24) | copy-start | bytes 98308

commit v4 on v3

--- a/solution.py
+++ b/solution.py
@@ -22,9 +22,9 @@
 VDIM = 128
 CTX = 32
 CHIPS = 8
-SLICES = 4
 PACKED = ROWS * WIDTH // 128
-KEYS = SLICES * ROWS
+HALF = ROWS // 2
+KEYS = HEADS * HALF
 WIDE = 640
 UNSEEN = -1e30
 COLS = 640
@@ -97,28 +97,35 @@
         pltpu.make_async_copy(source, target, sems.at[n])
         for n, (source, target) in enumerate(
             (
-                (values_hbm, values_ref),
-                (pattern_hbm, pattern_ref),
                 (tokens_hbm, tokens_ref),
                 (down_hbm, down_ref),
                 (up_hbm, up_ref),
+                (values_hbm, values_ref),
+                (pattern_hbm, pattern_ref),
             )
         )
     ]
     for copy in copies:
         copy.start()
-    for copy in copies:
+    for copy in copies[:3]:
         copy.wait()
-    densify(values_ref, pattern_ref, dense_ref)
     order = by_slot()
     tokens = tokens_ref[...]
     parts = [dot(tokens[:, b : b + 128], order).astype(BF16) for b in range(0, tokens.shape[1], 128)]
-    raw = dot(jnp.concatenate(parts, axis=1), dense_ref[...])
-    up = up_ref[...]
-    for term in thirds(dot_last(tokens, down_ref[...])):
-        raw += dot(term, up)
-    raw_ref[:, :, :WIDTH] = raw.reshape(HEADS, PIECE, WIDTH)
-    raw_ref[:, :, WIDTH:] = jnp.zeros((HEADS, PIECE, WIDE - WIDTH), F32)
+    low = jnp.concatenate(thirds(dot_last(tokens, down_ref[...])), axis=1)
+    raw = dot(low, jnp.concatenate([up_ref[...]] * 3, axis=0))
+    for copy in copies[3:]:
+        copy.wait()
+    densify(values_ref, pattern_ref, dense_ref)
+    raw += dot(jnp.concatenate(parts, axis=1), dense_ref[...])
+    for h in range(HEADS):
+        piece = raw[h * PIECE : (h + 1) * PIECE]
+        for c in range(LAT // 128):
+            raw_ref[h, c * PIECE : (c + 1) * PIECE, :] = piece[:, c * 128 : (c + 1) * 128]
+        rope = piece[:, LAT:]
+        raw_ref[h, LAT // 128 * PIECE :, :] = jnp.concatenate(
+            [rope[: PIECE // 2], rope[PIECE // 2 :]], axis=1
+        )
 
 
 def query_kernel(queries_ref, absorb_ref, table_ref, out_ref, token_ref):
@@ -138,11 +145,14 @@
     raw = parts_ref[0]
     for h in range(1, HEADS):
         raw += parts_ref[h]
-    latent = raw[:, :LAT]
+    latent = jnp.concatenate(
+        [raw[c * PIECE : (c + 1) * PIECE] for c in range(LAT // 128)], axis=1
+    )
+    rope = raw[LAT // 128 * PIECE :]
     meansq = jnp.mean(latent * latent, axis=-1, keepdims=True)
     normed = (latent * lax.rsqrt(meansq + 1e-06) * gain_ref[...]).astype(BF16)
     table = table_ref[pl.ds(pl.multiple_of(where_ref[3] * PIECE, PIECE), PIECE), :]
-    x = raw[:, LAT:WIDTH]
+    x = jnp.concatenate([rope[:, :ROPE], rope[:, ROPE:]], axis=0)
     half = ROPE // 2
     swapped = jnp.concatenate([x[:, half:], x[:, :half]], axis=1)
     turned = (x * table[:, :ROPE] + swapped * table[:, ROPE:]).astype(BF16)
@@ -165,14 +175,10 @@
 
 def unpack(keys_ref, part):
     latents, ropes = [], []
-    for k in range(part * SLICES, (part + 1) * SLICES):
-        latents.append(
-            jnp.concatenate(
-                [keys_ref[k, c * ROWS : (c + 1) * ROWS, :] for c in range(LAT // 128)], axis=1
-            )
-        )
-        rope = keys_ref[k, LAT // 128 * ROWS :, :]
-        ropes += [rope[:, :ROPE], rope[:, ROPE:]]
+    for k in range(HEADS):
+        rows = [c * ROWS + part * HALF for c in range(LAT // 128)]
+        latents.append(jnp.concatenate([keys_ref[k, r : r + HALF, :] for r in rows], axis=1))
+        ropes.append(keys_ref[k, LAT // 128 * ROWS :, part * ROPE : (part + 1) * ROPE])
     return jnp.concatenate(latents, axis=0), jnp.concatenate(ropes, axis=0)
 
 
@@ -182,34 +188,28 @@
         self.q_ref, self.m_ref, self.l_ref, self.acc_ref = q_ref, m_ref, l_ref, acc_ref
         self.scale = scale
 
-    def clear(self):
-        self.m_ref[...] = jnp.full(self.m_ref.shape, UNSEEN, F32)
-        self.l_ref[...] = jnp.zeros(self.l_ref.shape, F32)
-        self.acc_ref[...] = jnp.zeros(self.acc_ref.shape, F32)
-
-    def chunk(self, keys_ref, part, key_core=None):
+    def chunk(self, keys_ref, part, key_core, fresh):
         latent, rope = unpack(keys_ref, part)
         scores = dot(jnp.concatenate([latent, rope], axis=1), self.q_ref[...]) * self.scale
         if key_core is not None:
             query = lax.broadcasted_iota(jnp.int32, (1, ALL), 1) % ROWS
             key = lax.broadcasted_iota(jnp.int32, (KEYS, 1), 0)
             ahead = (2 * self.chip + self.core) * ROWS + query
-            place = (2 * (key % ROWS // PIECE) + key_core) * ROWS
-            place += (part * SLICES + key // ROWS) * PIECE + key % PIECE
+            place = (2 * (part * CHIPS // 2 + key % HALF // PIECE) + key_core) * ROWS
+            place += key // HALF * PIECE + key % PIECE
             scores = jnp.where(place <= ahead, scores, UNSEEN)
-        old = self.m_ref[...]
-        new = jnp.maximum(old, jnp.max(scores, axis=0, keepdims=True))
-        factor = jnp.exp2(old - new)
+        top = jnp.max(scores, axis=0, keepdims=True)
+        new = jnp.broadcast_to(top, (8, ALL)) if fresh else jnp.maximum(self.m_ref[...], top)
         weights = jnp.exp2(scores - new[:1])
+        total = jnp.sum(weights.reshape(KEYS // 8, 8, ALL), axis=0)
+        attended = dot(latent.T, weights.astype(BF16))
+        if not fresh:
+            factor = jnp.exp2(self.m_ref[...] - new)
+            total += self.l_ref[...] * factor
+            attended += self.acc_ref[...] * factor[:1]
         self.m_ref[...] = new
-        self.l_ref[...] = self.l_ref[...] * factor + jnp.sum(
-            weights.reshape(KEYS // 8, 8, ALL), axis=0
-        )
-        self.acc_ref[...] = self.acc_ref[...] * factor[:1] + dot(latent.T, weights.astype(BF16))
-
-    def run(self, keys_ref, key_core=None):
-        for part in range(HEADS // SLICES):
-            self.chunk(keys_ref, part, key_core)
+        self.l_ref[...] = total
+        self.acc_ref[...] = attended
 
     def head_out(self, h, absorb_ref):
         columns = slice(h * ROWS, (h + 1) * ROWS)
@@ -219,26 +219,32 @@
 
 
 def first_kernel(scale, where_ref, own_ref, partner_ref, keys_ref, *state):
+    far_chip = where_ref[1] >= CHIPS // 2
+
     @pl.when(where_ref[0] == 0)
     def _():
         rows = Rows(where_ref, partner_ref, *state, scale)
-        rows.clear()
-        rows.run(keys_ref)
+        rows.chunk(keys_ref, 0, None, True)
+        rows.chunk(keys_ref, 1, None, False)
 
     @pl.when(where_ref[0] == 1)
     def _():
         rows = Rows(where_ref, own_ref, *state, scale)
-        rows.clear()
-        rows.run(keys_ref, where_ref[2])
-
-
-def second_kernel(scale, where_ref, own_ref, partner_ref, keys_ref, absorb_ref, *refs):
+        rows.chunk(keys_ref, 0, where_ref[2], True)
+
+        @pl.when(far_chip)
+        def _():
+            rows.chunk(keys_ref, 1, where_ref[2], False)
+
+
+def second_kernel(scale, where_ref, partner_ref, keys_ref, absorb_ref, *refs):
     part_ref, *state = refs[3:]
 
     @pl.when(where_ref[0] == 0)
     def _():
         rows = Rows(where_ref, partner_ref, *state, scale)
-        rows.run(keys_ref)
+        rows.chunk(keys_ref, 0, None, False)
+        rows.chunk(keys_ref, 1, None, False)
         outs = [rows.head_out(h, absorb_ref) for h in range(HEADS)]
         for h, (out, _) in enumerate(outs):
             part_ref[h * VDIM : (h + 1) * VDIM, :] = out.astype(BF16)
@@ -246,18 +252,38 @@
         terms = [t.astype(F32) for t in thirds(logs)] + [jnp.zeros_like(logs)]
         part_ref[HEADS * VDIM :, :] = jnp.concatenate(terms, axis=0).astype(BF16)
 
-    @pl.when(where_ref[0] == 1)
+
+def third_kernel(scale, where_ref, own_ref, keys_ref, others_ref, values_ref, pattern_ref, *refs):
+    *state, dense_ref = refs[3:]
+    lower = where_ref[0] == 0
+    core = where_ref[2]
+    rows = Rows(where_ref, own_ref, *state, scale)
+
+    def weights(*steps):
+        for step in steps:
+            columns = slice(step * COLS, (step + 1) * COLS)
+            densify(values_ref.at[:, columns], pattern_ref.at[:, columns], dense_ref.at[:, columns])
+
+    @pl.when(where_ref[1] >= CHIPS // 2)
     def _():
-        Rows(where_ref, own_ref, *state, scale).run(keys_ref, 1 - where_ref[2])
-
-
-def third_kernel(scale, where_ref, own_ref, keys_ref, others_ref, *refs):
-    @pl.when(where_ref[0] == 0)
+        @pl.when(lower)
+        def _():
+            rows.chunk(keys_ref, 0, core, True)
+            rows.chunk(keys_ref, 1, core, False)
+
+        weights(0, 1)
+        rows.chunk(others_ref, 0, 1 - core, False)
+        weights(2, 3)
+        rows.chunk(others_ref, 1, 1 - core, False)
+
+    @pl.when(where_ref[1] < CHIPS // 2)
     def _():
-        rows = Rows(where_ref, own_ref, *refs[3:], scale)
-        rows.clear()
-        rows.run(keys_ref, where_ref[2])
-        rows.run(others_ref, 1 - where_ref[2])
+        @pl.when(lower)
+        def _():
+            rows.chunk(keys_ref, 0, core, True)
+
+        weights(0, 1, 2, 3)
+        rows.chunk(others_ref, 0, 1 - core, False)
 
 
 def output_kernel(
@@ -337,7 +363,7 @@
 
     raw = pl.pallas_call(
         project_kernel,
-        out_shape=shape(HEADS, PIECE, WIDE),
+        out_shape=shape(HEADS, PIECE * WIDTH // 128, 128),
         in_specs=[ANY] * 5,
         out_specs=VMEM,
         scratch_shapes=[
@@ -371,21 +397,6 @@
 
     own_query, own_token = query(columns, table)
     partner_query, partner_token = query(partner, partner_table)
-
-    step = out_cols // 2
-    dense = pl.pallas_call(
-        densify,
-        grid=(out_cols // step,),
-        out_shape=shape(2 * o_values.shape[0], out_cols, dtype=BF16),
-        in_specs=[
-            pl.BlockSpec((o_values.shape[0], step), lambda i: (0, i)),
-            pl.BlockSpec((o_pattern.shape[0], step), lambda i: (0, i)),
-        ],
-        out_specs=pl.BlockSpec((2 * o_values.shape[0], step), lambda i: (0, i)),
-        compiler_params=params(24),
-        cost_estimate=cost(2 * 256 * o_values.size, 12 * MIB),
-        name="densify",
-    )(o_values, o_pattern)
 
     piece = pl.pallas_call(
         finish_kernel,
@@ -428,24 +439,24 @@
     part, *second = pl.pallas_call(
         functools.partial(second_kernel, scale),
         out_shape=(shape(HEADS * VDIM + 4 * HEADS, ROWS, dtype=BF16),) + state,
-        in_specs=[SMEM] + [VMEM] * 7,
+        in_specs=[SMEM] + [VMEM] * 6,
         out_specs=(VMEM,) * 4,
-        input_output_aliases={5: 1, 6: 2, 7: 3},
+        input_output_aliases={4: 1, 5: 2, 6: 3},
         compiler_params=params(32),
         cost_estimate=work,
         name="second",
-    )(where, own_query, partner_query, others, absorb_v, *first)
+    )(where, partner_query, others, absorb_v, *first)
     received = lax.ppermute(part, "ctx", [(i, i + 2 * CHIPS) for i in range(2 * CHIPS)])
-    own = pl.pallas_call(
+    *own, dense = pl.pallas_call(
         functools.partial(third_kernel, scale),
-        out_shape=state,
-        in_specs=[SMEM] + [VMEM] * 6,
-        out_specs=(VMEM,) * 3,
-        input_output_aliases={4: 0, 5: 1, 6: 2},
+        out_shape=state + (shape(2 * o_values.shape[0], out_cols, dtype=BF16),),
+        in_specs=[SMEM] + [VMEM] * 8,
+        out_specs=(VMEM,) * 4,
+        input_output_aliases={6: 0, 7: 1, 8: 2},
         compiler_params=params(32),
         cost_estimate=work,
         name="third",
-    )(where, own_query, keys, others, *second)
+    )(where, own_query, keys, others, o_values, o_pattern, *second)
 
     terms = pl.pallas_call(
         output_kernel,

time: 99.5 us -> 94.5 us (0.950)
  the two profiles are of different devices: /device:TPU:1 before, /device:TPU:2 now
where the time goes in v4:
time: 94.5 us; the launch traced here: 94.1 us
  blocking collectives  35.2 us (37%)
  waiting for transfers between devices  21.5 us (23%)
  starting transfers between devices  19.4 us (21%)
  Pallas kernels  16.1 us (17%)
  local copies, waits for them, and re-layouts  1.36 us (1%)
    all_to_all x1, blocking collectives, local(): keys = lax.all_to_all(packed, 'head', 0, 0, tiled=True)  19.4 us
    all_to_all x1, blocking collectives, local(): lax.all_to_all(terms.reshape(HEADS, out_cols // HEADS, ROWS), 'head', 0,...  15.8 us
    ppermute x1, waiting for transfers between devices, local(): lax.ppermute(part, 'ctx', [(i, i + 2 * CHIPS) for i in range(2 * CHIPS)])  8.53 us
    all_to_all x1, starting transfers between devices, local(): lax.all_to_all(piece, 'ctx', 0, 0, tiled=True, axis_index_groups=along_z)  8.48 us
    all_to_all x1, waiting for transfers between devices, local(): lax.all_to_all(piece, 'ctx', 0, 0, tiled=True, axis_index_groups=along_z)  7.89 us
    all_to_all x1, starting transfers between devices, local(): parts = lax.all_to_all(raw, 'head', 0, 0, tiled=True)  6.05 us
    all_to_all x1, waiting for transfers between devices, local(): parts = lax.all_to_all(raw, 'head', 0, 0, tiled=True)  4.69 us
    pallas_call x1, Pallas kernels, local(): pl.pallas_call(functools.partial(third_kernel, scale), out_shape=state +...  4.12 us
  transfers between devices with their start and end apart: 5, of which 4 were waited for; matrix products, arithmetic and copies ran while one was open for 0% of the time, Pallas kernels for 9%

profile of v4, /device:TPU:2, one launch (start us, length us, event | category | flops | bytes accessed | tf_op | source)
XLA Modules:
  0.0 94.1 jit_solution(11861285690260319233)
XLA Ops:
  0.0 0.0 copy-start.4
  0.0 0.0 copy-start
  0.0 0.0 copy-start.7
  0.0 2.9 %project.1 = f32[8,72,128]{2,1,0:T(8,128)} custom-call(bf16[128,640]{1,0:T(8,128)(2,1)} %tokens_hbm.1, bf16[320,576]{1,0:T(8,128)(2,1)} %values_hbm.1, s32[160,576]{1,0:T(8,128)} %pattern_hbm.1, bf16[16,640]{1,0:T(8,128)(2,1)} %bitcast.19, bf16[16,576]{1,0:T(8,128)(2,1)} %up_hbm.1), custom_call_target="tpu_custom_call" | custom-call | tf_op jit(solution)/shard_map/project/pallas_call | solution.py:364
  2.9 6.0 %all-to-all-start = ((f32[8,72,128]{2,1,0:T(8,128)}), f32[8,72,128]{2,1,0:T(8,128)S(1)}, u32[]{:S(2)}, u32[]{:S(2)}) async-start(f32[8,72,128]{2,1,0:T(8,128)} %project.1), calls=%async_computation | async-start | bytes 589824 | tf_op jit(solution)/shard_map/all_to_all | solution.py:381
  8.9 3.3 %collective-permute-start = (bf16[8,192,128]{2,1,0:T(8,128)(2,1)}, bf16[8,192,128]{2,1,0:T(8,128)(2,1)S(1)}, u32[]{:S(2)}, u32[]{:S(2)}) collective-permute-start(bf16[8,192,128]{2,1,0:T(8,128)(2,1)} %bitcast.15), channel_id=1, source_target_pairs={{128,0},{136,8},{144,16},{152,24},{160,32},{168,40},{176,48},{184,... | collective-permute-start | bytes 1179656 | tf_op jit(solution)/shard_map/ppermute | solution.py:362
  12.3 0.2 multiply_cosine_fusion
  12.6 0.1 copy.20.table_ref
  12.7 0.0 copy-done.4
  12.7 0.0 copy-done
  12.7 0.5 query.2
  13.2 0.1 pad_add_fusion.where_ref
  13.3 4.7 %all-to-all-done.parts_ref = f32[8,72,128]{2,1,0:T(8,128)S(1)} async-done(((f32[8,72,128]{2,1,0:T(8,128)}), f32[8,72,128]{2,1,0:T(8,128)S(1)}, u32[]{:S(2)}, u32[]{:S(2)}) %all-to-all-start) | async-done | bytes 294944 | tf_op jit(solution)/shard_map/all_to_all | solution.py:381
  18.0 0.0 copy-done.7
  18.0 1.4 %finish.1 = bf16[8,16,640]{2,1,0:T(8,128)(2,1)} custom-call(s32[4]{0:T(128)S(1)} %pad_add_fusion.where_ref, f32[8,72,128]{2,1,0:T(8,128)S(1)} %all-to-all-done.parts_ref, f32[1,512]{1,0:T(1,128)S(1)} %bitcast.18, f32[128,128]{1,0:T(8,128)S(1)} %copy.20.table_ref, f32[8,128]{1,0:T(8,128)S(1)} %get-tuple-element.21.refs_0_), custom_call_target="tpu_custom_call" | custom-call | tf_op jit(solution)/shard_map/finish/pallas_call | solution.py:401
  19.3 8.5 %all-to-all-start.1 = ((bf16[8,16,640]{2,1,0:T(8,128)(2,1)}), bf16[8,16,640]{2,1,0:T(8,128)(2,1)S(1)}, u32[]{:S(2)}, u32[]{:S(2)}) async-start(bf16[8,16,640]{2,1,0:T(8,128)(2,1)} %finish.1), calls=%async_computation.1 | async-start | bytes 327680 | tf_op jit(solution)/shard_map/all_to_all | solution.py:415
  27.8 0.0 collective-permute-done.queries_ref
  27.8 0.5 query.3
  28.3 0.0 copy-start.8
  28.3 1.0 %copy-done.8 = bf16[576,1024]{1,0:T(8,128)(2,1)} copy-done((bf16[576,1024]{1,0:T(8,128)(2,1)}, bf16[576,1024]{1,0:T(8,128)(2,1)S(1)}, u32[]{:S(2)}) %copy-start.8) | copy-done | bytes 1179672
  29.4 7.9 %all-to-all-done.1.column_ref = bf16[8,16,640]{2,1,0:T(8,128)(2,1)S(1)} async-done(((bf16[8,16,640]{2,1,0:T(8,128)(2,1)}), bf16[8,16,640]{2,1,0:T(8,128)(2,1)S(1)}, u32[]{:S(2)}, u32[]{:S(2)}) %all-to-all-start.1) | async-done | bytes 163872 | tf_op jit(solution)/shard_map/all_to_all | solution.py:415
  37.3 0.0 copy-start.9
  37.3 0.2 pack.1
  37.4 19.4 %all_to_all.20.keys_ref = bf16[8,576,128]{2,1,0:T(8,128)(2,1)S(1)} all-to-all(bf16[8,576,128]{2,1,0:T(8,128)(2,1)S(1)} %pack.1), channel_id=1, replica_groups=mesh['ctx'=32,'head'=8] {'head'}, dimensions={0} | all-to-all | bytes 2359296 | tf_op jit(solution)/shard_map/all_to_all | solution.py:424
  56.8 0.0 collective-permute-start.1
  56.8 0.0 copy-done.9
  56.8 0.0 copy-start.3
  56.9 2.4 %first.1 = (f32[8,1024]{1,0:T(8,128)S(1)}, f32[8,1024]{1,0:T(8,128)S(1)}, f32[512,1024]{1,0:T(8,128)S(1)}) custom-call(s32[4]{0:T(128)S(1)} %pad_add_fusion.where_ref, bf16[576,1024]{1,0:T(8,128)(2,1)S(1)} %get-tuple-element.20.own_ref, bf16[576,1024]{1,0:T(8,128)(2,1)S(1)} %copy-done.9, bf16[8,576,128]{2,1,0:T(8,128)(2,1)S(1)} %all_to_all.20.keys_ref), custom_call_target="tpu_custom_call" | custom-call | flops 2281701376 | bytes 8388608 | tf_op jit(solution)/shard_map/first/pallas_call | solution.py:430
  59.3 0.4 collective-permute-done.1.keys_ref.others_ref
  59.7 0.0 copy-done.3
  59.7 0.0 copy-start.1
  59.7 0.0 copy-start.2
  59.7 0.7 second.1
  60.4 1.6 %collective-permute-start.2 = (bf16[1056,128]{1,0:T(8,128)(2,1)S(1)}, bf16[1056,128]{1,0:T(8,128)(2,1)S(1)}, u32[]{:S(2)}, u32[]{:S(2)}) collective-permute-start(bf16[1056,128]{1,0:T(8,128)(2,1)S(1)} %get-tuple-element.33), channel_id=1, source_target_pairs={{0,128},{8,136},{16,144},{24,152},{32,160},{40,168},{48,176},{56,1... | collective-permute-start | bytes 811016 | tf_op jit(solution)/shard_map/ppermute | solution.py:449
  62.0 0.0 copy-done.1
  62.0 0.2 copy-done.2
  62.2 0.0 copy-start.5
  62.2 0.0 copy-start.6
  62.2 4.1 %third.1 = (f32[8,1024]{1,0:T(8,128)S(1)}, f32[8,1024]{1,0:T(8,128)S(1)}, f32[512,1024]{1,0:T(8,128)S(1)}, bf16[1024,2560]{1,0:T(8,128)(2,1)S(1)}) custom-call(s32[4]{0:T(128)S(1)} %pad_add_fusion.where_ref, bf16[576,1024]{1,0:T(8,128)(2,1)S(1)} %get-tuple-element.20.own_ref, ...), custom_call_target="tpu_custom_call", output_to_operand_aliasing={{0}: (6, {}), {1}: (7, {}), {2}: (8, {})} | custom-call | flops 2281701376 | bytes 8388608 | tf_op jit(solution)/shard_map/third/pallas_call | solution.py:450
  66.4 8.5 %collective-permute-done.2.part_ref = bf16[1056,128]{1,0:T(8,128)(2,1)S(1)} collective-permute-done((bf16[1056,128]{1,0:T(8,128)(2,1)S(1)}, bf16[1056,128]{1,0:T(8,128)(2,1)S(1)}, u32[]{:S(2)}, u32[]{:S(2)}) %collective-permute-start.2) | collective-permute-done | bytes 270368 | tf_op jit(solution)/shard_map/ppermute | solution.py:449
  74.9 0.0 copy-done.5
  74.9 0.0 copy-done.6
  74.9 2.7 %output.1 = bf16[2560,128]{1,0:T(8,128)(2,1)S(1)} custom-call(s32[4]{0:T(128)S(1)} %pad_add_fusion.where_ref, f32[8,1024]{1,0:T(8,128)S(1)} %get-tuple-element.30.m_ref, f32[8,1024]{1,0:T(8,128)S(1)} %get-tuple-element.31.l_ref, f32[512,1024]{1,0:T(8,128)S(1)} %get-tuple-element.32.acc_ref, bf16[1056,128]{1,0:T(8,128)(2,1)S(1)} %collective-permute-done.2.part_ref, ...), custom_call_target="tpu_custom_call" | custom-call | flops 671088640 | bytes 8388608 | tf_op jit(solution)/shard_map/output/pallas_call | solution.py:461
  77.6 15.8 %all_to_all.21.parts_ref = bf16[8,320,128]{2,1,0:T(8,128)(2,1)S(1)} all-to-all(bf16[8,320,128]{2,1,0:T(8,128)(2,1)S(1)} %bitcast.14), channel_id=1, replica_groups=mesh['ctx'=32,'head'=8] {'head'}, dimensions={0} | all-to-all | bytes 1310720 | tf_op jit(solution)/shard_map/all_to_all | solution.py:470
  93.4 0.8 total.1
  (4 shorter events, 0.0 us)
Async XLA Ops:
  0.0 12.7 %copy-start.4 = (bf16[128,8,192]{0,2,1:T(8,128)(2,1)S(1)}, bf16[128,8,192]{0,2,1:T(8,128)(2,1)}, u32[]{:S(2)}) copy-start(bf16[128,8,192]{0,2,1:T(8,128)(2,1)} %param.19) | copy-start | bytes 1179652
  0.0 12.7 %copy-start = (bf16[8,128,512]{2,1,0:T(8,128)(2,1)S(1)}, bf16[8,128,512]{2,1,0:T(8,128)(2,1)}, u32[]{:S(2)}) copy-start(bf16[8,128,512]{2,1,0:T(8,128)(2,1)} %absorb_ref.5) | copy-start | bytes 3145732
  0.0 18.0 %copy-start.7 = (f32[512]{0:T(512)S(1)}, f32[512]{0:T(512)}, u32[]{:S(2)}) copy-start(f32[512]{0:T(512)} %param.18) | copy-start | bytes 6148
  2.9 15.1 %all-to-all-start = ((f32[8,72,128]{2,1,0:T(8,128)}), f32[8,72,128]{2,1,0:T(8,128)S(1)}, u32[]{:S(2)}, u32[]{:S(2)}) async-start(f32[8,72,128]{2,1,0:T(8,128)} %project.1), calls=%async_computation | async-start | bytes 589824 | tf_op jit(solution)/shard_map/all_to_all | solution.py:381
  8.9 18.9 %collective-permute-start = (bf16[8,192,128]{2,1,0:T(8,128)(2,1)}, bf16[8,192,128]{2,1,0:T(8,128)(2,1)S(1)}, u32[]{:S(2)}, u32[]{:S(2)}) collective-permute-start(bf16[8,192,128]{2,1,0:T(8,128)(2,1)} %bitcast.15), channel_id=1, source_target_pairs={{128,0},{136,8},{144,16},{152,24},{160,32},{168,40},{176,48},{184,... | collective-permute-start | bytes 1179656 | tf_op jit(solution)/shard_map/ppermute | solution.py:362
  19.3 17.9 %all-to-all-start.1 = ((bf16[8,16,640]{2,1,0:T(8,128)(2,1)}), bf16[8,16,640]{2,1,0:T(8,128)(2,1)S(1)}, u32[]{:S(2)}, u32[]{:S(2)}) async-start(bf16[8,16,640]{2,1,0:T(8,128)(2,1)} %finish.1), calls=%async_computation.1 | async-start | bytes 327680 | tf_op jit(solution)/shard_map/all_to_all | solution.py:415
  28.3 1.0 %copy-start.8 = (bf16[576,1024]{1,0:T(8,128)(2,1)}, bf16[576,1024]{1,0:T(8,128)(2,1)S(1)}, u32[]{:S(2)}) copy-start(bf16[576,1024]{1,0:T(8,128)(2,1)S(1)} %get-tuple-element.23.partner_ref) | copy-start | bytes 3538948
  37.3 19.6 %copy-start.9 = (bf16[576,1024]{1,0:T(8,128)(2,1)S(1)}, bf16[576,1024]{1,0:T(8,128)(2,1)}, u32[]{:S(2)}) copy-start(bf16[576,1024]{1,0:T(8,128)(2,1)} %copy-done.8) | copy-start | bytes 3538948
  56.8 2.8 %collective-permute-start.1 = (bf16[8,576,128]{2,1,0:T(8,128)(2,1)S(1)}, bf16[8,576,128]{2,1,0:T(8,128)(2,1)S(1)}, u32[]{:S(2)}, u32[]{:S(2)}) collective-permute-start(bf16[8,576,128]{2,1,0:T(8,128)(2,1)S(1)} %all_to_all.20.keys_ref), channel_id=1, source_target_pairs={{0,8},{8,0},{16,24},{24,16},{32,40},{40,32},{48,56},{56,48},{64,72... | collective-permute-start | bytes 3538952 | tf_op jit(solution)/shard_map/ppermute | solution.py:425
  56.8 2.8 %copy-start.3 = (bf16[8,512,128]{2,1,0:T(8,128)(2,1)S(1)}, bf16[8,512,128]{2,1,0:T(8,128)(2,1)}, u32[]{:S(2)}) copy-start(bf16[8,512,128]{2,1,0:T(8,128)(2,1)} %absorb_ref.7) | copy-start | bytes 3145732
  59.7 2.3 %copy-start.1 = (bf16[512,2560]{1,0:T(8,128)(2,1)S(1)}, bf16[512,2560]{1,0:T(8,128)(2,1)}, u32[]{:S(2)}) copy-start(bf16[512,2560]{1,0:T(8,128)(2,1)} %values_ref.1) | copy-start | bytes 7864324
  59.7 2.5 %copy-start.2 = (s32[256,2560]{1,0:T(8,128)S(1)}, s32[256,2560]{1,0:T(8,128)}, u32[]{:S(2)}) copy-start(s32[256,2560]{1,0:T(8,128)} %pattern_ref.1) | copy-start | bytes 7864324
  60.4 14.5 %collective-permute-start.2 = (bf16[1056,128]{1,0:T(8,128)(2,1)S(1)}, bf16[1056,128]{1,0:T(8,128)(2,1)S(1)}, u32[]{:S(2)}, u32[]{:S(2)}) collective-permute-start(bf16[1056,128]{1,0:T(8,128)(2,1)S(1)} %get-tuple-element.33), channel_id=1, source_target_pairs={{0,128},{8,136},{16,144},{24,152},{32,160},{40,168},{48,176},{56,1... | collective-permute-start | bytes 811016 | tf_op jit(solution)/shard_map/ppermute | solution.py:449
  62.2 12.7 %copy-start.5 = (bf16[16,2560]{1,0:T(8,128)(2,1)S(1)}, bf16[16,2560]{1,0:T(8,128)(2,1)}, u32[]{:S(2)}) copy-start(bf16[16,2560]{1,0:T(8,128)(2,1)} %up_ref.1) | copy-start | bytes 245764
  62.2 12.7 %copy-start.6 = (bf16[1024,16]{0,1:T(8,128)(2,1)S(1)}, bf16[1024,16]{0,1:T(8,128)(2,1)}, u32[]{:S(2)}) copy-start(bf16[1024,16]{0,1:T(8,128)(2,1)} %param.24) | copy-start | bytes 98308

commit v5 on v4

--- a/solution.py
+++ b/solution.py
@@ -66,19 +66,27 @@
         half = count // 2
         pair = dot(unpair(count), values_ref[begin : begin + count, :]).astype(BF16)
         v0, v1 = pair[:half], pair[half:]
-        p = pattern_ref[begin // 2 : begin // 2 + half, :].astype(F32).astype(BF16)
-        is_0, is_1, is_2, is_3, is_4, is_5 = (p == jnp.asarray(k, BF16) for k in range(6))
+        p = pattern_ref[begin // 2 : begin // 2 + half, :].astype(BF16)
+        is_0, is_1, is_3, is_5 = (p == jnp.asarray(k, BF16) for k in (0, 1, 3, 5))
+        from_0 = p < jnp.asarray(3, BF16)
+        later = jnp.where(from_0, zero, v0)
+        to_2 = is_1 | is_3
         slots = (
-            jnp.where(p < jnp.asarray(3, BF16), v0, zero),
-            jnp.where(is_0, v1, jnp.where(is_3 | is_4, v0, zero)),
-            jnp.where(is_1 | is_3, v1, jnp.where(is_5, v0, zero)),
-            jnp.where(is_2 | is_4 | is_5, v1, zero),
+            jnp.where(from_0, v0, zero),
+            jnp.where(is_0, v1, jnp.where(is_5, zero, later)),
+            jnp.where(to_2, v1, jnp.where(is_5, later, zero)),
+            jnp.where(is_0 | to_2, zero, v1),
         )
         for k, slot in enumerate(slots):
             for b in range(half // 32):
                 row = 2 * begin + 128 * b + 32 * k
                 dense_ref[row : row + 32, :] = slot[32 * b : 32 * b + 32]
         begin += count
+
+
+def position():
+    ctx = lax.axis_index("ctx")
+    return ctx >> 4, (ctx >> 1) & 7, ctx & 1, lax.axis_index("head")
 
 
 def thirds(x):
@@ -140,7 +148,7 @@
         out_ref[LAT:, columns] = (x * cos + swapped * sin).astype(BF16)
 
 
-def finish_kernel(where_ref, parts_ref, gain_ref, table_ref, *refs):
+def finish_kernel(parts_ref, gain_ref, table_ref, *refs):
     out_ref = refs[-1]
     raw = parts_ref[0]
     for h in range(1, HEADS):
@@ -151,7 +159,7 @@
     rope = raw[LAT // 128 * PIECE :]
     meansq = jnp.mean(latent * latent, axis=-1, keepdims=True)
     normed = (latent * lax.rsqrt(meansq + 1e-06) * gain_ref[...]).astype(BF16)
-    table = table_ref[pl.ds(pl.multiple_of(where_ref[3] * PIECE, PIECE), PIECE), :]
+    table = table_ref[pl.ds(pl.multiple_of(position()[3] * PIECE, PIECE), PIECE), :]
     x = jnp.concatenate([rope[:, :ROPE], rope[:, ROPE:]], axis=0)
     half = ROPE // 2
     swapped = jnp.concatenate([x[:, half:], x[:, :half]], axis=1)
@@ -183,8 +191,8 @@
 
 
 class Rows:
-    def __init__(self, where_ref, q_ref, m_ref, l_ref, acc_ref, scale):
-        self.chip, self.core = where_ref[1], where_ref[2]
+    def __init__(self, q_ref, m_ref, l_ref, acc_ref, scale):
+        _, self.chip, self.core, _ = position()
         self.q_ref, self.m_ref, self.l_ref, self.acc_ref = q_ref, m_ref, l_ref, acc_ref
         self.scale = scale
 
@@ -218,31 +226,32 @@
         return dot_first(absorb_ref[h], attended), self.m_ref[:1, columns] + jnp.log2(total)
 
 
-def first_kernel(scale, where_ref, own_ref, partner_ref, keys_ref, *state):
-    far_chip = where_ref[1] >= CHIPS // 2
-
-    @pl.when(where_ref[0] == 0)
+def first_kernel(scale, own_ref, partner_ref, keys_ref, *state):
+    half, chip, core, _ = position()
+
+    @pl.when(half == 0)
     def _():
-        rows = Rows(where_ref, partner_ref, *state, scale)
+        rows = Rows(partner_ref, *state, scale)
         rows.chunk(keys_ref, 0, None, True)
         rows.chunk(keys_ref, 1, None, False)
 
-    @pl.when(where_ref[0] == 1)
+    @pl.when(half == 1)
     def _():
-        rows = Rows(where_ref, own_ref, *state, scale)
-        rows.chunk(keys_ref, 0, where_ref[2], True)
-
-        @pl.when(far_chip)
+        rows = Rows(own_ref, *state, scale)
+        rows.chunk(keys_ref, 0, core, True)
+
+        @pl.when(chip >= CHIPS // 2)
         def _():
-            rows.chunk(keys_ref, 1, where_ref[2], False)
-
-
-def second_kernel(scale, where_ref, partner_ref, keys_ref, absorb_ref, *refs):
+            rows.chunk(keys_ref, 1, core, False)
+
+
+def second_kernel(scale, partner_ref, keys_ref, absorb_ref, *refs):
     part_ref, *state = refs[3:]
-
-    @pl.when(where_ref[0] == 0)
+    half = position()[0]
+
+    @pl.when(half == 0)
     def _():
-        rows = Rows(where_ref, partner_ref, *state, scale)
+        rows = Rows(partner_ref, *state, scale)
         rows.chunk(keys_ref, 0, None, False)
         rows.chunk(keys_ref, 1, None, False)
         outs = [rows.head_out(h, absorb_ref) for h in range(HEADS)]
@@ -253,56 +262,61 @@
         part_ref[HEADS * VDIM :, :] = jnp.concatenate(terms, axis=0).astype(BF16)
 
 
-def third_kernel(scale, where_ref, own_ref, keys_ref, others_ref, values_ref, pattern_ref, *refs):
-    *state, dense_ref = refs[3:]
-    lower = where_ref[0] == 0
-    core = where_ref[2]
-    rows = Rows(where_ref, own_ref, *state, scale)
+def third_kernel(
+    scale, own_ref, keys_ref, others_ref, values_ref, pattern_ref, absorb_ref, *refs
+):
+    out_ref, log_ref, dense_ref, *state = refs[3:]
+    half, chip, core, _ = position()
+    lower = half == 0
+    rows = Rows(own_ref, *state, scale)
 
     def weights(*steps):
         for step in steps:
             columns = slice(step * COLS, (step + 1) * COLS)
             densify(values_ref.at[:, columns], pattern_ref.at[:, columns], dense_ref.at[:, columns])
 
-    @pl.when(where_ref[1] >= CHIPS // 2)
+    @pl.when(chip >= CHIPS // 2)
+    def _():
+        @pl.when(lower)
+        def _():
+            rows.chunk(keys_ref, 0, None, True)
+            rows.chunk(keys_ref, 1, core, False)
+
+        weights(0, 1)
+        rows.chunk(others_ref, 0, None, False)
+        weights(2, 3)
+        rows.chunk(others_ref, 1, 1 - core, False)
+
+    @pl.when(chip < CHIPS // 2)
     def _():
         @pl.when(lower)
         def _():
             rows.chunk(keys_ref, 0, core, True)
-            rows.chunk(keys_ref, 1, core, False)
-
-        weights(0, 1)
-        rows.chunk(others_ref, 0, 1 - core, False)
-        weights(2, 3)
-        rows.chunk(others_ref, 1, 1 - core, False)
-
-    @pl.when(where_ref[1] < CHIPS // 2)
-    def _():
-        @pl.when(lower)
-        def _():
-            rows.chunk(keys_ref, 0, core, True)
 
         weights(0, 1, 2, 3)
         rows.chunk(others_ref, 0, 1 - core, False)
 
-
-def output_kernel(
-    where_ref, m_ref, l_ref, acc_ref, part_ref, absorb_ref, down_ref, up_ref, dense_ref,
-    out_ref,
-):
-    upper = where_ref[0]
-    rows = Rows(where_ref, None, m_ref, l_ref, acc_ref, None)
+    outs = [rows.head_out(h, absorb_ref) for h in range(HEADS)]
+    for h, (out, _) in enumerate(outs):
+        out_ref[h * VDIM : (h + 1) * VDIM, :] = out
+    log_ref[...] = jnp.concatenate([log for _, log in outs], axis=0)
+
+
+def output_kernel(mine_ref, log_ref, part_ref, down_ref, up_ref, dense_ref, out_ref):
+    upper = position()[0]
     logs = part_ref[HEADS * VDIM :, :].astype(F32)
     logs = logs[:HEADS] + logs[HEADS : 2 * HEADS] + logs[2 * HEADS : 3 * HEADS]
-    mine = [rows.head_out(h, absorb_ref) for h in range(HEADS)]
+    logs = jnp.where(upper == 1, logs, -jnp.inf)
+    own_logs = log_ref[...]
+    top = jnp.maximum(own_logs, logs)
+    own_weights, weights = jnp.exp2(own_logs - top), jnp.exp2(logs - top)
+    share = 1.0 / (own_weights + weights)
+    own_weights, weights = own_weights * share, weights * share
     outs = []
-    for h, (own, log) in enumerate(mine):
-        other_log = jnp.where(upper == 1, logs[h : h + 1], -jnp.inf)
-        top = jnp.maximum(log, other_log)
-        weight, other_weight = jnp.exp2(log - top), jnp.exp2(other_log - top)
-        share = 1.0 / (weight + other_weight)
-        other = part_ref[h * VDIM : (h + 1) * VDIM, :].astype(F32)
-        outs.append((own * (weight * share) + other * (other_weight * share)).astype(BF16))
+    for h in range(HEADS):
+        span = slice(h * VDIM, (h + 1) * VDIM)
+        other = part_ref[span, :].astype(F32) * weights[h : h + 1]
+        outs.append((mine_ref[span, :] * own_weights[h : h + 1] + other).astype(BF16))
     order = by_slot()
     flat = jnp.concatenate([dot_first(out, order).astype(BF16) for out in outs], axis=1)
     lowrank = dot(down_ref[...], jnp.concatenate(outs, axis=0))
@@ -334,7 +348,6 @@
 
 
 VMEM = pl.BlockSpec(memory_space=pltpu.VMEM)
-SMEM = pl.BlockSpec(memory_space=pltpu.SMEM)
 ANY = pl.BlockSpec(memory_space=pl.ANY)
 
 
@@ -351,9 +364,6 @@
     o_values, o_pattern, o_down, o_up,
 ):
     ctx = lax.axis_index("ctx")
-    head = lax.axis_index("head")
-    upper = ctx // (2 * CHIPS)
-    where = jnp.stack([upper, (ctx // 2) % CHIPS, ctx % 2, head]).astype(jnp.int32)
     scale = LOG2E / math.sqrt(queries.shape[2])
     out_cols = o_values.shape[1]
     rank = o_down.shape[1]
@@ -401,11 +411,11 @@
     piece = pl.pallas_call(
         finish_kernel,
         out_shape=shape(CHIPS, PIECE, WIDE, dtype=BF16),
-        in_specs=[SMEM] + [VMEM] * 4,
+        in_specs=[VMEM] * 4,
         out_specs=VMEM,
         compiler_params=params(16),
         name="finish",
-    )(where, parts, kv_gain.reshape(1, LAT), table, own_token)
+    )(parts, kv_gain.reshape(1, LAT), table, own_token)
 
     along_z = [
         [(u * CHIPS + chip) * 2 + core for chip in range(CHIPS)]
@@ -430,43 +440,48 @@
     first = pl.pallas_call(
         functools.partial(first_kernel, scale),
         out_shape=state,
-        in_specs=[SMEM, VMEM, VMEM, VMEM],
+        in_specs=[VMEM] * 3,
         out_specs=(VMEM,) * 3,
         compiler_params=params(32),
         cost_estimate=work,
         name="first",
-    )(where, own_query, partner_query, keys)
+    )(own_query, partner_query, keys)
     part, *second = pl.pallas_call(
         functools.partial(second_kernel, scale),
         out_shape=(shape(HEADS * VDIM + 4 * HEADS, ROWS, dtype=BF16),) + state,
-        in_specs=[SMEM] + [VMEM] * 6,
+        in_specs=[VMEM] * 6,
         out_specs=(VMEM,) * 4,
-        input_output_aliases={4: 1, 5: 2, 6: 3},
+        input_output_aliases={3: 1, 4: 2, 5: 3},
         compiler_params=params(32),
         cost_estimate=work,
         name="second",
-    )(where, partner_query, others, absorb_v, *first)
+    )(partner_query, others, absorb_v, *first)
     received = lax.ppermute(part, "ctx", [(i, i + 2 * CHIPS) for i in range(2 * CHIPS)])
-    *own, dense = pl.pallas_call(
+    mine, logs, dense, *_ = pl.pallas_call(
         functools.partial(third_kernel, scale),
-        out_shape=state + (shape(2 * o_values.shape[0], out_cols, dtype=BF16),),
-        in_specs=[SMEM] + [VMEM] * 8,
-        out_specs=(VMEM,) * 4,
-        input_output_aliases={6: 0, 7: 1, 8: 2},
+        out_shape=(
+            shape(HEADS * VDIM, ROWS),
+            shape(HEADS, ROWS),
+            shape(2 * o_values.shape[0], out_cols, dtype=BF16),
+        )
+        + state,
+        in_specs=[VMEM] * 9,
+        out_specs=(VMEM,) * 6,
+        input_output_aliases={6: 3, 7: 4, 8: 5},
         compiler_params=params(32),
         cost_estimate=work,
         name="third",
-    )(where, own_query, keys, others, o_values, o_pattern, *second)
+    )(own_query, keys, others, o_values, o_pattern, absorb_v, *second)
 
     terms = pl.pallas_call(
         output_kernel,
         out_shape=shape(out_cols, ROWS, dtype=BF16),
-        in_specs=[SMEM] + [VMEM] * 8,
+        in_specs=[VMEM] * 6,
         out_specs=VMEM,
         compiler_params=params(32),
         cost_estimate=cost(2 * ROWS * HEADS * VDIM * out_cols, 8 * MIB),
         name="output",
-    )(where, *own, received, absorb_v, o_down.T, o_up, dense)
+    )(mine, logs, received, o_down.T, o_up, dense)
     shares = lax.all_to_all(
         terms.reshape(HEADS, out_cols // HEADS, ROWS), "head", 0, 0, tiled=True
     )

time: 94.5 us -> 91.7 us (0.970)
  Pallas kernels: 16.1 us -> 12.8 us
    pallas_call x1, Pallas kernels: 2.73 us -> 1.73 us  [local(): pl.pallas_call(output_kernel, out_shape=shape(out_cols, ROWS, dtype=BF16)...]
  transfers between devices with their start and end apart: 5 -> 5, of which waited for: 4 -> 4; matrix products, arithmetic and copies ran while one was open for 0% -> 0% of each run, Pallas kernels for 9% -> 8%
where the time goes in v5:
time: 91.7 us; the launch traced here: 91.3 us
  blocking collectives  35.2 us (38%)
  waiting for transfers between devices  21.4 us (23%)
  starting transfers between devices  19.4 us (21%)
  Pallas kernels  12.8 us (14%)
  local copies, waits for them, and re-layouts  2.09 us (2%)
    all_to_all x1, blocking collectives, local(): keys = lax.all_to_all(packed, 'head', 0, 0, tiled=True)  19.4 us
    all_to_all x1, blocking collectives, local(): lax.all_to_all(terms.reshape(HEADS, out_cols // HEADS, ROWS), 'head', 0,...  15.7 us
    all_to_all x1, starting transfers between devices, local(): lax.all_to_all(piece, 'ctx', 0, 0, tiled=True, axis_index_groups=along_z)  8.48 us
    all_to_all x1, waiting for transfers between devices, local(): lax.all_to_all(piece, 'ctx', 0, 0, tiled=True, axis_index_groups=along_z)  7.89 us
    ppermute x1, waiting for transfers between devices, local(): lax.ppermute(part, 'ctx', [(i, i + 2 * CHIPS) for i in range(2 * CHIPS)])  7.71 us
    all_to_all x1, starting transfers between devices, local(): parts = lax.all_to_all(raw, 'head', 0, 0, tiled=True)  6.05 us
    all_to_all x1, waiting for transfers between devices, local(): parts = lax.all_to_all(raw, 'head', 0, 0, tiled=True)  4.83 us
    pallas_call x1, Pallas kernels, local(): pl.pallas_call(functools.partial(third_kernel, scale), out_shape=(shape(H...  3.7 us
  transfers between devices with their start and end apart: 5, of which 4 were waited for; matrix products, arithmetic and copies ran while one was open for 0% of the time, Pallas kernels for 8%

profile of v5, /device:TPU:2, one launch (start us, length us, event | category | flops | bytes accessed | tf_op | source)
XLA Modules:
  0.0 91.3 jit_solution(17616070877464267482)
XLA Ops:
  0.0 0.0 copy-start.4
  0.0 0.0 copy-start
  0.0 0.0 copy-start.7
  0.0 2.8 %project.1 = f32[8,72,128]{2,1,0:T(8,128)} custom-call(bf16[128,640]{1,0:T(8,128)(2,1)} %tokens_hbm.1, bf16[320,576]{1,0:T(8,128)(2,1)} %values_hbm.1, s32[160,576]{1,0:T(8,128)} %pattern_hbm.1, bf16[16,640]{1,0:T(8,128)(2,1)} %bitcast.15, bf16[16,576]{1,0:T(8,128)(2,1)} %up_hbm.1), custom_call_target="tpu_custom_call" | custom-call | tf_op jit(solution)/shard_map/project/pallas_call | solution.py:374
  2.8 6.0 %all-to-all-start = ((f32[8,72,128]{2,1,0:T(8,128)}), f32[8,72,128]{2,1,0:T(8,128)S(1)}, u32[]{:S(2)}, u32[]{:S(2)}) async-start(f32[8,72,128]{2,1,0:T(8,128)} %project.1), calls=%async_computation | async-start | bytes 589824 | tf_op jit(solution)/shard_map/all_to_all | solution.py:391
  8.9 3.3 %collective-permute-start = (bf16[8,192,128]{2,1,0:T(8,128)(2,1)}, bf16[8,192,128]{2,1,0:T(8,128)(2,1)S(1)}, u32[]{:S(2)}, u32[]{:S(2)}) collective-permute-start(bf16[8,192,128]{2,1,0:T(8,128)(2,1)} %bitcast.11), channel_id=1, source_target_pairs={{128,0},{136,8},{144,16},{152,24},{160,32},{168,40},{176,48},{184,... | collective-permute-start | bytes 1179656 | tf_op jit(solution)/shard_map/ppermute | solution.py:372
  12.3 0.2 multiply_cosine_fusion
  12.5 0.1 copy.20.table_ref
  12.6 0.0 copy-done.4
  12.6 0.0 copy-done
  12.6 0.5 query.2
  13.1 4.8 %all-to-all-done.parts_ref = f32[8,72,128]{2,1,0:T(8,128)S(1)} async-done(((f32[8,72,128]{2,1,0:T(8,128)}), f32[8,72,128]{2,1,0:T(8,128)S(1)}, u32[]{:S(2)}, u32[]{:S(2)}) %all-to-all-start) | async-done | bytes 294944 | tf_op jit(solution)/shard_map/all_to_all | solution.py:391
  17.9 0.0 copy-done.7
  17.9 0.8 finish.1
  18.8 8.5 %all-to-all-start.1 = ((bf16[8,16,640]{2,1,0:T(8,128)(2,1)}), bf16[8,16,640]{2,1,0:T(8,128)(2,1)S(1)}, u32[]{:S(2)}, u32[]{:S(2)}) async-start(bf16[8,16,640]{2,1,0:T(8,128)(2,1)} %finish.1), calls=%async_computation.1 | async-start | bytes 327680 | tf_op jit(solution)/shard_map/all_to_all | solution.py:425
  27.2 0.0 collective-permute-done.queries_ref
  27.3 0.5 query.3
  27.8 0.0 copy-start.8
  27.8 1.0 %copy-done.8 = bf16[576,1024]{1,0:T(8,128)(2,1)} copy-done((bf16[576,1024]{1,0:T(8,128)(2,1)}, bf16[576,1024]{1,0:T(8,128)(2,1)S(1)}, u32[]{:S(2)}) %copy-start.8) | copy-done | bytes 1179672
  28.8 7.9 %all-to-all-done.1.column_ref = bf16[8,16,640]{2,1,0:T(8,128)(2,1)S(1)} async-done(((bf16[8,16,640]{2,1,0:T(8,128)(2,1)}), bf16[8,16,640]{2,1,0:T(8,128)(2,1)S(1)}, u32[]{:S(2)}, u32[]{:S(2)}) %all-to-all-start.1) | async-done | bytes 163872 | tf_op jit(solution)/shard_map/all_to_all | solution.py:425
  36.7 0.0 copy-start.9
  36.7 0.2 pack.1
  36.8 19.4 %all_to_all.20.keys_ref = bf16[8,576,128]{2,1,0:T(8,128)(2,1)S(1)} all-to-all(bf16[8,576,128]{2,1,0:T(8,128)(2,1)S(1)} %pack.1), channel_id=1, replica_groups=mesh['ctx'=32,'head'=8] {'head'}, dimensions={0} | all-to-all | bytes 2359296 | tf_op jit(solution)/shard_map/all_to_all | solution.py:434
  56.3 0.0 collective-permute-start.1
  56.3 0.0 copy-done.9
  56.3 0.0 copy-start.3
  56.3 1.9 %first.1 = (f32[8,1024]{1,0:T(8,128)S(1)}, f32[8,1024]{1,0:T(8,128)S(1)}, f32[512,1024]{1,0:T(8,128)S(1)}) custom-call(bf16[576,1024]{1,0:T(8,128)(2,1)S(1)} %get-tuple-element.19.own_ref, bf16[576,1024]{1,0:T(8,128)(2,1)S(1)} %copy-done.9, bf16[8,576,128]{2,1,0:T(8,128)(2,1)S(1)} %all_to_all.20.keys_ref), custom_call_target="tpu_custom_call" | custom-call | flops 2281701376 | bytes 8388608 | tf_op jit(solution)/shard_map/first/pallas_call | solution.py:440
  58.2 0.9 %collective-permute-done.1.keys_ref.others_ref = bf16[8,576,128]{2,1,0:T(8,128)(2,1)S(1)} collective-permute-done((bf16[8,576,128]{2,1,0:T(8,128)(2,1)S(1)}, bf16[8,576,128]{2,1,0:T(8,128)(2,1)S(1)}, u32[]{:S(2)}, u32[]{:S(2)}) %collective-permute-start.1) | collective-permute-done | bytes 1179680 | tf_op jit(solution)/shard_map/ppermute | solution.py:435
  59.1 0.0 copy-done.3
  59.1 0.0 copy-start.1
  59.1 0.0 copy-start.2
  59.1 1.6 %collective-permute-start.2 = (bf16[1056,128]{1,0:T(8,128)(2,1)S(1)}, bf16[1056,128]{1,0:T(8,128)(2,1)S(1)}, u32[]{:S(2)}, u32[]{:S(2)}) collective-permute-start(bf16[1056,128]{1,0:T(8,128)(2,1)S(1)} %get-tuple-element.31), channel_id=1, source_target_pairs={{0,128},{8,136},{16,144},{24,152},{32,160},{40,168},{48,176},{56,1... | collective-permute-start | bytes 811016 | tf_op jit(solution)/shard_map/ppermute | solution.py:459
  60.7 0.2 copy-done.1
  60.9 0.8 copy-done.2
  61.6 0.0 copy-start.5
  61.6 0.0 copy-start.6
  61.6 3.7 %third.1 = (f32[1024,128]{1,0:T(8,128)S(1)}, f32[8,128]{1,0:T(8,128)S(1)}, bf16[1024,2560]{1,0:T(8,128)(2,1)S(1)}, f32[8,1024]{1,0:T(8,128)S(1)}, f32[8,1024]{1,0:T(8,128)S(1)}, /*index=5*/f32[512,1024]{1,0:T(8,128)S(1)}) custom-call(bf16[576,1024]{1,0:T(8,128)(2,1)S(1)} %get-tuple-element.19.own_ref, ...), custom_call_target="tpu_custom_call", output_to_operand_aliasing={{3}: (6, {}), {4}: (7, {}), {5}: (8, {})} | custom-call | flops 2281701376 | bytes 8388608 | tf_op jit(solution)/shard_map/third/pallas_call | solution.py:460
  65.4 7.7 %collective-permute-done.2.part_ref = bf16[1056,128]{1,0:T(8,128)(2,1)S(1)} collective-permute-done((bf16[1056,128]{1,0:T(8,128)(2,1)S(1)}, bf16[1056,128]{1,0:T(8,128)(2,1)S(1)}, u32[]{:S(2)}, u32[]{:S(2)}) %collective-permute-start.2) | collective-permute-done | bytes 270368 | tf_op jit(solution)/shard_map/ppermute | solution.py:459
  73.1 0.0 copy-done.5
  73.1 0.0 copy-done.6
  73.1 1.7 %output.1 = bf16[2560,128]{1,0:T(8,128)(2,1)S(1)} custom-call(f32[1024,128]{1,0:T(8,128)S(1)} %get-tuple-element.29.mine_ref, f32[8,128]{1,0:T(8,128)S(1)} %get-tuple-element.30.log_ref, bf16[1056,128]{1,0:T(8,128)(2,1)S(1)} %collective-permute-done.2.part_ref, bf16[16,1024]{1,0:T(8,128)(2,1)S(1)} %bitcast.13, bf16[16,2560]{1,0:T(8,128)(2,1)S(1)} %copy-done.5, ...), custom_call_target="tpu_custom_call" | custom-call | flops 671088640 | bytes 8388608 | tf_op jit(solution)/shard_map/output/pallas_call | solution.py:476
  74.8 15.7 %all_to_all.21.parts_ref = bf16[8,320,128]{2,1,0:T(8,128)(2,1)S(1)} all-to-all(bf16[8,320,128]{2,1,0:T(8,128)(2,1)S(1)} %bitcast.10), channel_id=1, replica_groups=mesh['ctx'=32,'head'=8] {'head'}, dimensions={0} | all-to-all | bytes 1310720 | tf_op jit(solution)/shard_map/all_to_all | solution.py:485
  90.5 0.8 total.1
  (5 shorter events, 0.0 us)
Async XLA Ops:
  0.0 12.6 %copy-start.4 = (bf16[128,8,192]{0,2,1:T(8,128)(2,1)S(1)}, bf16[128,8,192]{0,2,1:T(8,128)(2,1)}, u32[]{:S(2)}) copy-start(bf16[128,8,192]{0,2,1:T(8,128)(2,1)} %param.19) | copy-start | bytes 1179652
  0.0 12.6 %copy-start = (bf16[8,128,512]{2,1,0:T(8,128)(2,1)S(1)}, bf16[8,128,512]{2,1,0:T(8,128)(2,1)}, u32[]{:S(2)}) copy-start(bf16[8,128,512]{2,1,0:T(8,128)(2,1)} %absorb_ref.5) | copy-start | bytes 3145732
  0.0 17.9 %copy-start.7 = (f32[512]{0:T(512)S(1)}, f32[512]{0:T(512)}, u32[]{:S(2)}) copy-start(f32[512]{0:T(512)} %param.18) | copy-start | bytes 6148
  2.8 15.1 %all-to-all-start = ((f32[8,72,128]{2,1,0:T(8,128)}), f32[8,72,128]{2,1,0:T(8,128)S(1)}, u32[]{:S(2)}, u32[]{:S(2)}) async-start(f32[8,72,128]{2,1,0:T(8,128)} %project.1), calls=%async_computation | async-start | bytes 589824 | tf_op jit(solution)/shard_map/all_to_all | solution.py:391
  8.9 18.4 %collective-permute-start = (bf16[8,192,128]{2,1,0:T(8,128)(2,1)}, bf16[8,192,128]{2,1,0:T(8,128)(2,1)S(1)}, u32[]{:S(2)}, u32[]{:S(2)}) collective-permute-start(bf16[8,192,128]{2,1,0:T(8,128)(2,1)} %bitcast.11), channel_id=1, source_target_pairs={{128,0},{136,8},{144,16},{152,24},{160,32},{168,40},{176,48},{184,... | collective-permute-start | bytes 1179656 | tf_op jit(solution)/shard_map/ppermute | solution.py:372
  18.8 17.9 %all-to-all-start.1 = ((bf16[8,16,640]{2,1,0:T(8,128)(2,1)}), bf16[8,16,640]{2,1,0:T(8,128)(2,1)S(1)}, u32[]{:S(2)}, u32[]{:S(2)}) async-start(bf16[8,16,640]{2,1,0:T(8,128)(2,1)} %finish.1), calls=%async_computation.1 | async-start | bytes 327680 | tf_op jit(solution)/shard_map/all_to_all | solution.py:425
  27.8 1.0 %copy-start.8 = (bf16[576,1024]{1,0:T(8,128)(2,1)}, bf16[576,1024]{1,0:T(8,128)(2,1)S(1)}, u32[]{:S(2)}) copy-start(bf16[576,1024]{1,0:T(8,128)(2,1)S(1)} %get-tuple-element.22.partner_ref) | copy-start | bytes 3538948
  36.7 19.6 %copy-start.9 = (bf16[576,1024]{1,0:T(8,128)(2,1)S(1)}, bf16[576,1024]{1,0:T(8,128)(2,1)}, u32[]{:S(2)}) copy-start(bf16[576,1024]{1,0:T(8,128)(2,1)} %copy-done.8) | copy-start | bytes 3538948
  56.3 2.8 %collective-permute-start.1 = (bf16[8,576,128]{2,1,0:T(8,128)(2,1)S(1)}, bf16[8,576,128]{2,1,0:T(8,128)(2,1)S(1)}, u32[]{:S(2)}, u32[]{:S(2)}) collective-permute-start(bf16[8,576,128]{2,1,0:T(8,128)(2,1)S(1)} %all_to_all.20.keys_ref), channel_id=1, source_target_pairs={{0,8},{8,0},{16,24},{24,16},{32,40},{40,32},{48,56},{56,48},{64,72... | collective-permute-start | bytes 3538952 | tf_op jit(solution)/shard_map/ppermute | solution.py:435
  56.3 2.8 %copy-start.3 = (bf16[8,512,128]{2,1,0:T(8,128)(2,1)S(1)}, bf16[8,512,128]{2,1,0:T(8,128)(2,1)}, u32[]{:S(2)}) copy-start(bf16[8,512,128]{2,1,0:T(8,128)(2,1)} %absorb_ref.7) | copy-start | bytes 3145732
  59.1 1.7 %copy-start.1 = (bf16[512,2560]{1,0:T(8,128)(2,1)S(1)}, bf16[512,2560]{1,0:T(8,128)(2,1)}, u32[]{:S(2)}) copy-start(bf16[512,2560]{1,0:T(8,128)(2,1)} %values_ref.1) | copy-start | bytes 7864324
  59.1 2.5 %copy-start.2 = (s32[256,2560]{1,0:T(8,128)S(1)}, s32[256,2560]{1,0:T(8,128)}, u32[]{:S(2)}) copy-start(s32[256,2560]{1,0:T(8,128)} %pattern_ref.1) | copy-start | bytes 7864324
  59.1 13.9 %collective-permute-start.2 = (bf16[1056,128]{1,0:T(8,128)(2,1)S(1)}, bf16[1056,128]{1,0:T(8,128)(2,1)S(1)}, u32[]{:S(2)}, u32[]{:S(2)}) collective-permute-start(bf16[1056,128]{1,0:T(8,128)(2,1)S(1)} %get-tuple-element.31), channel_id=1, source_target_pairs={{0,128},{8,136},{16,144},{24,152},{32,160},{40,168},{48,176},{56,1... | collective-permute-start | bytes 811016 | tf_op jit(solution)/shard_map/ppermute | solution.py:459
  61.6 11.4 %copy-start.5 = (bf16[16,2560]{1,0:T(8,128)(2,1)S(1)}, bf16[16,2560]{1,0:T(8,128)(2,1)}, u32[]{:S(2)}) copy-start(bf16[16,2560]{1,0:T(8,128)(2,1)} %up_ref.1) | copy-start | bytes 245764
  61.6 11.4 %copy-start.6 = (bf16[1024,16]{0,1:T(8,128)(2,1)S(1)}, bf16[1024,16]{0,1:T(8,128)(2,1)}, u32[]{:S(2)}) copy-start(bf16[1024,16]{0,1:T(8,128)(2,1)} %param.24) | copy-start | bytes 98308

commit v6 on v5

--- a/solution.py
+++ b/solution.py
@@ -22,6 +22,9 @@
 VDIM = 128
 CTX = 32
 CHIPS = 8
+ORDER = (4, 5, 6, 7, 0, 1, 2, 3)
+FIRST = 4
+PLACES = tuple((place + FIRST) % HEADS for place in range(HEADS))
 PACKED = ROWS * WIDTH // 128
 HALF = ROWS // 2
 KEYS = HEADS * HALF
@@ -127,7 +130,7 @@
     densify(values_ref, pattern_ref, dense_ref)
     raw += dot(jnp.concatenate(parts, axis=1), dense_ref[...])
     for h in range(HEADS):
-        piece = raw[h * PIECE : (h + 1) * PIECE]
+        piece = raw[PLACES[h] * PIECE : (PLACES[h] + 1) * PIECE]
         for c in range(LAT // 128):
             raw_ref[h, c * PIECE : (c + 1) * PIECE, :] = piece[:, c * 128 : (c + 1) * 128]
         rope = piece[:, LAT:]
@@ -172,7 +175,7 @@
 
 def pack_kernel(column_ref, *refs):
     out_ref = refs[-1]
-    keys = column_ref[...].reshape(ROWS, WIDE)
+    keys = jnp.concatenate([column_ref[ORDER.index(chip)] for chip in range(CHIPS)], axis=0)
     rope = keys[:, LAT:WIDTH]
     rope = jnp.concatenate([rope[: ROWS // 2], rope[ROWS // 2 :]], axis=1)
     for k in range(HEADS):
@@ -204,7 +207,7 @@
             key = lax.broadcasted_iota(jnp.int32, (KEYS, 1), 0)
             ahead = (2 * self.chip + self.core) * ROWS + query
             place = (2 * (part * CHIPS // 2 + key % HALF // PIECE) + key_core) * ROWS
-            place += key // HALF * PIECE + key % PIECE
+            place += (key // HALF + FIRST) % HEADS * PIECE + key % PIECE
             scores = jnp.where(place <= ahead, scores, UNSEEN)
         top = jnp.max(scores, axis=0, keepdims=True)
         new = jnp.broadcast_to(top, (8, ALL)) if fresh else jnp.maximum(self.m_ref[...], top)
@@ -325,7 +328,8 @@
         up = up_ref[:, c : c + COLS]
         terms = dot(flat, dense_ref[:, c : c + COLS])
         terms += dot(low, jnp.concatenate([up] * 3, axis=0))
-        out_ref[c : c + COLS, :] = terms.T.astype(BF16)
+        row = (c - FIRST * out_ref.shape[0] // HEADS) % out_ref.shape[0]
+        out_ref[row : row + COLS, :] = terms.T.astype(BF16)
 
 
 def sum_kernel(parts_ref, out_ref):
@@ -388,7 +392,11 @@
         compiler_params=params(56),
         name="project",
     )(tokens, kv_values, kv_pattern, kv_down.T, kv_up)
-    parts = lax.all_to_all(raw, "head", 0, 0, tiled=True)
+
+    def exchange(x):
+        return lax.all_to_all(x, "head", 0, 0, tiled=True, axis_index_groups=[list(PLACES)])
+
+    parts = exchange(raw)
 
     positions = ctx * ROWS + jnp.arange(ROWS, dtype=jnp.int32)
     table = tables(positions)
@@ -418,7 +426,7 @@
     )(parts, kv_gain.reshape(1, LAT), table, own_token)
 
     along_z = [
-        [(u * CHIPS + chip) * 2 + core for chip in range(CHIPS)]
+        [(u * CHIPS + chip) * 2 + core for chip in ORDER]
         for u in range(2)
         for core in range(2)
     ]
@@ -431,7 +439,7 @@
         compiler_params=params(16),
         name="pack",
     )(column, partner_token)
-    keys = lax.all_to_all(packed, "head", 0, 0, tiled=True)
+    keys = exchange(packed)
     others = lax.ppermute(keys, "ctx", [(i, i ^ 1) for i in range(CTX)])
 
     state = (shape(8, ALL), shape(8, ALL), shape(LAT, ALL))
@@ -442,7 +450,7 @@
         out_shape=state,
         in_specs=[VMEM] * 3,
         out_specs=(VMEM,) * 3,
-        compiler_params=params(32),
+        compiler_params=params(20),
         cost_estimate=work,
         name="first",
     )(own_query, partner_query, keys)
@@ -452,7 +460,7 @@
         in_specs=[VMEM] * 6,
         out_specs=(VMEM,) * 4,
         input_output_aliases={3: 1, 4: 2, 5: 3},
-        compiler_params=params(32),
+        compiler_params=params(20),
         cost_estimate=work,
         name="second",
     )(partner_query, others, absorb_v, *first)
@@ -468,7 +476,7 @@
         in_specs=[VMEM] * 9,
         out_specs=(VMEM,) * 6,
         input_output_aliases={6: 3, 7: 4, 8: 5},
-        compiler_params=params(32),
+        compiler_params=params(20),
         cost_estimate=work,
         name="third",
     )(own_query, keys, others, o_values, o_pattern, absorb_v, *second)
@@ -478,13 +486,11 @@
         out_shape=shape(out_cols, ROWS, dtype=BF16),
         in_specs=[VMEM] * 6,
         out_specs=VMEM,
-        compiler_params=params(32),
+        compiler_params=params(20),
         cost_estimate=cost(2 * ROWS * HEADS * VDIM * out_cols, 8 * MIB),
         name="output",
     )(mine, logs, received, o_down.T, o_up, dense)
-    shares = lax.all_to_all(
-        terms.reshape(HEADS, out_cols // HEADS, ROWS), "head", 0, 0, tiled=True
-    )
+    shares = exchange(terms.reshape(HEADS, out_cols // HEADS, ROWS))
     return pl.pallas_call(
         sum_kernel,
         out_shape=shape(out_cols // HEADS, ROWS),

time: 91.7 us -> 87.3 us (0.952)
  waiting for transfers between devices: 21.4 us -> 14.5 us
  starting transfers between devices: 19.4 us -> 22 us
  blocking collectives: 35.2 us -> 34.2 us
    all_to_all x1, waiting for transfers between devices: 7.89 us -> 2.51 us  [local(): lax.all_to_all(piece, 'ctx', 0, 0, tiled=True, axis_index_groups=along_z)]
    all_to_all x1, starting transfers between devices: 8.48 us -> 10.5 us  [local(): lax.all_to_all(piece, 'ctx', 0, 0, tiled=True, axis_index_groups=along_z)]
    all_to_all x1, starting transfers between devices: 6.05 us -> 7.45 us  [exchange(): lax.all_to_all(x, 'head', 0, 0, tiled=True, axis_index_groups=[list(PLACE...]
    all_to_all x1, waiting for transfers between devices: 4.83 us -> 3.46 us  [exchange(): lax.all_to_all(x, 'head', 0, 0, tiled=True, axis_index_groups=[list(PLACE...]
    all_to_all x2, blocking collectives: 35.2 us -> 34.2 us  [exchange(): lax.all_to_all(x, 'head', 0, 0, tiled=True, axis_index_groups=[list(PLACE...]
  transfers between devices with their start and end apart: 5 -> 5, of which waited for: 4 -> 4; matrix products, arithmetic and copies ran while one was open for 0% -> 0% of each run, Pallas kernels for 8% -> 9%
where the time goes in v6:
time: 87.3 us; the launch traced here: 86.2 us
  blocking collectives  34.2 us (39%)
  starting transfers between devices  22 us (25%)
  waiting for transfers between devices  14.5 us (17%)
  Pallas kernels  12.9 us (15%)
  local copies, waits for them, and re-layouts  2.09 us (2%)
    all_to_all x2, blocking collectives, exchange(): lax.all_to_all(x, 'head', 0, 0, tiled=True, axis_index_groups=[list(PLACE...  34.2 us
    all_to_all x1, starting transfers between devices, local(): lax.all_to_all(piece, 'ctx', 0, 0, tiled=True, axis_index_groups=along_z)  10.5 us
    ppermute x1, waiting for transfers between devices, local(): lax.ppermute(part, 'ctx', [(i, i + 2 * CHIPS) for i in range(2 * CHIPS)])  7.65 us
    all_to_all x1, starting transfers between devices, exchange(): lax.all_to_all(x, 'head', 0, 0, tiled=True, axis_index_groups=[list(PLACE...  7.45 us
    pallas_call x1, Pallas kernels, local(): pl.pallas_call(functools.partial(third_kernel, scale), out_shape=(shape(H...  3.75 us
    all_to_all x1, waiting for transfers between devices, exchange(): lax.all_to_all(x, 'head', 0, 0, tiled=True, axis_index_groups=[list(PLACE...  3.46 us
    pallas_call x1, Pallas kernels, local(): pl.pallas_call(project_kernel, out_shape=shape(HEADS, PIECE * WIDTH // 12...  2.82 us
    all_to_all x1, waiting for transfers between devices, local(): lax.all_to_all(piece, 'ctx', 0, 0, tiled=True, axis_index_groups=along_z)  2.51 us
  transfers between devices with their start and end apart: 5, of which 4 were waited for; matrix products, arithmetic and copies ran while one was open for 0% of the time, Pallas kernels for 9%

profile of v6, /device:TPU:2, one launch (start us, length us, event | category | flops | bytes accessed | tf_op | source)
XLA Modules:
  0.0 86.2 jit_solution(18209731639171946269)
XLA Ops:
  0.0 0.0 copy-start.4
  0.0 0.0 copy-start
  0.0 0.0 copy-start.7
  0.0 2.8 %project.1 = f32[8,72,128]{2,1,0:T(8,128)} custom-call(bf16[128,640]{1,0:T(8,128)(2,1)} %tokens_hbm.1, bf16[320,576]{1,0:T(8,128)(2,1)} %values_hbm.1, s32[160,576]{1,0:T(8,128)} %pattern_hbm.1, bf16[16,640]{1,0:T(8,128)(2,1)} %bitcast.15, bf16[16,576]{1,0:T(8,128)(2,1)} %up_hbm.1), custom_call_target="tpu_custom_call" | custom-call | tf_op jit(solution)/shard_map/project/pallas_call | solution.py:378
  2.8 7.5 %all-to-all-start = ((f32[8,72,128]{2,1,0:T(8,128)}), f32[8,72,128]{2,1,0:T(8,128)S(1)}, u32[]{:S(2)}, u32[]{:S(2)}) async-start(f32[8,72,128]{2,1,0:T(8,128)} %project.1), calls=%async_computation | async-start | bytes 589824 | tf_op jit(solution)/shard_map/all_to_all | solution.py:397
  10.3 2.5 %collective-permute-start = (bf16[8,192,128]{2,1,0:T(8,128)(2,1)}, bf16[8,192,128]{2,1,0:T(8,128)(2,1)S(1)}, u32[]{:S(2)}, u32[]{:S(2)}) collective-permute-start(bf16[8,192,128]{2,1,0:T(8,128)(2,1)} %bitcast.11), channel_id=1, source_target_pairs={{128,0},{136,8},{144,16},{152,24},{160,32},{168,40},{176,48},{184,... | collective-permute-start | bytes 1179656 | tf_op jit(solution)/shard_map/ppermute | solution.py:376
  12.8 0.2 multiply_cosine_fusion
  13.1 0.1 copy.20.table_ref
  13.2 0.0 copy-done.4
  13.2 0.0 copy-done
  13.2 0.5 query.2
  13.7 3.5 %all-to-all-done.parts_ref = f32[8,72,128]{2,1,0:T(8,128)S(1)} async-done(((f32[8,72,128]{2,1,0:T(8,128)}), f32[8,72,128]{2,1,0:T(8,128)S(1)}, u32[]{:S(2)}, u32[]{:S(2)}) %all-to-all-start) | async-done | bytes 294944 | tf_op jit(solution)/shard_map/all_to_all | solution.py:397
  17.1 0.0 copy-done.7
  17.1 0.8 finish.1
  18.0 10.5 %all-to-all-start.1 = ((bf16[8,16,640]{2,1,0:T(8,128)(2,1)}), bf16[8,16,640]{2,1,0:T(8,128)(2,1)S(1)}, u32[]{:S(2)}, u32[]{:S(2)}) async-start(bf16[8,16,640]{2,1,0:T(8,128)(2,1)} %finish.1), calls=%async_computation.1 | async-start | bytes 327680 | tf_op jit(solution)/shard_map/all_to_all | solution.py:433
  28.4 0.0 collective-permute-done.queries_ref
  28.5 0.5 query.3
  28.9 0.0 copy-start.8
  29.0 1.0 %copy-done.8 = bf16[576,1024]{1,0:T(8,128)(2,1)} copy-done((bf16[576,1024]{1,0:T(8,128)(2,1)}, bf16[576,1024]{1,0:T(8,128)(2,1)S(1)}, u32[]{:S(2)}) %copy-start.8) | copy-done | bytes 1179672
  30.0 2.5 %all-to-all-done.1.column_ref = bf16[8,16,640]{2,1,0:T(8,128)(2,1)S(1)} async-done(((bf16[8,16,640]{2,1,0:T(8,128)(2,1)}), bf16[8,16,640]{2,1,0:T(8,128)(2,1)S(1)}, u32[]{:S(2)}, u32[]{:S(2)}) %all-to-all-start.1) | async-done | bytes 163872 | tf_op jit(solution)/shard_map/all_to_all | solution.py:433
  32.5 0.0 copy-start.9
  32.5 0.2 pack.1
  32.7 18.6 %all_to_all.20.keys_ref = bf16[8,576,128]{2,1,0:T(8,128)(2,1)S(1)} all-to-all(bf16[8,576,128]{2,1,0:T(8,128)(2,1)S(1)} %pack.1), channel_id=1, replica_groups={{4,5,6,7,0,1,2,3},{12,13,14,15,8,9,10,11},{20,21,22,23,16,17,18,19},{28..., dimensions={0} | all-to-all | bytes 2359296 | tf_op jit(solution)/shard_map/all_to_all | solution.py:397
  51.3 0.0 collective-permute-start.1
  51.3 0.0 copy-done.9
  51.3 0.0 copy-start.3
  51.3 1.9 %first.1 = (f32[8,1024]{1,0:T(8,128)S(1)}, f32[8,1024]{1,0:T(8,128)S(1)}, f32[512,1024]{1,0:T(8,128)S(1)}) custom-call(bf16[576,1024]{1,0:T(8,128)(2,1)S(1)} %get-tuple-element.19.own_ref, bf16[576,1024]{1,0:T(8,128)(2,1)S(1)} %copy-done.9, bf16[8,576,128]{2,1,0:T(8,128)(2,1)S(1)} %all_to_all.20.keys_ref), custom_call_target="tpu_custom_call" | custom-call | flops 2281701376 | bytes 8388608 | tf_op jit(solution)/shard_map/first/pallas_call | solution.py:448
  53.2 0.9 %collective-permute-done.1.keys_ref.others_ref = bf16[8,576,128]{2,1,0:T(8,128)(2,1)S(1)} collective-permute-done((bf16[8,576,128]{2,1,0:T(8,128)(2,1)S(1)}, bf16[8,576,128]{2,1,0:T(8,128)(2,1)S(1)}, u32[]{:S(2)}, u32[]{:S(2)}) %collective-permute-start.1) | collective-permute-done | bytes 1179680 | tf_op jit(solution)/shard_map/ppermute | solution.py:443
  54.1 0.0 copy-done.3
  54.1 0.0 copy-start.1
  54.1 0.0 copy-start.2
  54.2 1.6 %collective-permute-start.2 = (bf16[1056,128]{1,0:T(8,128)(2,1)S(1)}, bf16[1056,128]{1,0:T(8,128)(2,1)S(1)}, u32[]{:S(2)}, u32[]{:S(2)}) collective-permute-start(bf16[1056,128]{1,0:T(8,128)(2,1)S(1)} %get-tuple-element.31), channel_id=1, source_target_pairs={{0,128},{8,136},{16,144},{24,152},{32,160},{40,168},{48,176},{56,1... | collective-permute-start | bytes 811016 | tf_op jit(solution)/shard_map/ppermute | solution.py:467
  55.7 0.2 copy-done.1
  55.9 0.8 copy-done.2
  56.7 0.0 copy-start.5
  56.7 0.0 copy-start.6
  56.7 3.7 %third.1 = (f32[1024,128]{1,0:T(8,128)S(1)}, f32[8,128]{1,0:T(8,128)S(1)}, bf16[1024,2560]{1,0:T(8,128)(2,1)S(1)}, f32[8,1024]{1,0:T(8,128)S(1)}, f32[8,1024]{1,0:T(8,128)S(1)}, /*index=5*/f32[512,1024]{1,0:T(8,128)S(1)}) custom-call(bf16[576,1024]{1,0:T(8,128)(2,1)S(1)} %get-tuple-element.19.own_ref, ...), custom_call_target="tpu_custom_call", output_to_operand_aliasing={{3}: (6, {}), {4}: (7, {}), {5}: (8, {})} | custom-call | flops 2281701376 | bytes 8388608 | tf_op jit(solution)/shard_map/third/pallas_call | solution.py:468
  60.4 7.7 %collective-permute-done.2.part_ref = bf16[1056,128]{1,0:T(8,128)(2,1)S(1)} collective-permute-done((bf16[1056,128]{1,0:T(8,128)(2,1)S(1)}, bf16[1056,128]{1,0:T(8,128)(2,1)S(1)}, u32[]{:S(2)}, u32[]{:S(2)}) %collective-permute-start.2) | collective-permute-done | bytes 270368 | tf_op jit(solution)/shard_map/ppermute | solution.py:467
  68.1 0.0 copy-done.5
  68.1 0.0 copy-done.6
  68.1 1.7 %output.1 = bf16[2560,128]{1,0:T(8,128)(2,1)S(1)} custom-call(f32[1024,128]{1,0:T(8,128)S(1)} %get-tuple-element.29.mine_ref, f32[8,128]{1,0:T(8,128)S(1)} %get-tuple-element.30.log_ref, bf16[1056,128]{1,0:T(8,128)(2,1)S(1)} %collective-permute-done.2.part_ref, bf16[16,1024]{1,0:T(8,128)(2,1)S(1)} %bitcast.13, bf16[16,2560]{1,0:T(8,128)(2,1)S(1)} %copy-done.5, ...), custom_call_target="tpu_custom_call" | custom-call | flops 671088640 | bytes 8388608 | tf_op jit(solution)/shard_map/output/pallas_call | solution.py:484
  69.8 15.6 %all_to_all.21.parts_ref = bf16[8,320,128]{2,1,0:T(8,128)(2,1)S(1)} all-to-all(bf16[8,320,128]{2,1,0:T(8,128)(2,1)S(1)} %bitcast.10), channel_id=1, replica_groups={{4,5,6,7,0,1,2,3},{12,13,14,15,8,9,10,11},{20,21,22,23,16,17,18,19},{28..., dimensions={0} | all-to-all | bytes 1310720 | tf_op jit(solution)/shard_map/all_to_all | solution.py:397
  85.4 0.8 total.1
  (5 shorter events, 0.0 us)
Async XLA Ops:
  0.0 13.2 %copy-start.4 = (bf16[128,8,192]{0,2,1:T(8,128)(2,1)S(1)}, bf16[128,8,192]{0,2,1:T(8,128)(2,1)}, u32[]{:S(2)}) copy-start(bf16[128,8,192]{0,2,1:T(8,128)(2,1)} %param.19) | copy-start | bytes 1179652
  0.0 13.2 %copy-start = (bf16[8,128,512]{2,1,0:T(8,128)(2,1)S(1)}, bf16[8,128,512]{2,1,0:T(8,128)(2,1)}, u32[]{:S(2)}) copy-start(bf16[8,128,512]{2,1,0:T(8,128)(2,1)} %absorb_ref.5) | copy-start | bytes 3145732
  0.0 17.1 %copy-start.7 = (f32[512]{0:T(512)S(1)}, f32[512]{0:T(512)}, u32[]{:S(2)}) copy-start(f32[512]{0:T(512)} %param.18) | copy-start | bytes 6148
  2.8 14.3 %all-to-all-start = ((f32[8,72,128]{2,1,0:T(8,128)}), f32[8,72,128]{2,1,0:T(8,128)S(1)}, u32[]{:S(2)}, u32[]{:S(2)}) async-start(f32[8,72,128]{2,1,0:T(8,128)} %project.1), calls=%async_computation | async-start | bytes 589824 | tf_op jit(solution)/shard_map/all_to_all | solution.py:397
  10.3 18.2 %collective-permute-start = (bf16[8,192,128]{2,1,0:T(8,128)(2,1)}, bf16[8,192,128]{2,1,0:T(8,128)(2,1)S(1)}, u32[]{:S(2)}, u32[]{:S(2)}) collective-permute-start(bf16[8,192,128]{2,1,0:T(8,128)(2,1)} %bitcast.11), channel_id=1, source_target_pairs={{128,0},{136,8},{144,16},{152,24},{160,32},{168,40},{176,48},{184,... | collective-permute-start | bytes 1179656 | tf_op jit(solution)/shard_map/ppermute | solution.py:376
  18.0 14.5 %all-to-all-start.1 = ((bf16[8,16,640]{2,1,0:T(8,128)(2,1)}), bf16[8,16,640]{2,1,0:T(8,128)(2,1)S(1)}, u32[]{:S(2)}, u32[]{:S(2)}) async-start(bf16[8,16,640]{2,1,0:T(8,128)(2,1)} %finish.1), calls=%async_computation.1 | async-start | bytes 327680 | tf_op jit(solution)/shard_map/all_to_all | solution.py:433
  28.9 1.0 %copy-start.8 = (bf16[576,1024]{1,0:T(8,128)(2,1)}, bf16[576,1024]{1,0:T(8,128)(2,1)S(1)}, u32[]{:S(2)}) copy-start(bf16[576,1024]{1,0:T(8,128)(2,1)S(1)} %get-tuple-element.22.partner_ref) | copy-start | bytes 3538948
  32.5 18.8 %copy-start.9 = (bf16[576,1024]{1,0:T(8,128)(2,1)S(1)}, bf16[576,1024]{1,0:T(8,128)(2,1)}, u32[]{:S(2)}) copy-start(bf16[576,1024]{1,0:T(8,128)(2,1)} %copy-done.8) | copy-start | bytes 3538948
  51.3 2.8 %collective-permute-start.1 = (bf16[8,576,128]{2,1,0:T(8,128)(2,1)S(1)}, bf16[8,576,128]{2,1,0:T(8,128)(2,1)S(1)}, u32[]{:S(2)}, u32[]{:S(2)}) collective-permute-start(bf16[8,576,128]{2,1,0:T(8,128)(2,1)S(1)} %all_to_all.20.keys_ref), channel_id=1, source_target_pairs={{0,8},{8,0},{16,24},{24,16},{32,40},{40,32},{48,56},{56,48},{64,72... | collective-permute-start | bytes 3538952 | tf_op jit(solution)/shard_map/ppermute | solution.py:443
  51.3 2.8 %copy-start.3 = (bf16[8,512,128]{2,1,0:T(8,128)(2,1)S(1)}, bf16[8,512,128]{2,1,0:T(8,128)(2,1)}, u32[]{:S(2)}) copy-start(bf16[8,512,128]{2,1,0:T(8,128)(2,1)} %absorb_ref.7) | copy-start | bytes 3145732
  54.1 1.7 %copy-start.1 = (bf16[512,2560]{1,0:T(8,128)(2,1)S(1)}, bf16[512,2560]{1,0:T(8,128)(2,1)}, u32[]{:S(2)}) copy-start(bf16[512,2560]{1,0:T(8,128)(2,1)} %values_ref.1) | copy-start | bytes 7864324
  54.1 2.5 %copy-start.2 = (s32[256,2560]{1,0:T(8,128)S(1)}, s32[256,2560]{1,0:T(8,128)}, u32[]{:S(2)}) copy-start(s32[256,2560]{1,0:T(8,128)} %pattern_ref.1) | copy-start | bytes 7864324
  54.2 13.9 %collective-permute-start.2 = (bf16[1056,128]{1,0:T(8,128)(2,1)S(1)}, bf16[1056,128]{1,0:T(8,128)(2,1)S(1)}, u32[]{:S(2)}, u32[]{:S(2)}) collective-permute-start(bf16[1056,128]{1,0:T(8,128)(2,1)S(1)} %get-tuple-element.31), channel_id=1, source_target_pairs={{0,128},{8,136},{16,144},{24,152},{32,160},{40,168},{48,176},{56,1... | collective-permute-start | bytes 811016 | tf_op jit(solution)/shard_map/ppermute | solution.py:467
  56.7 11.4 %copy-start.5 = (bf16[16,2560]{1,0:T(8,128)(2,1)S(1)}, bf16[16,2560]{1,0:T(8,128)(2,1)}, u32[]{:S(2)}) copy-start(bf16[16,2560]{1,0:T(8,128)(2,1)} %up_ref.1) | copy-start | bytes 245764
  56.7 11.4 %copy-start.6 = (bf16[1024,16]{0,1:T(8,128)(2,1)S(1)}, bf16[1024,16]{0,1:T(8,128)(2,1)}, u32[]{:S(2)}) copy-start(bf16[1024,16]{0,1:T(8,128)(2,1)} %param.24) | copy-start | bytes 98308

commit v7 on v6

--- a/solution.py
+++ b/solution.py
@@ -332,13 +332,6 @@
         out_ref[row : row + COLS, :] = terms.T.astype(BF16)
 
 
-def sum_kernel(parts_ref, out_ref):
-    total = parts_ref[0].astype(F32)
-    for h in range(1, HEADS):
-        total += parts_ref[h].astype(F32)
-    out_ref[...] = total
-
-
 def shape(*dims, dtype=F32):
     return jax.ShapeDtypeStruct(dims, dtype)
 
@@ -419,11 +412,11 @@
     piece = pl.pallas_call(
         finish_kernel,
         out_shape=shape(CHIPS, PIECE, WIDE, dtype=BF16),
-        in_specs=[VMEM] * 4,
+        in_specs=[VMEM] * 3,
         out_specs=VMEM,
         compiler_params=params(16),
         name="finish",
-    )(parts, kv_gain.reshape(1, LAT), table, own_token)
+    )(parts, kv_gain.reshape(1, LAT), table)
 
     along_z = [
         [(u * CHIPS + chip) * 2 + core for chip in ORDER]
@@ -434,11 +427,11 @@
     packed = pl.pallas_call(
         pack_kernel,
         out_shape=shape(HEADS, PACKED, 128, dtype=BF16),
-        in_specs=[VMEM] * 2,
+        in_specs=[VMEM] * 3,
         out_specs=VMEM,
         compiler_params=params(16),
         name="pack",
-    )(column, partner_token)
+    )(column, own_token, partner_token)
     keys = exchange(packed)
     others = lax.ppermute(keys, "ctx", [(i, i ^ 1) for i in range(CTX)])
 
@@ -491,14 +484,7 @@
         name="output",
     )(mine, logs, received, o_down.T, o_up, dense)
     shares = exchange(terms.reshape(HEADS, out_cols // HEADS, ROWS))
-    return pl.pallas_call(
-        sum_kernel,
-        out_shape=shape(out_cols // HEADS, ROWS),
-        in_specs=[VMEM],
-        out_specs=VMEM,
-        compiler_params=params(16),
-        name="total",
-    )(shares).T
+    return jnp.sum(shares.astype(F32), axis=0).T
 
 
 def solution(mesh):

time: 87.3 us -> 87.3 us (level)
  no operation moved by 1% of the time
where the time goes in v7:
time: 87.3 us; the launch traced here: 86.2 us
  blocking collectives  34.2 us (39%)
  starting transfers between devices  22 us (25%)
  waiting for transfers between devices  14.5 us (17%)
  Pallas kernels  12.2 us (14%)
  local copies, waits for them, and re-layouts  2.1 us (2%)
  other arithmetic  0.99 us (1%)
    all_to_all x2, blocking collectives, exchange(): lax.all_to_all(x, 'head', 0, 0, tiled=True, axis_index_groups=[list(PLACE...  34.2 us
    all_to_all x1, starting transfers between devices, local(): lax.all_to_all(piece, 'ctx', 0, 0, tiled=True, axis_index_groups=along_z)  10.5 us
    ppermute x1, waiting for transfers between devices, local(): lax.ppermute(part, 'ctx', [(i, i + 2 * CHIPS) for i in range(2 * CHIPS)])  7.64 us
    all_to_all x1, starting transfers between devices, exchange(): lax.all_to_all(x, 'head', 0, 0, tiled=True, axis_index_groups=[list(PLACE...  7.45 us
    all_to_all x1, waiting for transfers between devices, exchange(): lax.all_to_all(x, 'head', 0, 0, tiled=True, axis_index_groups=[list(PLACE...  3.97 us
    pallas_call x1, Pallas kernels, local(): pl.pallas_call(functools.partial(third_kernel, scale), out_shape=(shape(H...  3.75 us
    pallas_call x1, Pallas kernels, local(): pl.pallas_call(project_kernel, out_shape=shape(HEADS, PIECE * WIDTH // 12...  2.82 us
    ppermute x1, starting transfers between devices, local(): lax.ppermute(columns, 'ctx', [(i + 2 * CHIPS, i) for i in range(2 * CHIPS)])  2.5 us
  transfers between devices with their start and end apart: 5, of which 4 were waited for; matrix products, arithmetic and copies ran while one was open for 0% of the time, Pallas kernels for 9%

profile of v7, /device:TPU:2, one launch (start us, length us, event | category | flops | bytes accessed | tf_op | source)
XLA Modules:
  0.0 86.2 jit_solution(15359799674085446967)
XLA Ops:
  0.0 0.0 copy-start.4
  0.0 0.0 copy-start.7
  0.0 0.0 copy-start
  0.0 2.8 %project.1 = f32[8,72,128]{2,1,0:T(8,128)} custom-call(bf16[128,640]{1,0:T(8,128)(2,1)} %tokens_hbm.1, bf16[320,576]{1,0:T(8,128)(2,1)} %values_hbm.1, s32[160,576]{1,0:T(8,128)} %pattern_hbm.1, bf16[16,640]{1,0:T(8,128)(2,1)} %bitcast.15, bf16[16,576]{1,0:T(8,128)(2,1)} %up_hbm.1), custom_call_target="tpu_custom_call" | custom-call | tf_op jit(solution)/shard_map/project/pallas_call | solution.py:371
  2.8 7.5 %all-to-all-start = ((f32[8,72,128]{2,1,0:T(8,128)}), f32[8,72,128]{2,1,0:T(8,128)S(1)}, u32[]{:S(2)}, u32[]{:S(2)}) async-start(f32[8,72,128]{2,1,0:T(8,128)} %project.1), calls=%async_computation | async-start | bytes 589824 | tf_op jit(solution)/shard_map/all_to_all | solution.py:390
  10.3 2.5 %collective-permute-start = (bf16[8,192,128]{2,1,0:T(8,128)(2,1)}, bf16[8,192,128]{2,1,0:T(8,128)(2,1)S(1)}, u32[]{:S(2)}, u32[]{:S(2)}) collective-permute-start(bf16[8,192,128]{2,1,0:T(8,128)(2,1)} %bitcast.11), channel_id=1, source_target_pairs={{128,0},{136,8},{144,16},{152,24},{160,32},{168,40},{176,48},{184,... | collective-permute-start | bytes 1179656 | tf_op jit(solution)/shard_map/ppermute | solution.py:369
  12.8 0.2 multiply_cosine_fusion
  13.1 0.1 copy.20.table_ref
  13.2 4.0 %all-to-all-done.parts_ref = f32[8,72,128]{2,1,0:T(8,128)S(1)} async-done(((f32[8,72,128]{2,1,0:T(8,128)}), f32[8,72,128]{2,1,0:T(8,128)S(1)}, u32[]{:S(2)}, u32[]{:S(2)}) %all-to-all-start) | async-done | bytes 294944 | tf_op jit(solution)/shard_map/all_to_all | solution.py:390
  17.1 0.0 copy-done.7
  17.1 0.8 finish.1
  18.0 10.5 %all-to-all-start.1 = ((bf16[8,16,640]{2,1,0:T(8,128)(2,1)}), bf16[8,16,640]{2,1,0:T(8,128)(2,1)S(1)}, u32[]{:S(2)}, u32[]{:S(2)}) async-start(bf16[8,16,640]{2,1,0:T(8,128)(2,1)} %finish.1), calls=%async_computation.1 | async-start | bytes 327680 | tf_op jit(solution)/shard_map/all_to_all | solution.py:426
  28.4 0.0 copy-done.4
  28.4 0.0 copy-done
  28.5 0.5 query.2
  28.9 0.0 collective-permute-done.queries_ref
  29.0 0.5 query.3
  29.4 0.0 copy-start.8
  29.5 1.0 %copy-done.8 = bf16[576,1024]{1,0:T(8,128)(2,1)} copy-done((bf16[576,1024]{1,0:T(8,128)(2,1)}, bf16[576,1024]{1,0:T(8,128)(2,1)S(1)}, u32[]{:S(2)}) %copy-start.8) | copy-done | bytes 1179672
  30.5 2.0 %all-to-all-done.1.column_ref = bf16[8,16,640]{2,1,0:T(8,128)(2,1)S(1)} async-done(((bf16[8,16,640]{2,1,0:T(8,128)(2,1)}), bf16[8,16,640]{2,1,0:T(8,128)(2,1)S(1)}, u32[]{:S(2)}, u32[]{:S(2)}) %all-to-all-start.1) | async-done | bytes 163872 | tf_op jit(solution)/shard_map/all_to_all | solution.py:426
  32.5 0.0 copy-start.9
  32.5 0.2 pack.1
  32.7 18.6 %all_to_all.20.keys_ref = bf16[8,576,128]{2,1,0:T(8,128)(2,1)S(1)} all-to-all(bf16[8,576,128]{2,1,0:T(8,128)(2,1)S(1)} %pack.1), channel_id=1, replica_groups={{4,5,6,7,0,1,2,3},{12,13,14,15,8,9,10,11},{20,21,22,23,16,17,18,19},{28..., dimensions={0} | all-to-all | bytes 2359296 | tf_op jit(solution)/shard_map/all_to_all | solution.py:390
  51.3 0.0 collective-permute-start.1
  51.3 0.0 copy-done.9
  51.3 0.0 copy-start.3
  51.3 1.9 %first.1 = (f32[8,1024]{1,0:T(8,128)S(1)}, f32[8,1024]{1,0:T(8,128)S(1)}, f32[512,1024]{1,0:T(8,128)S(1)}) custom-call(bf16[576,1024]{1,0:T(8,128)(2,1)S(1)} %get-tuple-element.19.own_ref, bf16[576,1024]{1,0:T(8,128)(2,1)S(1)} %copy-done.9, bf16[8,576,128]{2,1,0:T(8,128)(2,1)S(1)} %all_to_all.20.keys_ref), custom_call_target="tpu_custom_call" | custom-call | flops 2281701376 | bytes 8388608 | tf_op jit(solution)/shard_map/first/pallas_call | solution.py:441
  53.2 0.9 %collective-permute-done.1.keys_ref.others_ref = bf16[8,576,128]{2,1,0:T(8,128)(2,1)S(1)} collective-permute-done((bf16[8,576,128]{2,1,0:T(8,128)(2,1)S(1)}, bf16[8,576,128]{2,1,0:T(8,128)(2,1)S(1)}, u32[]{:S(2)}, u32[]{:S(2)}) %collective-permute-start.1) | collective-permute-done | bytes 1179680 | tf_op jit(solution)/shard_map/ppermute | solution.py:436
  54.1 0.0 copy-done.3
  54.1 0.0 copy-start.1
  54.1 0.0 copy-start.2
  54.2 1.6 %collective-permute-start.2 = (bf16[1056,128]{1,0:T(8,128)(2,1)S(1)}, bf16[1056,128]{1,0:T(8,128)(2,1)S(1)}, u32[]{:S(2)}, u32[]{:S(2)}) collective-permute-start(bf16[1056,128]{1,0:T(8,128)(2,1)S(1)} %get-tuple-element.31), channel_id=1, source_target_pairs={{0,128},{8,136},{16,144},{24,152},{32,160},{40,168},{48,176},{56,1... | collective-permute-start | bytes 811016 | tf_op jit(solution)/shard_map/ppermute | solution.py:460
  55.7 0.2 copy-done.1
  55.9 0.8 copy-done.2
  56.7 0.0 copy-start.5
  56.7 0.0 copy-start.6
  56.7 3.7 %third.1 = (f32[1024,128]{1,0:T(8,128)S(1)}, f32[8,128]{1,0:T(8,128)S(1)}, bf16[1024,2560]{1,0:T(8,128)(2,1)S(1)}, f32[8,1024]{1,0:T(8,128)S(1)}, f32[8,1024]{1,0:T(8,128)S(1)}, /*index=5*/f32[512,1024]{1,0:T(8,128)S(1)}) custom-call(bf16[576,1024]{1,0:T(8,128)(2,1)S(1)} %get-tuple-element.19.own_ref, ...), custom_call_target="tpu_custom_call", output_to_operand_aliasing={{3}: (6, {}), {4}: (7, {}), {5}: (8, {})} | custom-call | flops 2281701376 | bytes 8388608 | tf_op jit(solution)/shard_map/third/pallas_call | solution.py:461
  60.4 7.6 %collective-permute-done.2.part_ref = bf16[1056,128]{1,0:T(8,128)(2,1)S(1)} collective-permute-done((bf16[1056,128]{1,0:T(8,128)(2,1)S(1)}, bf16[1056,128]{1,0:T(8,128)(2,1)S(1)}, u32[]{:S(2)}, u32[]{:S(2)}) %collective-permute-start.2) | collective-permute-done | bytes 270368 | tf_op jit(solution)/shard_map/ppermute | solution.py:460
  68.1 0.0 copy-done.5
  68.1 0.0 copy-done.6
  68.1 1.7 %output.1 = bf16[2560,128]{1,0:T(8,128)(2,1)S(1)} custom-call(f32[1024,128]{1,0:T(8,128)S(1)} %get-tuple-element.29.mine_ref, f32[8,128]{1,0:T(8,128)S(1)} %get-tuple-element.30.log_ref, bf16[1056,128]{1,0:T(8,128)(2,1)S(1)} %collective-permute-done.2.part_ref, bf16[16,1024]{1,0:T(8,128)(2,1)S(1)} %bitcast.13, bf16[16,2560]{1,0:T(8,128)(2,1)S(1)} %copy-done.5, ...), custom_call_target="tpu_custom_call" | custom-call | flops 671088640 | bytes 8388608 | tf_op jit(solution)/shard_map/output/pallas_call | solution.py:477
  69.8 15.6 %all_to_all.21 = bf16[8,320,128]{2,1,0:T(8,128)(2,1)S(1)} all-to-all(bf16[8,320,128]{2,1,0:T(8,128)(2,1)S(1)} %bitcast.10), channel_id=1, replica_groups={{4,5,6,7,0,1,2,3},{12,13,14,15,8,9,10,11},{20,21,22,23,16,17,18,19},{28..., dimensions={0} | all-to-all | bytes 1310720 | tf_op jit(solution)/shard_map/all_to_all | solution.py:390
  85.4 0.8 convert_reduce_fusion
  (5 shorter events, 0.0 us)
Async XLA Ops:
  0.0 28.4 %copy-start.4 = (bf16[128,8,192]{0,2,1:T(8,128)(2,1)S(1)}, bf16[128,8,192]{0,2,1:T(8,128)(2,1)}, u32[]{:S(2)}) copy-start(bf16[128,8,192]{0,2,1:T(8,128)(2,1)} %param.19) | copy-start | bytes 1179652
  0.0 17.1 %copy-start.7 = (f32[512]{0:T(512)S(1)}, f32[512]{0:T(512)}, u32[]{:S(2)}) copy-start(f32[512]{0:T(512)} %param.18) | copy-start | bytes 6148
  0.0 28.4 %copy-start = (bf16[8,128,512]{2,1,0:T(8,128)(2,1)S(1)}, bf16[8,128,512]{2,1,0:T(8,128)(2,1)}, u32[]{:S(2)}) copy-start(bf16[8,128,512]{2,1,0:T(8,128)(2,1)} %absorb_ref.5) | copy-start | bytes 3145732
  2.8 14.3 %all-to-all-start = ((f32[8,72,128]{2,1,0:T(8,128)}), f32[8,72,128]{2,1,0:T(8,128)S(1)}, u32[]{:S(2)}, u32[]{:S(2)}) async-start(f32[8,72,128]{2,1,0:T(8,128)} %project.1), calls=%async_computation | async-start | bytes 589824 | tf_op jit(solution)/shard_map/all_to_all | solution.py:390
  10.3 18.7 %collective-permute-start = (bf16[8,192,128]{2,1,0:T(8,128)(2,1)}, bf16[8,192,128]{2,1,0:T(8,128)(2,1)S(1)}, u32[]{:S(2)}, u32[]{:S(2)}) collective-permute-start(bf16[8,192,128]{2,1,0:T(8,128)(2,1)} %bitcast.11), channel_id=1, source_target_pairs={{128,0},{136,8},{144,16},{152,24},{160,32},{168,40},{176,48},{184,... | collective-permute-start | bytes 1179656 | tf_op jit(solution)/shard_map/ppermute | solution.py:369
  18.0 14.5 %all-to-all-start.1 = ((bf16[8,16,640]{2,1,0:T(8,128)(2,1)}), bf16[8,16,640]{2,1,0:T(8,128)(2,1)S(1)}, u32[]{:S(2)}, u32[]{:S(2)}) async-start(bf16[8,16,640]{2,1,0:T(8,128)(2,1)} %finish.1), calls=%async_computation.1 | async-start | bytes 327680 | tf_op jit(solution)/shard_map/all_to_all | solution.py:426
  29.4 1.0 %copy-start.8 = (bf16[576,1024]{1,0:T(8,128)(2,1)}, bf16[576,1024]{1,0:T(8,128)(2,1)S(1)}, u32[]{:S(2)}) copy-start(bf16[576,1024]{1,0:T(8,128)(2,1)S(1)} %get-tuple-element.22.partner_ref) | copy-start | bytes 3538948
  32.5 18.8 %copy-start.9 = (bf16[576,1024]{1,0:T(8,128)(2,1)S(1)}, bf16[576,1024]{1,0:T(8,128)(2,1)}, u32[]{:S(2)}) copy-start(bf16[576,1024]{1,0:T(8,128)(2,1)} %copy-done.8) | copy-start | bytes 3538948
  51.3 2.8 %collective-permute-start.1 = (bf16[8,576,128]{2,1,0:T(8,128)(2,1)S(1)}, bf16[8,576,128]{2,1,0:T(8,128)(2,1)S(1)}, u32[]{:S(2)}, u32[]{:S(2)}) collective-permute-start(bf16[8,576,128]{2,1,0:T(8,128)(2,1)S(1)} %all_to_all.20.keys_ref), channel_id=1, source_target_pairs={{0,8},{8,0},{16,24},{24,16},{32,40},{40,32},{48,56},{56,48},{64,72... | collective-permute-start | bytes 3538952 | tf_op jit(solution)/shard_map/ppermute | solution.py:436
  51.3 2.8 %copy-start.3 = (bf16[8,512,128]{2,1,0:T(8,128)(2,1)S(1)}, bf16[8,512,128]{2,1,0:T(8,128)(2,1)}, u32[]{:S(2)}) copy-start(bf16[8,512,128]{2,1,0:T(8,128)(2,1)} %absorb_ref.7) | copy-start | bytes 3145732
  54.1 1.7 %copy-start.1 = (bf16[512,2560]{1,0:T(8,128)(2,1)S(1)}, bf16[512,2560]{1,0:T(8,128)(2,1)}, u32[]{:S(2)}) copy-start(bf16[512,2560]{1,0:T(8,128)(2,1)} %values_ref.1) | copy-start | bytes 7864324
  54.1 2.5 %copy-start.2 = (s32[256,2560]{1,0:T(8,128)S(1)}, s32[256,2560]{1,0:T(8,128)}, u32[]{:S(2)}) copy-start(s32[256,2560]{1,0:T(8,128)} %pattern_ref.1) | copy-start | bytes 7864324
  54.2 13.9 %collective-permute-start.2 = (bf16[1056,128]{1,0:T(8,128)(2,1)S(1)}, bf16[1056,128]{1,0:T(8,128)(2,1)S(1)}, u32[]{:S(2)}, u32[]{:S(2)}) collective-permute-start(bf16[1056,128]{1,0:T(8,128)(2,1)S(1)} %get-tuple-element.31), channel_id=1, source_target_pairs={{0,128},{8,136},{16,144},{24,152},{32,160},{40,168},{48,176},{56,1... | collective-permute-start | bytes 811016 | tf_op jit(solution)/shard_map/ppermute | solution.py:460
  56.7 11.4 %copy-start.5 = (bf16[16,2560]{1,0:T(8,128)(2,1)S(1)}, bf16[16,2560]{1,0:T(8,128)(2,1)}, u32[]{:S(2)}) copy-start(bf16[16,2560]{1,0:T(8,128)(2,1)} %up_ref.1) | copy-start | bytes 245764
  56.7 11.4 %copy-start.6 = (bf16[1024,16]{0,1:T(8,128)(2,1)S(1)}, bf16[1024,16]{0,1:T(8,128)(2,1)}, u32[]{:S(2)}) copy-start(bf16[1024,16]{0,1:T(8,128)(2,1)} %param.24) | copy-start | bytes 98308
